TPU v7x, 128 devices: a whole 4x4x4 slice. The times are simulated.
128 devices in a mesh: space: 8 (over x, y_hi), mode: 16 (over z, y_lo, core).
Axes of the slice: x: 4, y: 4 (y_hi: 2, y_lo: 2; y = y_hi * 2 + y_lo), z: 4, core: 2. Of those that a mesh axis runs over, the one named last changes fastest.
Arguments:
- displacement: bfloat16 [256, 64, 4096], P('mode', 'space'), may hold values from -0.29882812 to 0.29882812
- direction: bfloat16 [256, 64, 4096], P('mode', 'space'), may hold values from -0.29882812 to 0.29882812
- quad_nodes: float32 [512, 8], replicated, may hold values from -3 to 3
- quad_weights: float32 [512], replicated, may hold values from 0.0009765625 to 0.00390625
- gap_nominal: float32 [512], replicated, may hold values from 1 to 2
- pressure_load: float32 [512], replicated, may hold values from 0.2 to 0.6
- degrees: int32 [256, 8], replicated, may hold values from 0 to 4, as said below
Outputs:
- residual: float32 [256, 64, 4096], P('mode', 'space')
- tangent: float32 [256, 64, 4096], P('mode', 'space')
Inputs may be any that keep to these rules, and one draw needn't show every extreme that they name: `degrees`: the rows are distinct multi-indices of total degree at most 4 in order of non-decreasing total degree: every multi-index of a total degree appears before any of a higher one, and all of each lower total degree are present.
All inputs are finite; a program needn't handle non-finite values.
Results may differ from a plain program's by a relative error of at most 0.007.
Values may be sent and summed in bfloat16 or wider, within the bound.
No kernel may reach another device: no remote copies, remote signals or barrier semaphores. Data moves between devices by JAX's collectives and lax.ppermute only.
A program may use at most 128 MiB of HBM per device.

v0:
```python
import jax
import jax.numpy as jnp
from jax import lax
from jax.sharding import PartitionSpec as P

HALF_ROOT = 0.7071067811865476
THIRD_NORM = 0.4082482904638631
FOURTH_NORM = 0.2041241452319315
FLOOR = 0.3
STEEP = 4.0
STIFF = 0.1


def with_halo(cells, sides, width):
    for axis, dim in sides:
        count = lax.axis_size(axis)
        ends = count - 1
        head = lax.slice_in_dim(cells, 0, width, axis=dim)
        tail = lax.slice_in_dim(cells, cells.shape[dim] - width, cells.shape[dim], axis=dim)
        cells = jnp.concatenate(
            [
                lax.ppermute(tail, axis, [(i, (i + 1) % count) for i in range(ends)]),
                cells,
                lax.ppermute(head, axis, [((i + 1) % count, i) for i in range(ends)]),
            ],
            axis=dim,
        )
    return cells


def basis(quad_nodes, degrees):
    points = quad_nodes[None, :, :]
    degree_grid = degrees[:, None, :]
    square = points * points
    third = (square * points - 3.0 * points) * THIRD_NORM
    fourth = (square * square - 6.0 * square + 3.0) * FOURTH_NORM
    second = (square - 1.0) * HALF_ROOT
    factor = jnp.where(
        degree_grid == 0,
        1.0,
        jnp.where(
            degree_grid == 1,
            points,
            jnp.where(degree_grid == 2, second, jnp.where(degree_grid == 3, third, fourth)),
        ),
    )
    return jnp.prod(factor, axis=2).astype(jnp.bfloat16)


def quad_forces(
    first_field, second_field, table, table_t, quad_weights, gap_nominal, pressure_load
):
    count = first_field.shape[0]
    height = first_field.shape[1]
    breadth = first_field.shape[2]
    first = first_field.reshape(count, height * breadth)
    second = second_field.reshape(count, height * breadth)
    values_q = jnp.dot(table_t, first, preferred_element_type=jnp.float32)
    probe_q = jnp.dot(table_t, second, preferred_element_type=jnp.float32)
    shifted = STEEP * (gap_nominal[:, None] - values_q - FLOOR)
    gap = FLOOR + jax.nn.softplus(shifted) / STEEP
    pressure = pressure_load[:, None] / (gap * gap)
    slope_q = 2.0 * pressure_load[:, None] * jax.nn.sigmoid(shifted) / (gap * gap * gap)
    weighted = (quad_weights[:, None] * pressure).astype(jnp.bfloat16)
    weighted_t = (quad_weights[:, None] * slope_q * probe_q).astype(jnp.bfloat16)
    force = jnp.dot(table, weighted, preferred_element_type=jnp.float32).astype(jnp.bfloat16)
    force_t = jnp.dot(table, weighted_t, preferred_element_type=jnp.float32).astype(jnp.bfloat16)
    return (force.reshape(count, height, breadth), force_t.reshape(count, height, breadth))


def column_moved(field, across):
    if across == 0:
        return field
    zero_cols = jnp.zeros(field.shape[:-1] + (abs(across),), field.dtype)
    if across > 0:
        return jnp.concatenate([field[..., across:], zero_cols], axis=-1)
    return jnp.concatenate([zero_cols, field[..., :across]], axis=-1)


def biharm_rows(row_padded):
    height = row_padded.shape[-2] - 4

    def offset_view(down, across):
        return column_moved(row_padded[..., 2 + down : 2 + down + height, :], across)

    center = 20.0 * offset_view(0, 0)
    near = offset_view(1, 0) + offset_view(-1, 0) + offset_view(0, 1) + offset_view(0, -1)
    corner = offset_view(1, 1) + offset_view(1, -1) + offset_view(-1, 1) + offset_view(-1, -1)
    far = offset_view(2, 0) + offset_view(-2, 0) + offset_view(0, 2) + offset_view(0, -2)
    return center - 8.0 * near + 2.0 * corner + far


def shards(displacement, direction, quad_nodes, quad_weights, gap_nominal, pressure_load, degrees):
    table = basis(quad_nodes, degrees)
    table_t = table.T
    force_node, force_t_node = quad_forces(
        lax.all_to_all(displacement, "mode", split_axis=2, concat_axis=0, tiled=True),
        lax.all_to_all(direction, "mode", split_axis=2, concat_axis=0, tiled=True),
        table,
        table_t,
        quad_weights,
        gap_nominal,
        pressure_load,
    )
    force = lax.all_to_all(force_node, "mode", split_axis=0, concat_axis=2, tiled=True)
    force_t = lax.all_to_all(force_t_node, "mode", split_axis=0, concat_axis=2, tiled=True)
    padded_disp, padded_dir = (
        with_halo(displacement, (("space", 1),), 2),
        with_halo(direction, (("space", 1),), 2),
    )
    res_out = STIFF * biharm_rows(padded_disp.astype(jnp.float32)) - force.astype(jnp.float32)
    tan_out = STIFF * biharm_rows(padded_dir.astype(jnp.float32)) - force_t.astype(jnp.float32)
    return (res_out, tan_out)


def solution(mesh):
    in_specs = (P("mode", "space", None), P("mode", "space", None), P(), P(), P(), P(), P())
    out_specs = (P("mode", "space", None), P("mode", "space", None))
    return jax.shard_map(shards, mesh=mesh, in_specs=in_specs, out_specs=out_specs, check_vma=False)
```

profile of v0, /device:TPU:1, one launch (start us, length us, event | category | flops | bytes accessed | tf_op | source)
XLA Modules:
  0.0 216.6 jit_solution(8305561297586313336)
XLA Ops:
  0.6 8.6 %copy.83 = bf16[16,8,4096]{0,1,2:T(8,128)(2,1)} copy(bf16[16,8,4096]{2,1,0:T(8,128)(2,1)} %param.7) | data formatting | bytes 2097152 | tf_op args[0]
  9.2 11.2 %reshape.63 = bf16[16,2,16384]{2,1,0:T(2,128)(2,1)} reshape(bf16[4096,8,16]{2,1,0:T(8,128)(2,1)} %bitcast.36) | data formatting | bytes 2097152
  20.5 8.0 %all-to-all-start = ((bf16[16,2,16384]{2,1,0:T(2,128)(2,1)}), bf16[16,2,16384]{2,1,0:T(2,128)(2,1)}, u32[]{:S(2)}, u32[]{:S(2)}) async-start(bf16[16,2,16384]{2,1,0:T(2,128)(2,1)} %reshape.63), calls=%async_computation | async-start | bytes 2097152 | tf_op jit(solution)/shard_map/all_to_all | solution.py:97
  29.2 4.5 %collective-permute-start.2 = (bf16[16,2,4096]{2,0,1:T(8,128)(2,1)S(1)}, bf16[16,2,4096]{2,0,1:T(8,128)(2,1)S(1)}, u32[]{:S(2)}, u32[]{:S(2)}) collective-permute-start(bf16[16,2,4096]{2,0,1:T(8,128)(2,1)S(1)} %copy.95), channel_id=1, source_target_pairs={{0,16},{16,32},{32,48},{48,64},{64,80},{80,96},{96,112},{1,17},{17... | collective-permute-start | bytes 786440 | tf_op jit(solution)/shard_map/ppermute | solution.py:22
  37.3 6.2 %collective-permute-start = (bf16[16,2,4096]{2,0,1:T(8,128)(2,1)}, bf16[16,2,4096]{2,0,1:T(8,128)(2,1)}, u32[]{:S(2)}, u32[]{:S(2)}) collective-permute-start(bf16[16,2,4096]{2,0,1:T(8,128)(2,1)} %copy.93), channel_id=1, source_target_pairs={{0,16},{16,32},{32,48},{48,64},{64,80},{80,96},{96,112},{1,17},{17... | collective-permute-start | bytes 786440 | tf_op jit(solution)/shard_map/ppermute | solution.py:22
  44.3 1.5 collective-permute-start.1
  46.5 2.2 %select_reduce_fusion = bf16[256,512]{1,0:T(8,128)(2,1)S(1)} fusion(f32[512,8]{0,1:T(8,128)S(1)} %get-tuple-element.23, f32[512,8]{0,1:T(8,128)S(1)} %get-tuple-element.24, f32[512,8]{0,1:T(8,128)S(1)} %get-tuple-element.22, f32[512,8]{0,1:T(8,128)S(1)} %copy-done.11, pred[256,8]{1,0:T(8,128)(4,1)S(1)} %copy.82, pred[256,8]{1,0:T(8,128)(4,1)S(1)} %copy.81, ...), kind=kLoop, calls=%fused_computation.11 | loop fusion | flops 5111808 | bytes 335872 | tf_op jit(solution)/shard_map/reduce_prod | solution.py:47
  48.8 7.4 %copy.90 = bf16[16,8,4096]{0,1,2:T(8,128)(2,1)} copy(bf16[16,8,4096]{2,1,0:T(8,128)(2,1)S(1)} %copy-done.7) | data formatting | bytes 2097152 | tf_op args[1]
  56.2 11.2 %reshape.65 = bf16[16,2,16384]{2,1,0:T(2,128)(2,1)} reshape(bf16[4096,8,16]{2,1,0:T(8,128)(2,1)} %bitcast.37) | data formatting | bytes 2097152
  69.8 5.2 %fusion.51 = (f32[16,8,4095]{2,1,0:T(8,128)S(1)}, f32[16,8,4095]{2,1,0:T(8,128)}, f32[16,8,4095]{2,1,0:T(8,128)}, f32[16,8,4095]{2,1,0:T(8,128)}, f32[16,8,4095]{2,1,0:T(8,128)}, /*index=5*/f32[16,8,4095]{2,1,0:T(8,128)}) fusion(f32[16,12,4096]{2,1,0:T(8,128)S(1)} %maximum_convert_fusion.1), kind=kLoop, calls=%fused_computation.73 | loop fusion | bytes 25159680 | tf_op jit(solution)/shard_map/slice | solution.py:76
  78.4 1.9 copy-done.1
  80.4 5.4 %fusion.53 = (f32[16,8,4095]{2,1,0:T(8,128)}, f32[16,8,4095]{2,1,0:T(8,128)}, f32[16,8,4095]{2,1,0:T(8,128)}, f32[16,8,4095]{2,1,0:T(8,128)}, f32[16,8,4095]{2,1,0:T(8,128)}, /*index=5*/f32[16,8,4095]{2,1,0:T(8,128)}) fusion(f32[16,12,4096]{2,1,0:T(8,128)S(1)} %maximum_convert_fusion), kind=kLoop, calls=%fused_computation.75 | loop fusion | bytes 25159680 | tf_op jit(solution)/shard_map/slice | solution.py:76
  85.8 6.0 %all-to-all-start.2 = ((bf16[16,2,16384]{2,1,0:T(2,128)(2,1)}), bf16[16,2,16384]{2,1,0:T(2,128)(2,1)S(1)}, u32[]{:S(2)}, u32[]{:S(2)}) async-start(bf16[16,2,16384]{2,1,0:T(2,128)(2,1)} %reshape.65), calls=%async_computation.2 | async-start | bytes 2097152 | tf_op jit(solution)/shard_map/all_to_all | solution.py:98
  91.8 6.1 %fusion.52 = (f32[16,8,4094]{2,1,0:T(8,128)}, f32[16,8,4094]{2,1,0:T(8,128)}) fusion(f32[16,12,4096]{2,1,0:T(8,128)} %copy-done), kind=kLoop, calls=%fused_computation.74 | loop fusion | bytes 8384512 | tf_op jit(solution)/shard_map/slice | solution.py:76
  97.9 9.0 %reshape.64 = bf16[4096,8,16]{2,1,0:T(8,128)(2,1)} reshape(bf16[16,2,16384]{2,1,0:T(2,128)(2,1)} %all-to-all-done) | data formatting | bytes 2097152
  106.9 9.4 %copy.84 = bf16[16,8,16,256]{3,1,0,2:T(8,128)(2,1)} copy(bf16[16,8,16,256]{0,1,3,2:T(8,128)(2,1)} %bitcast.34) | data formatting | bytes 2097152 | tf_op jit(solution)/shard_map/all_to_all | solution.py:97
  116.3 2.5 %copy.97 = bf16[32,8,8,256]{3,1,2,0:T(8,128)(2,1)} copy(bf16[32,8,8,256]{3,2,1,0:T(8,128)(2,1)} %bitcast.41) | data formatting | bytes 2097152
  118.8 7.6 %reshape.66 = bf16[4096,8,16]{2,1,0:T(8,128)(2,1)} reshape(bf16[16,2,16384]{2,1,0:T(2,128)(2,1)S(1)} %all-to-all-done.2) | data formatting | bytes 2097152
  126.3 8.6 %copy.91 = bf16[16,8,16,256]{3,1,0,2:T(8,128)(2,1)S(1)} copy(bf16[16,8,16,256]{0,1,3,2:T(8,128)(2,1)} %bitcast.35) | data formatting | bytes 2097152 | tf_op jit(solution)/shard_map/all_to_all | solution.py:98
  136.2 2.7 %fusion.57 = f32[512,2048]{1,0:T(8,128)} fusion(bf16[256,512]{1,0:T(8,128)(2,1)S(1)} %select_reduce_fusion, bf16[256,2048]{1,0:T(8,128)(2,1)S(1)} %bitcast.45), kind=kOutput, calls=%fused_computation.79 | convolution fusion | flops 536870912 | bytes 5505024 | tf_op jit(solution)/shard_map/dot_general | solution.py:58
  138.9 8.9 %convolution_convert_fusion = bf16[256,2048]{1,0:T(8,128)(2,1)} fusion(f32[512,2048]{1,0:T(8,128)} %fusion.57, bf16[256,2048]{1,0:T(8,128)(2,1)S(1)} %bitcast.46, f32[512]{0:T(512)S(1)} %broadcast_multiply_fusion, f32[512]{0:T(512)S(1)} %copy-done.14, f32[512]{0:T(512)S(1)} %copy-done.15, bf16[256,512]{1,0:T(8,128)(2,1)S(1)} %select_reduce_fusion), kind=kOutput, calls=%fused_computation.13 | convolution fusion | flops 1096286208 | bytes 6559744 | tf_op jit(solution)/shard_map/dot_general | solution.py:67
  147.8 2.6 %copy.100 = bf16[32,8,8,256]{3,2,1,0:T(8,128)(2,1)} copy(bf16[32,8,8,256]{3,1,2,0:T(8,128)(2,1)} %bitcast.47) | data formatting | bytes 2097152
  150.4 5.7 %all-to-all-start.3 = ((bf16[256,8,256]{2,1,0:T(8,128)(2,1)}), bf16[256,8,256]{2,1,0:T(8,128)(2,1)S(1)}, u32[]{:S(2)}, u32[]{:S(2)}) async-start(bf16[256,8,256]{2,1,0:T(8,128)(2,1)} %bitcast.44), calls=%async_computation.3 | async-start | bytes 2097152 | tf_op jit(solution)/shard_map/all_to_all | solution.py:106
  156.1 6.4 %convolution_convert_fusion.1 = bf16[256,2048]{1,0:T(8,128)(2,1)S(1)} fusion(f32[512,2048]{1,0:T(8,128)} %fusion.57, f32[512]{0:T(512)S(1)} %copy-done.14, f32[512]{0:T(512)S(1)} %copy-done.13, f32[512]{0:T(512)S(1)} %copy-done.15, bf16[256,512]{1,0:T(8,128)(2,1)S(1)} %select_reduce_fusion), kind=kOutput, calls=%fused_computation.14 | convolution fusion | flops 553123840 | bytes 5511168 | tf_op jit(solution)/shard_map/dot_general | solution.py:66
  163.7 8.2 %all-to-all-done.3 = bf16[256,8,256]{2,1,0:T(8,128)(2,1)S(1)} async-done(((bf16[256,8,256]{2,1,0:T(8,128)(2,1)}), bf16[256,8,256]{2,1,0:T(8,128)(2,1)S(1)}, u32[]{:S(2)}, u32[]{:S(2)}) %all-to-all-start.3) | async-done | bytes 1048608 | tf_op jit(solution)/shard_map/all_to_all | solution.py:106
  171.9 4.9 %all-to-all-start.1 = ((bf16[256,8,256]{2,1,0:T(8,128)(2,1)}), bf16[256,8,256]{2,1,0:T(8,128)(2,1)}, u32[]{:S(2)}, u32[]{:S(2)}) async-start(bf16[256,8,256]{2,1,0:T(8,128)(2,1)} %bitcast.43), calls=%async_computation.1 | async-start | bytes 2097152 | tf_op jit(solution)/shard_map/all_to_all | solution.py:105
  176.8 6.1 %fusion.54 = (f32[16,8,4094]{2,1,0:T(8,128)}, f32[16,8,4094]{2,1,0:T(8,128)}) fusion(f32[16,12,4096]{2,1,0:T(8,128)} %copy-done.1), kind=kLoop, calls=%fused_computation.76 | loop fusion | bytes 8384512 | tf_op jit(solution)/shard_map/slice | solution.py:76
  182.9 1.5 copy.92
  184.4 8.4 %all-to-all-done.1 = bf16[256,8,256]{2,1,0:T(8,128)(2,1)} async-done(((bf16[256,8,256]{2,1,0:T(8,128)(2,1)}), bf16[256,8,256]{2,1,0:T(8,128)(2,1)}, u32[]{:S(2)}, u32[]{:S(2)}) %all-to-all-start.1) | async-done | bytes 1048608 | tf_op jit(solution)/shard_map/all_to_all | solution.py:105
  192.9 2.9 %copy.85 = f32[16,16,8,256]{3,2,0,1:T(8,128)} copy(bf16[16,16,8,256]{3,2,1,0:T(8,128)(2,1)} %bitcast.10) | data formatting | bytes 3145728 | tf_op jit(solution)/shard_map/convert_element_type | solution.py:111
  195.8 14.0 %fusion.12 = f32[16,8,4096]{2,1,0:T(8,128)} fusion(f32[16,8,4096]{2,1,0:T(8,128)} %bitcast.39, f32[16,12,4096]{2,1,0:T(8,128)} %copy-done, f32[16,8,4094]{2,1,0:T(8,128)} %get-tuple-element.9, f32[16,8,4094]{2,1,0:T(8,128)} %get-tuple-element.8, f32[16,8,4095]{2,1,0:T(8,128)S(1)} %copy-done.3, f32[16,8,4095]{2,1,0:T(8,128)} %get-tuple-element.4, ...), kind=kLoop, calls=%fused_computation.20 | loop fusion | flops 8912896 | bytes 31452160 | tf_op jit(solution)/shard_map/sub | solution.py:112
  209.8 6.8 %fusion.22 = f32[16,8,4096]{2,1,0:T(8,128)} fusion(f32[16,8,4096]{2,1,0:T(8,128)} %bitcast.38, f32[16,12,4096]{2,1,0:T(8,128)S(1)} %copy-done.2, f32[16,8,4094]{2,1,0:T(8,128)} %get-tuple-element.17, f32[16,8,4094]{2,1,0:T(8,128)} %get-tuple-element.16, f32[16,8,4095]{2,1,0:T(8,128)S(1)} %copy-done.5, f32[16,8,4095]{2,1,0:T(8,128)S(1)} %copy-done.6, ...), kind=kLoop, calls=%fused_computation.33 | loop fusion | flops 8912896 | bytes 31452160 | tf_op jit(solution)/shard_map/sub | solution.py:111
  (59 shorter events, 14.2 us)
Async XLA Ops:
  20.5 8.0 %copy-start.7 = (bf16[16,8,4096]{2,1,0:T(8,128)(2,1)S(1)}, bf16[16,8,4096]{2,1,0:T(8,128)(2,1)}, u32[]{:S(2)}) copy-start(bf16[16,8,4096]{2,1,0:T(8,128)(2,1)} %param.8) | copy-start | bytes 3145732
  20.5 15.4 %copy-start.8 = (bf16[16,8,4096]{2,1,0:T(8,128)(2,1)S(1)}, bf16[16,8,4096]{2,1,0:T(8,128)(2,1)}, u32[]{:S(2)}) copy-start(bf16[16,8,4096]{2,1,0:T(8,128)(2,1)} %param.7) | copy-start | bytes 3145732
  20.5 65.3 %all-to-all-start = ((bf16[16,2,16384]{2,1,0:T(2,128)(2,1)}), bf16[16,2,16384]{2,1,0:T(2,128)(2,1)}, u32[]{:S(2)}, u32[]{:S(2)}) async-start(bf16[16,2,16384]{2,1,0:T(2,128)(2,1)} %reshape.63), calls=%async_computation | async-start | bytes 2097152 | tf_op jit(solution)/shard_map/all_to_all | solution.py:97
  28.5 17.3 %copy-start.12 = (s32[256,8]{0,1:T(8,128)S(1)}, s32[256,8]{0,1:T(8,128)}, u32[]{:S(2)}) copy-start(s32[256,8]{0,1:T(8,128)} %param.13) | copy-start | bytes 24580
  28.5 18.0 %copy-start.11 = (f32[512,8]{0,1:T(8,128)S(1)}, f32[512,8]{0,1:T(8,128)}, u32[]{:S(2)}) copy-start(f32[512,8]{0,1:T(8,128)} %param.9) | copy-start | bytes 49156
  29.2 38.2 %collective-permute-start.2 = (bf16[16,2,4096]{2,0,1:T(8,128)(2,1)S(1)}, bf16[16,2,4096]{2,0,1:T(8,128)(2,1)S(1)}, u32[]{:S(2)}, u32[]{:S(2)}) collective-permute-start(bf16[16,2,4096]{2,0,1:T(8,128)(2,1)S(1)} %copy.95), channel_id=1, source_target_pairs={{0,16},{16,32},{32,48},{48,64},{64,80},{80,96},{96,112},{1,17},{17... | collective-permute-start | bytes 786440 | tf_op jit(solution)/shard_map/ppermute | solution.py:22
  34.6 33.1 %collective-permute-start.3 = (bf16[16,2,4096]{2,0,1:T(8,128)(2,1)}, bf16[16,2,4096]{2,0,1:T(8,128)(2,1)}, u32[]{:S(2)}, u32[]{:S(2)}) collective-permute-start(bf16[16,2,4096]{2,0,1:T(8,128)(2,1)} %copy.96), channel_id=1, source_target_pairs={{16,0},{32,16},{48,32},{64,48},{80,64},{96,80},{112,96},{17,1},{33... | collective-permute-start | bytes 786440 | tf_op jit(solution)/shard_map/ppermute | solution.py:24
  37.3 37.8 %collective-permute-start = (bf16[16,2,4096]{2,0,1:T(8,128)(2,1)}, bf16[16,2,4096]{2,0,1:T(8,128)(2,1)}, u32[]{:S(2)}, u32[]{:S(2)}) collective-permute-start(bf16[16,2,4096]{2,0,1:T(8,128)(2,1)} %copy.93), channel_id=1, source_target_pairs={{0,16},{16,32},{32,48},{48,64},{64,80},{80,96},{96,112},{1,17},{17... | collective-permute-start | bytes 786440 | tf_op jit(solution)/shard_map/ppermute | solution.py:22
  44.3 32.0 %collective-permute-start.1 = (bf16[16,2,4096]{2,0,1:T(8,128)(2,1)}, bf16[16,2,4096]{2,0,1:T(8,128)(2,1)}, u32[]{:S(2)}, u32[]{:S(2)}) collective-permute-start(bf16[16,2,4096]{2,0,1:T(8,128)(2,1)} %copy.94), channel_id=1, source_target_pairs={{16,0},{32,16},{48,32},{64,48},{80,64},{96,80},{112,96},{17,1},{33... | collective-permute-start | bytes 786440 | tf_op jit(solution)/shard_map/ppermute | solution.py:24
  56.2 11.2 %copy-start.13 = (f32[512]{0:T(512)S(1)}, f32[512]{0:T(512)}, u32[]{:S(2)}) copy-start(f32[512]{0:T(512)} %param.12) | copy-start | bytes 6148
  69.8 5.2 %copy-start = (f32[16,12,4096]{2,1,0:T(8,128)}, f32[16,12,4096]{2,1,0:T(8,128)S(1)}, u32[]{:S(2)}) copy-start(f32[16,12,4096]{2,1,0:T(8,128)S(1)} %maximum_convert_fusion.1) | copy-start | bytes 9437188
  78.4 1.9 copy-start.1
  85.8 33.0 %all-to-all-start.2 = ((bf16[16,2,16384]{2,1,0:T(2,128)(2,1)}), bf16[16,2,16384]{2,1,0:T(2,128)(2,1)S(1)}, u32[]{:S(2)}, u32[]{:S(2)}) async-start(bf16[16,2,16384]{2,1,0:T(2,128)(2,1)} %reshape.65), calls=%async_computation.2 | async-start | bytes 2097152 | tf_op jit(solution)/shard_map/all_to_all | solution.py:98
  134.9 1.3 copy-start.9
  136.2 2.7 %copy-start.10 = (bf16[32,8,8,256]{3,1,2,0:T(8,128)(2,1)S(1)}, bf16[32,8,8,256]{3,1,2,0:T(8,128)(2,1)}, u32[]{:S(2)}) copy-start(bf16[32,8,8,256]{3,1,2,0:T(8,128)(2,1)} %copy.99) | copy-start | bytes 3145732
  136.2 2.7 %copy-start.14 = (f32[512]{0:T(512)S(1)}, f32[512]{0:T(512)}, u32[]{:S(2)}) copy-start(f32[512]{0:T(512)} %param.11) | copy-start | bytes 6148
  136.2 2.7 %copy-start.15 = (f32[512]{0:T(512)S(1)}, f32[512]{0:T(512)}, u32[]{:S(2)}) copy-start(f32[512]{0:T(512)} %param.10) | copy-start | bytes 6148
  150.4 21.5 %all-to-all-start.3 = ((bf16[256,8,256]{2,1,0:T(8,128)(2,1)}), bf16[256,8,256]{2,1,0:T(8,128)(2,1)S(1)}, u32[]{:S(2)}, u32[]{:S(2)}) async-start(bf16[256,8,256]{2,1,0:T(8,128)(2,1)} %bitcast.44), calls=%async_computation.3 | async-start | bytes 2097152 | tf_op jit(solution)/shard_map/all_to_all | solution.py:106
  171.9 21.0 %all-to-all-start.1 = ((bf16[256,8,256]{2,1,0:T(8,128)(2,1)}), bf16[256,8,256]{2,1,0:T(8,128)(2,1)}, u32[]{:S(2)}, u32[]{:S(2)}) async-start(bf16[256,8,256]{2,1,0:T(8,128)(2,1)} %bitcast.43), calls=%async_computation.1 | async-start | bytes 2097152 | tf_op jit(solution)/shard_map/all_to_all | solution.py:105
  192.9 2.9 %copy-start.3 = (f32[16,8,4095]{2,1,0:T(8,128)S(1)}, f32[16,8,4095]{2,1,0:T(8,128)}, u32[]{:S(2)}) copy-start(f32[16,8,4095]{2,1,0:T(8,128)} %get-tuple-element.3) | copy-start | bytes 6289924
  195.8 14.0 %copy-start.2 = (f32[16,12,4096]{2,1,0:T(8,128)S(1)}, f32[16,12,4096]{2,1,0:T(8,128)}, u32[]{:S(2)}) copy-start(f32[16,12,4096]{2,1,0:T(8,128)} %copy-done.1) | copy-start | bytes 9437188
  195.8 14.0 %copy-start.4 = (f32[16,8,4095]{2,1,0:T(8,128)S(1)}, f32[16,8,4095]{2,1,0:T(8,128)}, u32[]{:S(2)}) copy-start(f32[16,8,4095]{2,1,0:T(8,128)} %get-tuple-element.10) | copy-start | bytes 6289924
  195.8 14.0 %copy-start.5 = (f32[16,8,4095]{2,1,0:T(8,128)S(1)}, f32[16,8,4095]{2,1,0:T(8,128)}, u32[]{:S(2)}) copy-start(f32[16,8,4095]{2,1,0:T(8,128)} %get-tuple-element.11) | copy-start | bytes 6289924
  195.8 14.1 %copy-start.6 = (f32[16,8,4095]{2,1,0:T(8,128)S(1)}, f32[16,8,4095]{2,1,0:T(8,128)}, u32[]{:S(2)}) copy-start(f32[16,8,4095]{2,1,0:T(8,128)} %get-tuple-element.12) | copy-start | bytes 6289924
where the time goes:
time: 221 us; the launch traced here: 217 us
  local copies, waits for them, and re-layouts  118 us (53%)
  starting transfers between devices  38.1 us (17%)
  other arithmetic  24.8 us (11%)
  matrix products  17.9 us (8%)
  waiting for transfers between devices  16.6 us (8%)
    unnamed x46, local copies, waits for them, and re-layouts  67.5 us
    slice x4, local copies, waits for them, and re-layouts, column_moved(): return jnp.concatenate([field[..., across:], zero_cols], axis=-1)  22.8 us
    sub x1, other arithmetic, shards(): STIFF * biharm_rows(padded_dir.astype(jnp.float32))  14 us
    ppermute x2, starting transfers between devices, with_halo(): lax.ppermute(tail, axis, [(i, (i + 1) % count) for i in range(ends)])  10.7 us
    all_to_all x1, local copies, waits for them, and re-layouts, shards(): lax.all_to_all(displacement, 'mode', split_axis=2, concat_axis=0, tiled=T...  9.36 us
    dot_general x1, matrix products, quad_forces(): jnp.dot(table, weighted_t, preferred_element_type=jnp.float32)  8.87 us
    all_to_all x1, local copies, waits for them, and re-layouts, shards(): lax.all_to_all(direction, 'mode', split_axis=2, concat_axis=0, tiled=True)  8.56 us
    all_to_all x1, waiting for transfers between devices, shards(): lax.all_to_all(force_node, 'mode', split_axis=0, concat_axis=2, tiled=True)  8.43 us
  transfers between devices with their start and end apart: 8, of which 2 were waited for; matrix products, arithmetic and copies ran while one was open for 39% of the time, Pallas kernels for 0%

commit v1 on v0

v1 whole, which is shorter than its diff:
```python
import functools

import jax
import jax.numpy as jnp
from jax import lax
from jax.experimental import pallas as pl
from jax.experimental.pallas import tpu as pltpu
from jax.sharding import PartitionSpec as P

HALF_ROOT = 0.7071067811865476
THIRD_NORM = 0.4082482904638631
FOURTH_NORM = 0.2041241452319315
FLOOR = 0.3
STEEP = 4.0
STIFF = 0.1
LOG2E = 1.4426950408889634
LN2 = 0.6931471805599453
MIB = 1 << 20
F32 = jnp.float32
BF16 = jnp.bfloat16


def basis(quad_nodes, degrees):
    points = quad_nodes[None, :, :]
    degree_grid = degrees[:, None, :]
    square = points * points
    third = (square * points - 3.0 * points) * THIRD_NORM
    fourth = (square * square - 6.0 * square + 3.0) * FOURTH_NORM
    second = (square - 1.0) * HALF_ROOT
    factor = jnp.where(
        degree_grid == 0,
        1.0,
        jnp.where(
            degree_grid == 1,
            points,
            jnp.where(degree_grid == 2, second, jnp.where(degree_grid == 3, third, fourth)),
        ),
    )
    return jnp.prod(factor, axis=2).astype(BF16)


def iotas(shape):
    return lax.broadcasted_iota(jnp.int32, shape, 0), lax.broadcasted_iota(jnp.int32, shape, 1)


def one_hot(hit):
    return jnp.where(hit, 1.0, 0.0).astype(BF16)


def pack_kernel(dests, disp_ref, dir_ref, send_ref, low_ref, high_ref):
    modes, rows, width = disp_ref.shape
    both = 2 * modes
    size = both * rows
    to, frm = iotas((size, size))
    perm = one_hot(frm == (to % both) * rows + to // both)
    each = width // dests
    for d in range(dests):
        cols = pl.ds(d * each, each)
        fields = jnp.concatenate(
            [disp_ref[:, :, cols].reshape(modes * rows, each), dir_ref[:, :, cols].reshape(modes * rows, each)], axis=0
        )
        moved = jnp.dot(perm, fields, preferred_element_type=F32).astype(BF16).reshape(rows, both, each)
        send_ref[d] = moved
        low_ref[:, :, cols] = moved[:2]
        high_ref[:, :, cols] = moved[rows - 2 :]


def pack(displacement, direction, count, dests=4):
    modes, rows, width = displacement.shape
    each = width // count
    both = 2 * modes
    field = pl.BlockSpec((modes, rows, dests * each), lambda i: (0, 0, i))
    edge = pl.BlockSpec((2, both, dests * each), lambda i: (0, 0, i))
    return pl.pallas_call(
        functools.partial(pack_kernel, dests),
        grid=(count // dests,),
        in_specs=[field, field],
        out_specs=[pl.BlockSpec((dests, rows, both, each), lambda i: (i, 0, 0, 0)), edge, edge],
        out_shape=[
            jax.ShapeDtypeStruct((count, rows, both, each), BF16),
            jax.ShapeDtypeStruct((2, both, width), BF16),
            jax.ShapeDtypeStruct((2, both, width), BF16),
        ],
        compiler_params=pltpu.CompilerParams(vmem_limit_bytes=16 * MIB),
        cost_estimate=pl.CostEstimate(flops=2 * (2 * modes * rows) ** 2 * width, bytes_accessed=5 * MIB, transcendentals=0),
        name="pack",
    )(displacement, direction)


def quad_kernel(chunk, got_ref, table_t_ref, table_w_ref, shift_ref, out_ref, w_ref, wt_ref):
    count, _, both, width = got_ref.shape
    modes = both // 2
    quad = table_t_ref.shape[0]
    total = count * modes
    disp = got_ref[:, 0, :modes, :].reshape(total, width)
    dire = got_ref[:, 0, modes:, :].reshape(total, width)
    for q in range(quad // chunk):
        at = pl.ds(q * chunk, chunk)
        left = table_t_ref[at, :]
        shift = shift_ref[at, :]
        shift = jnp.concatenate([shift] * (width // shift.shape[1]), axis=1)
        s = shift - STEEP * jnp.dot(left, disp, preferred_element_type=F32)
        probe = jnp.dot(left, dire, preferred_element_type=F32)
        e = jnp.exp2(jnp.abs(s) * (-LOG2E))
        one = 1.0 + e
        gap = (jnp.maximum(s, 0.0) * (1.0 / STEEP) + FLOOR) + jnp.log2(one) * (LN2 / STEEP)
        sig = jnp.where(s >= 0.0, 1.0, e) * pl.reciprocal(one, approx=True)
        inv = pl.reciprocal(gap, approx=True)
        square = inv * inv
        w_ref[at, :] = square.astype(BF16)
        wt_ref[at, :] = (sig * (inv + inv) * square * probe).astype(BF16)
    table_w = table_w_ref[...]
    force = jnp.dot(table_w, w_ref[...], preferred_element_type=F32).astype(BF16)
    force_t = jnp.dot(table_w, wt_ref[...], preferred_element_type=F32).astype(BF16)
    out_ref[:, 0, :modes, :] = force.reshape(count, modes, width)
    out_ref[:, 0, modes:, :] = force_t.reshape(count, modes, width)


def quad_forces(got, table_t, table_w, shift):
    count, rows, both, width = got.shape
    quad, total = table_t.shape
    block = pl.BlockSpec((count, 1, both, width), lambda i: (0, i, 0, 0))
    return pl.pallas_call(
        functools.partial(quad_kernel, 128),
        grid=(rows,),
        in_specs=[
            block,
            pl.BlockSpec((quad, total), lambda i: (0, 0)),
            pl.BlockSpec((total, quad), lambda i: (0, 0)),
            pl.BlockSpec(shift.shape, lambda i: (0, 0)),
        ],
        out_specs=block,
        out_shape=jax.ShapeDtypeStruct(got.shape, BF16),
        scratch_shapes=[pltpu.VMEM((quad, width), BF16), pltpu.VMEM((quad, width), BF16)],
        compiler_params=pltpu.CompilerParams(vmem_limit_bytes=16 * MIB),
        cost_estimate=pl.CostEstimate(
            flops=8 * quad * total * rows * width, bytes_accessed=5 * MIB, transcendentals=4 * quad * rows * width
        ),
        name="quad_forces",
    )(got, table_t, table_w, shift)


def stencil_kernel(chunk, x_ref, above_ref, below_ref, out_ref, side_ref):
    modes, rows, width = x_ref.shape
    size = modes * rows
    edge = 2 * modes
    span = size + 2 * edge
    to, frm = iotas((size, span))
    late = frm - size
    outer = late // modes
    row_in = jnp.where(late < 0, frm % rows, jnp.where(outer < 2, outer - 2, outer + rows - 2))
    mode_in = jnp.where(late < 0, frm // rows, late % modes)
    gap = jnp.abs(row_in - to % rows)
    same = mode_in == to // rows

    def weights(zero, one, two):
        value = jnp.where(gap == 0, zero, jnp.where(gap == 1, one, jnp.where(gap == 2, two, 0.0)))
        return jnp.where(same, value, 0.0).astype(BF16)

    centre = weights(20.0, -8.0, 1.0)
    side = weights(-8.0, 2.0, 0.0)
    for c in range(width // chunk):
        cols = pl.ds(c * chunk, chunk)
        operand = jnp.concatenate(
            [
                x_ref[:, :, cols].reshape(size, chunk),
                above_ref[:, :, cols].reshape(edge, chunk),
                below_ref[:, :, cols].reshape(edge, chunk),
            ],
            axis=0,
        )
        out_ref[:, :, cols] = jnp.dot(centre, operand, preferred_element_type=F32).reshape(modes, rows, chunk)
        side_ref[:, :, cols] = jnp.dot(side, operand, preferred_element_type=F32).reshape(modes, rows, chunk)
    lane = lax.broadcasted_iota(jnp.int32, (rows, width), 1)

    def one_mode(m, _):
        x = x_ref[m].astype(F32)
        y = side_ref[m]

        def from_right(v):
            return jnp.where(lane == width - 1, 0.0, pltpu.roll(v, width - 1, 1))

        def from_left(v):
            return jnp.where(lane == 0, 0.0, pltpu.roll(v, 1, 1))

        total = out_ref[m] + from_right(y + from_right(x)) + from_left(y + from_left(x))
        out_ref[m] = STIFF * total
        return 0

    lax.fori_loop(0, modes, one_mode, 0)


def stencil(x, above, below, field):
    modes, rows, width = x.shape
    edge = pl.BlockSpec((2, modes, width), lambda i: (0, field, 0))
    whole = pl.BlockSpec((modes, rows, width), lambda i: (0, 0, 0))
    return pl.pallas_call(
        functools.partial(stencil_kernel, 512),
        grid=(1,),
        in_specs=[whole, edge, edge],
        out_specs=whole,
        out_shape=jax.ShapeDtypeStruct(x.shape, F32),
        scratch_shapes=[pltpu.VMEM(x.shape, F32)],
        compiler_params=pltpu.CompilerParams(vmem_limit_bytes=20 * MIB),
        cost_estimate=pl.CostEstimate(flops=4 * 128 * 192 * 4096 * 2, bytes_accessed=4 * MIB, transcendentals=0),
        name="stencil",
    )(x, above, below)


def merge_kernel(sources, force_ref, res_ref, tan_ref, res_out, tan_out):
    _, rows, both, each = force_ref.shape
    modes = both // 2
    size = both * rows
    to, frm = iotas((size, size))
    perm = one_hot(frm == (to % rows) * both + to // rows)
    for d in range(sources):
        cols = pl.ds(d * each, each)
        moved = jnp.dot(perm, force_ref[d].reshape(size, each), preferred_element_type=F32)
        moved = moved.reshape(both, rows, each)
        res_out[:, :, cols] = res_ref[:, :, cols] - moved[:modes]
        tan_out[:, :, cols] = tan_ref[:, :, cols] - moved[modes:]


def merge(force, res, tan, sources=4):
    count, rows, both, each = force.shape
    modes = both // 2
    field = pl.BlockSpec((modes, rows, sources * each), lambda i: (0, 0, i))
    return pl.pallas_call(
        functools.partial(merge_kernel, sources),
        grid=(count // sources,),
        in_specs=[pl.BlockSpec((sources, rows, both, each), lambda i: (i, 0, 0, 0)), field, field],
        out_specs=[field, field],
        out_shape=[jax.ShapeDtypeStruct(res.shape, F32)] * 2,
        compiler_params=pltpu.CompilerParams(vmem_limit_bytes=20 * MIB),
        cost_estimate=pl.CostEstimate(flops=2 * (both * rows) ** 2 * each * count, bytes_accessed=10 * MIB, transcendentals=0),
        name="merge",
    )(force, res, tan)


def shards(displacement, direction, quad_nodes, quad_weights, gap_nominal, pressure_load, degrees):
    count = lax.axis_size("mode")
    bands = lax.axis_size("space")
    send, low, high = pack(displacement, direction, count)
    got = lax.all_to_all(send, "mode", split_axis=0, concat_axis=0, tiled=True)
    above = lax.ppermute(high, "space", [(i, i + 1) for i in range(bands - 1)])
    below = lax.ppermute(low, "space", [(i + 1, i) for i in range(bands - 1)])
    table = basis(quad_nodes, degrees)
    table_w = (table.astype(F32) * (quad_weights * pressure_load)[None, :]).astype(BF16)
    shift = jnp.broadcast_to((STEEP * (gap_nominal - FLOOR))[:, None], (gap_nominal.shape[0], 128))
    force = quad_forces(got, table.T, table_w, shift)
    back = lax.all_to_all(force, "mode", split_axis=0, concat_axis=0, tiled=True)
    res = stencil(displacement, above, below, 0)
    tan = stencil(direction, above, below, 1)
    return tuple(merge(back, res, tan))


def solution(mesh):
    in_specs = (P("mode", "space", None), P("mode", "space", None), P(), P(), P(), P(), P())
    out_specs = (P("mode", "space", None), P("mode", "space", None))
    return jax.shard_map(shards, mesh=mesh, in_specs=in_specs, out_specs=out_specs, check_vma=False)
```

time: 221 us -> 122 us (0.55)
  the two profiles are of different devices: /device:TPU:1 before, /device:TPU:2 now
where the time goes in v1:
time: 122 us
  waiting for transfers between devices  66.6 us (55%)
  Pallas kernels  19.7 us (16%)
  starting transfers between devices  18.8 us (15%)
  local copies, waits for them, and re-layouts  13.4 us (11%)
  other arithmetic  2.3 us (2%)
    ppermute x1, waiting for transfers between devices, shards(): above = lax.ppermute(high, 'space', [(i, i + 1) for i in range(bands - 1)])  38.7 us
    all_to_all x1, waiting for transfers between devices, shards(): got = lax.all_to_all(send, 'mode', split_axis=0, concat_axis=0, tiled=True)  24.7 us
    unnamed x34, local copies, waits for them, and re-layouts  12.5 us
    pallas_call x2, Pallas kernels, stencil(): pl.pallas_call(functools.partial(stencil_kernel, 512), grid=(1,), in_spec...  8.23 us
    pallas_call x1, Pallas kernels, quad_forces(): pl.pallas_call(functools.partial(quad_kernel, 128), grid=(rows,), in_spec...  6.92 us
    all_to_all x1, starting transfers between devices, shards(): got = lax.all_to_all(send, 'mode', split_axis=0, concat_axis=0, tiled=True)  6.57 us
    ppermute x1, starting transfers between devices, shards(): above = lax.ppermute(high, 'space', [(i, i + 1) for i in range(bands - 1)])  4.82 us
    all_to_all x1, starting transfers between devices, shards(): lax.all_to_all(force, 'mode', split_axis=0, concat_axis=0, tiled=True)  3.85 us
  transfers between devices with their start and end apart: 4, of which 3 were waited for; matrix products, arithmetic and copies ran while one was open for 3% of the time, Pallas kernels for 7%

profile of v1, /device:TPU:2, one launch (start us, length us, event | category | flops | bytes accessed | tf_op | source)
XLA Modules:
  0.0 121.7 jit_solution(9793341543242514814)
XLA Ops:
  0.6 1.2 copy-done.4
  1.9 1.2 %copy-done.6 = bf16[16,8,4096]{2,1,0:T(8,128)(2,1)S(1)} copy-done((bf16[16,8,4096]{2,1,0:T(8,128)(2,1)S(1)}, bf16[16,8,4096]{2,1,0:T(8,128)(2,1)}, u32[]{:S(2)}) %copy-start.6) | copy-done | bytes 1048600
  3.1 1.5 %pack.1 = (bf16[16,8,32,256]{3,2,1,0:T(8,128)(2,1)S(1)}, bf16[2,32,4096]{2,1,0:T(8,128)(2,1)S(1)}, bf16[2,32,4096]{2,1,0:T(8,128)(2,1)S(1)}) custom-call(bf16[16,8,4096]{2,1,0:T(8,128)(2,1)S(1)} %copy-done.6, bf16[16,8,4096]{2,1,0:T(8,128)(2,1)S(1)} %copy-done.4), custom_call_target="tpu_custom_call" | custom-call | flops 536870912 | bytes 5242880 | tf_op jit(solution)/shard_map/pack/pallas_call | solution.py:74
  4.6 0.0 copy-start.8
  4.6 1.3 %copy-done.8 = bf16[16,8,32,256]{3,2,1,0:T(8,128)(2,1)} copy-done((bf16[16,8,32,256]{3,2,1,0:T(8,128)(2,1)}, bf16[16,8,32,256]{3,2,1,0:T(8,128)(2,1)S(1)}, u32[]{:S(2)}) %copy-start.8) | copy-done | bytes 2097176
  5.9 0.8 copy-done.10
  6.7 0.8 copy-done.11
  7.5 0.0 copy-start.16
  7.5 6.6 %all-to-all-start = ((bf16[16,8,32,256]{3,2,1,0:T(8,128)(2,1)}), bf16[16,8,32,256]{3,2,1,0:T(8,128)(2,1)S(1)}, u32[]{:S(2)}, u32[]{:S(2)}) async-start(bf16[16,8,32,256]{3,2,1,0:T(8,128)(2,1)} %copy-done.8), calls=%async_computation | async-start | bytes 4194304 | tf_op jit(solution)/shard_map/all_to_all | solution.py:244
  14.1 0.2 copy.18
  14.3 0.2 copy.19
  14.5 0.2 copy.21
  14.6 0.2 copy.20
  14.8 2.2 %select_reduce_fusion = bf16[256,512]{1,0:T(8,128)(2,1)S(1)} fusion(f32[512,8]{0,1:T(8,128)S(1)} %get-tuple-element.9, f32[512,8]{0,1:T(8,128)S(1)} %get-tuple-element.10, f32[512,8]{0,1:T(8,128)S(1)} %get-tuple-element.8, f32[512,8]{0,1:T(8,128)S(1)} %copy-done.12, pred[256,8]{1,0:T(8,128)(4,1)S(1)} %copy.21, pred[256,8]{1,0:T(8,128)(4,1)S(1)} %copy.20, ...), kind=kLoop, calls=%fused_computation | loop fusion | flops 5111808 | bytes 335872 | tf_op jit(solution)/shard_map/reduce_prod | solution.py:39
  17.1 0.1 copy.22.table_t_ref
  17.3 24.7 %all-to-all-done.got_ref = bf16[16,8,32,256]{3,2,1,0:T(8,128)(2,1)S(1)} async-done(((bf16[16,8,32,256]{3,2,1,0:T(8,128)(2,1)}), bf16[16,8,32,256]{3,2,1,0:T(8,128)(2,1)S(1)}, u32[]{:S(2)}, u32[]{:S(2)}) %all-to-all-start) | async-done | bytes 2097184 | tf_op jit(solution)/shard_map/all_to_all | solution.py:244
  42.0 0.1 broadcast_in_dim.80.shift_ref
  42.1 6.9 %quad_forces.1 = bf16[16,8,32,256]{3,2,1,0:T(8,128)(2,1)S(1)} custom-call(bf16[16,8,32,256]{3,2,1,0:T(8,128)(2,1)S(1)} %all-to-all-done.got_ref, bf16[512,256]{1,0:T(8,128)(2,1)S(1)} %copy.22.table_t_ref, bf16[256,512]{1,0:T(8,128)(2,1)S(1)} %multiply_convert_fusion.table_w_ref, f32[512,128]{1,0:T(8,128)S(1)} %broadcast_in_dim.80.shift_ref), custom_call_target="tpu_custom_call" | custom-call | flops 2147483648 | bytes 5242880 | tf_op jit(solution)/shard_map/quad_forces/pallas_call | solution.py:123
  49.0 0.0 copy-start.9
  49.0 1.3 %copy-done.9 = bf16[16,8,32,256]{3,2,1,0:T(8,128)(2,1)} copy-done((bf16[16,8,32,256]{3,2,1,0:T(8,128)(2,1)}, bf16[16,8,32,256]{3,2,1,0:T(8,128)(2,1)S(1)}, u32[]{:S(2)}) %copy-start.9) | copy-done | bytes 2097176
  50.4 3.9 %all-to-all-start.1 = ((bf16[16,8,32,256]{3,2,1,0:T(8,128)(2,1)}), bf16[16,8,32,256]{3,2,1,0:T(8,128)(2,1)S(1)}, u32[]{:S(2)}, u32[]{:S(2)}) async-start(bf16[16,8,32,256]{3,2,1,0:T(8,128)(2,1)} %copy-done.9), calls=%async_computation.1 | async-start | bytes 4194304 | tf_op jit(solution)/shard_map/all_to_all | solution.py:251
  54.2 4.8 %collective-permute-start = (bf16[2,32,4096]{2,1,0:T(8,128)(2,1)}, bf16[2,32,4096]{2,1,0:T(8,128)(2,1)S(1)}, u32[]{:S(2)}, u32[]{:S(2)}) collective-permute-start(bf16[2,32,4096]{2,1,0:T(8,128)(2,1)} %copy-done.11), channel_id=1, source_target_pairs={{0,16},{16,32},{32,48},{48,64},{64,80},{80,96},{96,112},{1,17},{17... | collective-permute-start | bytes 1572872 | tf_op jit(solution)/shard_map/ppermute | solution.py:245
  59.0 3.6 %collective-permute-start.1 = (bf16[2,32,4096]{2,1,0:T(8,128)(2,1)}, bf16[2,32,4096]{2,1,0:T(8,128)(2,1)S(1)}, u32[]{:S(2)}, u32[]{:S(2)}) collective-permute-start(bf16[2,32,4096]{2,1,0:T(8,128)(2,1)} %copy-done.10), channel_id=1, source_target_pairs={{16,0},{32,16},{48,32},{64,48},{80,64},{96,80},{112,96},{17,1},{33... | collective-permute-start | bytes 1572872 | tf_op jit(solution)/shard_map/ppermute | solution.py:246
  62.6 38.7 %collective-permute-done.above_ref = bf16[2,32,4096]{2,1,0:T(8,128)(2,1)S(1)} collective-permute-done((bf16[2,32,4096]{2,1,0:T(8,128)(2,1)}, bf16[2,32,4096]{2,1,0:T(8,128)(2,1)S(1)}, u32[]{:S(2)}, u32[]{:S(2)}) %collective-permute-start) | collective-permute-done | bytes 524320 | tf_op jit(solution)/shard_map/ppermute | solution.py:245
  101.3 3.3 %collective-permute-done.1.below_ref = bf16[2,32,4096]{2,1,0:T(8,128)(2,1)S(1)} collective-permute-done((bf16[2,32,4096]{2,1,0:T(8,128)(2,1)}, bf16[2,32,4096]{2,1,0:T(8,128)(2,1)S(1)}, u32[]{:S(2)}, u32[]{:S(2)}) %collective-permute-start.1) | collective-permute-done | bytes 524320 | tf_op jit(solution)/shard_map/ppermute | solution.py:246
  104.6 4.1 %stencil.3.tan_ref = f32[16,8,4096]{2,1,0:T(8,128)S(1)} custom-call(bf16[16,8,4096]{2,1,0:T(8,128)(2,1)S(1)} %copy-done.5, bf16[2,32,4096]{2,1,0:T(8,128)(2,1)S(1)} %collective-permute-done.above_ref, bf16[2,32,4096]{2,1,0:T(8,128)(2,1)S(1)} %collective-permute-done.1.below_ref), custom_call_target="tpu_custom_call" | custom-call | flops 805306368 | bytes 4194304 | tf_op jit(solution)/shard_map/stencil/pallas_call | solution.py:197
  108.7 1.3 %copy-done = f32[16,8,4096]{2,1,0:T(8,128)} copy-done((f32[16,8,4096]{2,1,0:T(8,128)}, f32[16,8,4096]{2,1,0:T(8,128)S(1)}, u32[]{:S(2)}) %copy-start) | copy-done | bytes 2097176
  110.0 4.1 %stencil.2.res_ref = f32[16,8,4096]{2,1,0:T(8,128)S(1)} custom-call(bf16[16,8,4096]{2,1,0:T(8,128)(2,1)S(1)} %copy-done.7, bf16[2,32,4096]{2,1,0:T(8,128)(2,1)S(1)} %collective-permute-done.above_ref, bf16[2,32,4096]{2,1,0:T(8,128)(2,1)S(1)} %collective-permute-done.1.below_ref), custom_call_target="tpu_custom_call" | custom-call | flops 805306368 | bytes 4194304 | tf_op jit(solution)/shard_map/stencil/pallas_call | solution.py:197
  114.2 1.3 %copy-done.2 = f32[16,8,4096]{2,1,0:T(8,128)} copy-done((f32[16,8,4096]{2,1,0:T(8,128)}, f32[16,8,4096]{2,1,0:T(8,128)S(1)}, u32[]{:S(2)}) %copy-start.2) | copy-done | bytes 2097176
  115.5 1.6 %copy-done.1 = f32[16,8,4096]{2,1,0:T(8,128)S(1)} copy-done((f32[16,8,4096]{2,1,0:T(8,128)S(1)}, f32[16,8,4096]{2,1,0:T(8,128)}, u32[]{:S(2)}) %copy-start.1) | copy-done | bytes 2097176
  117.1 1.6 %copy-done.3 = f32[16,8,4096]{2,1,0:T(8,128)S(1)} copy-done((f32[16,8,4096]{2,1,0:T(8,128)S(1)}, f32[16,8,4096]{2,1,0:T(8,128)}, u32[]{:S(2)}) %copy-start.3) | copy-done | bytes 2097176
  118.7 3.1 %merge.1 = (f32[16,8,4096]{2,1,0:T(8,128)}, f32[16,8,4096]{2,1,0:T(8,128)}) custom-call(bf16[16,8,32,256]{3,2,1,0:T(8,128)(2,1)S(1)} %all-to-all-done.1.force_ref, f32[16,8,4096]{2,1,0:T(8,128)S(1)} %copy-done.3, f32[16,8,4096]{2,1,0:T(8,128)S(1)} %copy-done.1), custom_call_target="tpu_custom_call" | custom-call | flops 536870912 | bytes 10485760 | tf_op jit(solution)/shard_map/merge/pallas_call | solution.py:228
  (27 shorter events, 0.1 us)
Async XLA Ops:
  0.6 1.2 %copy-start.4 = (bf16[16,8,4096]{2,1,0:T(8,128)(2,1)S(1)}, bf16[16,8,4096]{2,1,0:T(8,128)(2,1)}, u32[]{:S(2)}) copy-start(bf16[16,8,4096]{2,1,0:T(8,128)(2,1)} %x_ref.3) | copy-start | bytes 3145732
  1.9 1.2 %copy-start.6 = (bf16[16,8,4096]{2,1,0:T(8,128)(2,1)S(1)}, bf16[16,8,4096]{2,1,0:T(8,128)(2,1)}, u32[]{:S(2)}) copy-start(bf16[16,8,4096]{2,1,0:T(8,128)(2,1)} %x_ref.2) | copy-start | bytes 3145732
  4.6 1.3 %copy-start.8 = (bf16[16,8,32,256]{3,2,1,0:T(8,128)(2,1)}, bf16[16,8,32,256]{3,2,1,0:T(8,128)(2,1)S(1)}, u32[]{:S(2)}) copy-start(bf16[16,8,32,256]{3,2,1,0:T(8,128)(2,1)S(1)} %get-tuple-element.5) | copy-start | bytes 6291460
  5.9 0.8 copy-start.10
  6.7 0.8 copy-start.11
  7.5 6.6 %copy-start.13 = (s32[256,8]{0,1:T(8,128)S(1)}, s32[256,8]{0,1:T(8,128)}, u32[]{:S(2)}) copy-start(s32[256,8]{0,1:T(8,128)} %param.13) | copy-start | bytes 24580
  7.5 7.3 %copy-start.12 = (f32[512,8]{0,1:T(8,128)S(1)}, f32[512,8]{0,1:T(8,128)}, u32[]{:S(2)}) copy-start(f32[512,8]{0,1:T(8,128)} %param.9) | copy-start | bytes 49156
  7.5 9.7 %copy-start.14 = (f32[512]{0:T(512)S(1)}, f32[512]{0:T(512)}, u32[]{:S(2)}) copy-start(f32[512]{0:T(512)} %param.10) | copy-start | bytes 6148
  7.5 9.7 %copy-start.15 = (f32[512]{0:T(512)S(1)}, f32[512]{0:T(512)}, u32[]{:S(2)}) copy-start(f32[512]{0:T(512)} %param.12) | copy-start | bytes 6148
  7.5 9.7 %copy-start.16 = (f32[512]{0:T(512)S(1)}, f32[512]{0:T(512)}, u32[]{:S(2)}) copy-start(f32[512]{0:T(512)} %param.11) | copy-start | bytes 6148
  7.5 34.5 %all-to-all-start = ((bf16[16,8,32,256]{3,2,1,0:T(8,128)(2,1)}), bf16[16,8,32,256]{3,2,1,0:T(8,128)(2,1)S(1)}, u32[]{:S(2)}, u32[]{:S(2)}) async-start(bf16[16,8,32,256]{3,2,1,0:T(8,128)(2,1)} %copy-done.8), calls=%async_computation | async-start | bytes 4194304 | tf_op jit(solution)/shard_map/all_to_all | solution.py:244
  49.0 1.3 %copy-start.9 = (bf16[16,8,32,256]{3,2,1,0:T(8,128)(2,1)}, bf16[16,8,32,256]{3,2,1,0:T(8,128)(2,1)S(1)}, u32[]{:S(2)}) copy-start(bf16[16,8,32,256]{3,2,1,0:T(8,128)(2,1)S(1)} %quad_forces.1) | copy-start | bytes 6291460
  50.3 54.2 %copy-start.5 = (bf16[16,8,4096]{2,1,0:T(8,128)(2,1)S(1)}, bf16[16,8,4096]{2,1,0:T(8,128)(2,1)}, u32[]{:S(2)}) copy-start(bf16[16,8,4096]{2,1,0:T(8,128)(2,1)} %x_ref.3) | copy-start | bytes 3145732
  50.4 65.1 %all-to-all-start.1 = ((bf16[16,8,32,256]{3,2,1,0:T(8,128)(2,1)}), bf16[16,8,32,256]{3,2,1,0:T(8,128)(2,1)S(1)}, u32[]{:S(2)}, u32[]{:S(2)}) async-start(bf16[16,8,32,256]{3,2,1,0:T(8,128)(2,1)} %copy-done.9), calls=%async_computation.1 | async-start | bytes 4194304 | tf_op jit(solution)/shard_map/all_to_all | solution.py:251
  54.2 47.1 %collective-permute-start = (bf16[2,32,4096]{2,1,0:T(8,128)(2,1)}, bf16[2,32,4096]{2,1,0:T(8,128)(2,1)S(1)}, u32[]{:S(2)}, u32[]{:S(2)}) collective-permute-start(bf16[2,32,4096]{2,1,0:T(8,128)(2,1)} %copy-done.11), channel_id=1, source_target_pairs={{0,16},{16,32},{32,48},{48,64},{64,80},{80,96},{96,112},{1,17},{17... | collective-permute-start | bytes 1572872 | tf_op jit(solution)/shard_map/ppermute | solution.py:245
  59.0 51.0 %copy-start.7 = (bf16[16,8,4096]{2,1,0:T(8,128)(2,1)S(1)}, bf16[16,8,4096]{2,1,0:T(8,128)(2,1)}, u32[]{:S(2)}) copy-start(bf16[16,8,4096]{2,1,0:T(8,128)(2,1)} %x_ref.2) | copy-start | bytes 3145732
  59.0 45.5 %collective-permute-start.1 = (bf16[2,32,4096]{2,1,0:T(8,128)(2,1)}, bf16[2,32,4096]{2,1,0:T(8,128)(2,1)S(1)}, u32[]{:S(2)}, u32[]{:S(2)}) collective-permute-start(bf16[2,32,4096]{2,1,0:T(8,128)(2,1)} %copy-done.10), channel_id=1, source_target_pairs={{16,0},{32,16},{48,32},{64,48},{80,64},{96,80},{112,96},{17,1},{33... | collective-permute-start | bytes 1572872 | tf_op jit(solution)/shard_map/ppermute | solution.py:246
  108.7 1.3 %copy-start = (f32[16,8,4096]{2,1,0:T(8,128)}, f32[16,8,4096]{2,1,0:T(8,128)S(1)}, u32[]{:S(2)}) copy-start(f32[16,8,4096]{2,1,0:T(8,128)S(1)} %stencil.3.tan_ref) | copy-start | bytes 6291460
  114.2 1.3 %copy-start.2 = (f32[16,8,4096]{2,1,0:T(8,128)}, f32[16,8,4096]{2,1,0:T(8,128)S(1)}, u32[]{:S(2)}) copy-start(f32[16,8,4096]{2,1,0:T(8,128)S(1)} %stencil.2.res_ref) | copy-start | bytes 6291460
  115.5 1.6 %copy-start.1 = (f32[16,8,4096]{2,1,0:T(8,128)S(1)}, f32[16,8,4096]{2,1,0:T(8,128)}, u32[]{:S(2)}) copy-start(f32[16,8,4096]{2,1,0:T(8,128)} %copy-done) | copy-start | bytes 6291460
  117.1 1.6 %copy-start.3 = (f32[16,8,4096]{2,1,0:T(8,128)S(1)}, f32[16,8,4096]{2,1,0:T(8,128)}, u32[]{:S(2)}) copy-start(f32[16,8,4096]{2,1,0:T(8,128)} %copy-done.2) | copy-start | bytes 6291460

commit v2 on v1

v2 whole, which is shorter than its diff:
```python
import functools

import jax
import jax.numpy as jnp
from jax import lax
from jax.experimental import pallas as pl
from jax.experimental.pallas import tpu as pltpu
from jax.sharding import PartitionSpec as P

HALF_ROOT = 0.7071067811865476
THIRD_NORM = 0.4082482904638631
FOURTH_NORM = 0.2041241452319315
FLOOR = 0.3
STEEP = 4.0
STIFF = 0.1
LOG2E = 1.4426950408889634
LN2 = 0.6931471805599453
MIB = 1 << 20
VMEM = 24 * MIB
F32 = jnp.float32
BF16 = jnp.bfloat16
HBM = pltpu.HBM


def basis(quad_nodes, degrees):
    points = quad_nodes[None, :, :]
    degree_grid = degrees[:, None, :]
    square = points * points
    third = (square * points - 3.0 * points) * THIRD_NORM
    fourth = (square * square - 6.0 * square + 3.0) * FOURTH_NORM
    second = (square - 1.0) * HALF_ROOT
    factor = jnp.where(
        degree_grid == 0,
        1.0,
        jnp.where(
            degree_grid == 1,
            points,
            jnp.where(degree_grid == 2, second, jnp.where(degree_grid == 3, third, fourth)),
        ),
    )
    return jnp.prod(factor, axis=2).astype(BF16)


def iotas(shape):
    return lax.broadcasted_iota(jnp.int32, shape, 0), lax.broadcasted_iota(jnp.int32, shape, 1)


def one_hot(hit):
    return jnp.where(hit, 1.0, 0.0).astype(BF16)


def pack_kernel(groups, disp_ref, dir_ref, send_ref, in_buf, out_buf, in_sem, out_sem):
    modes, rows, width = disp_ref.shape
    count, _, both, each = send_ref.shape
    size = both * rows
    per = count // groups
    span = per * each

    def loads(g):
        cols = pl.ds(g * span, span)
        return [
            pltpu.make_async_copy(ref.at[:, :, cols], in_buf.at[f, :, :, cols], in_sem.at[f, g])
            for f, ref in enumerate((disp_ref, dir_ref))
        ]

    def store(g):
        at = pl.ds(g * per, per)
        return pltpu.make_async_copy(out_buf.at[at], send_ref.at[at], out_sem.at[g])

    for g in range(groups):
        for copy in loads(g):
            copy.start()
    to, frm = iotas((size, size))
    perm = one_hot(frm == (to % both) * rows + to // both)
    for g in range(groups):
        for copy in loads(g):
            copy.wait()
        for d in range(g * per, (g + 1) * per):
            fields = in_buf[:, :, :, pl.ds(d * each, each)].reshape(size, each)
            moved = jnp.dot(perm, fields, preferred_element_type=F32).astype(BF16)
            out_buf[d] = moved.reshape(rows, both, each)
        store(g).start()
    for g in range(groups):
        store(g).wait()


def pack(displacement, direction, count, groups=8):
    modes, rows, width = displacement.shape
    each = width // count
    both = 2 * modes
    hbm = pl.BlockSpec(memory_space=HBM)
    shape = (count, rows, both, each)
    return pl.pallas_call(
        functools.partial(pack_kernel, groups),
        in_specs=[hbm, hbm],
        out_specs=hbm,
        out_shape=pltpu.HBM(shape, BF16),
        scratch_shapes=[
            pltpu.VMEM((2, modes, rows, width), BF16),
            pltpu.VMEM(shape, BF16),
            pltpu.SemaphoreType.DMA((2, groups)),
            pltpu.SemaphoreType.DMA((groups,)),
        ],
        compiler_params=pltpu.CompilerParams(vmem_limit_bytes=VMEM),
        cost_estimate=pl.CostEstimate(flops=2 * (2 * modes * rows) ** 2 * width, bytes_accessed=4 * MIB, transcendentals=0),
        name="pack",
    )(pltpu.with_memory_space_constraint(displacement, HBM), pltpu.with_memory_space_constraint(direction, HBM))


def quad_kernel(chunk, got_ref, table_t_ref, table_w_ref, shift_ref, out_ref, out_buf, w_ref, out_sem):
    count, rows, both, width = got_ref.shape
    modes = both // 2
    quad = table_t_ref.shape[0]
    total = count * modes

    def store(r):
        return pltpu.make_async_copy(out_buf.at[r], out_ref.at[:, r], out_sem.at[r])

    def one_row(r, _):
        disp = got_ref[:, r, :modes, :].reshape(total, width)
        dire = got_ref[:, r, modes:, :].reshape(total, width)
        for q in range(quad // chunk):
            at = pl.ds(q * chunk, chunk)
            left = table_t_ref[at, :]
            shift = shift_ref[at, :]
            shift = jnp.concatenate([shift] * (width // shift.shape[1]), axis=1)
            s = shift + jnp.dot(left, disp, preferred_element_type=F32)
            probe = jnp.dot(left, dire, preferred_element_type=F32)
            e = jnp.exp2(jnp.minimum(s, 80.0) * LOG2E)
            one = 1.0 + e
            big = jnp.maximum(s, jnp.log2(one) * LN2) + STEEP * FLOOR
            inv = pl.reciprocal(big, approx=True)
            sig = e * pl.reciprocal(one, approx=True)
            square = inv * inv
            w_ref[0, at, :] = square.astype(BF16)
            w_ref[1, at, :] = ((sig * inv) * (square * probe)).astype(BF16)
        table_w = table_w_ref[...]
        for f in range(2):
            force = jnp.dot(table_w, w_ref[f], preferred_element_type=F32).astype(BF16)
            out_buf[r, :, f * modes : (f + 1) * modes, :] = force.reshape(count, modes, width)
        store(r).start()
        return 0

    lax.fori_loop(0, rows, one_row, 0)
    for r in range(rows):
        store(r).wait()


def quad_forces(got, table_t, table_w, shift):
    count, rows, both, width = got.shape
    quad, total = table_t.shape
    hbm = pl.BlockSpec(memory_space=HBM)
    vmem = pl.BlockSpec(memory_space=pltpu.VMEM)
    return pl.pallas_call(
        functools.partial(quad_kernel, 128),
        in_specs=[vmem] * 4,
        out_specs=hbm,
        out_shape=pltpu.HBM(got.shape, BF16),
        scratch_shapes=[
            pltpu.VMEM((rows, count, both, width), BF16),
            pltpu.VMEM((2, quad, width), BF16),
            pltpu.SemaphoreType.DMA((rows,)),
        ],
        compiler_params=pltpu.CompilerParams(vmem_limit_bytes=VMEM),
        cost_estimate=pl.CostEstimate(flops=8589934592, bytes_accessed=4194304, transcendentals=0),
        name="quad_forces",
    )(got, table_t, table_w, shift)


def shifted(v, lane, by):
    width = v.shape[-1]
    inside = lane < width - 1 if by > 0 else lane > 0
    return jnp.where(inside, pltpu.roll(v, width - 1 if by > 0 else 1, 1), 0.0)


def stencil_kernel(chunk, x_ref, above_ref, below_ref, out_ref, inner_ref, side_ref):
    modes, rows, width = x_ref.shape
    size = modes * rows
    to, frm = iotas((size, size))
    gap = jnp.abs(to - frm)
    same = to // rows == frm // rows
    centre = jnp.where(gap == 0, 20.0, jnp.where(gap == 1, -8.0, jnp.where(gap == 2, 1.0, 0.0)))
    centre = jnp.where(same, centre, 0.0).astype(BF16)
    side = jnp.where(gap == 0, -8.0, jnp.where(gap == 1, 2.0, 0.0))
    side = jnp.where(same, side, 0.0).astype(BF16)
    edge = 2 * modes
    to, frm = iotas((size, 2 * edge))
    row = jnp.where(frm < edge, frm // modes, rows - 4 + frm // modes)
    place = one_hot((frm % modes == to // rows) & (row == to % rows))
    for c in range(width // chunk):
        cols = pl.ds(c * chunk, chunk)
        terms = jnp.concatenate([above_ref[:, :, cols].reshape(edge, chunk), below_ref[:, :, cols].reshape(edge, chunk)], axis=0)
        operand = x_ref[:, :, cols].reshape(size, chunk)
        inner = STIFF * jnp.dot(centre, operand, preferred_element_type=F32) + jnp.dot(place, terms, preferred_element_type=F32)
        inner_ref[:, :, cols] = inner.reshape(modes, rows, chunk)
        side_ref[:, :, cols] = jnp.dot(side, operand, preferred_element_type=F32).reshape(modes, rows, chunk)
    lane = lax.broadcasted_iota(jnp.int32, (rows, width), 1)

    def one_mode(m, _):
        x = x_ref[m].astype(F32)
        y = side_ref[m]
        right = shifted(y + shifted(x, lane, 1), lane, 1)
        left = shifted(y + shifted(x, lane, -1), lane, -1)
        out_ref[m] = (inner_ref[m] + STIFF * (right + left)).astype(BF16)
        return 0

    lax.fori_loop(0, modes, one_mode, 0)


def stencil(x, above, below, field):
    modes, rows, width = x.shape
    edge = pl.BlockSpec((2, modes, width), lambda i: (0, field, 0))
    whole = pl.BlockSpec(x.shape, lambda i: (0, 0, 0))
    return pl.pallas_call(
        functools.partial(stencil_kernel, 512),
        grid=(1,),
        in_specs=[whole, edge, edge],
        out_specs=whole,
        out_shape=pltpu.HBM(x.shape, BF16),
        scratch_shapes=[pltpu.VMEM(x.shape, F32)] * 2,
        compiler_params=pltpu.CompilerParams(vmem_limit_bytes=VMEM),
        cost_estimate=pl.CostEstimate(flops=8589934592, bytes_accessed=4 * MIB, transcendentals=0),
        name="stencil",
    )(pltpu.with_memory_space_constraint(x, HBM), above, below)


def edges_kernel(chunk, disp_ref, dir_ref, low_ref, high_ref):
    modes, rows, width = disp_ref.shape
    last = rows - 1
    to, frm = iotas((4 * modes, modes * rows))
    part, row = to // modes, frm % rows
    same = to % modes == frm // rows
    outer = jnp.where(part < 2, 0, last)
    inner = jnp.where(part < 2, 1, last - 1)
    full = (part == 1) | (part == 2)
    plain = jnp.where(
        full,
        jnp.where(row == outer, -8.0, jnp.where(row == inner, 1.0, 0.0)),
        jnp.where(row == outer, 1.0, 0.0),
    )
    plain = jnp.where(same, plain, 0.0).astype(BF16)
    to, frm = iotas((2 * modes, modes * rows))
    outer = jnp.where(to // modes == 0, 0, last)
    corner = jnp.where((to % modes == frm // rows) & (frm % rows == outer), 2.0, 0.0).astype(BF16)
    lane = lax.broadcasted_iota(jnp.int32, (2 * modes, width), 1)
    for field, ref in enumerate((disp_ref, dir_ref)):
        at = pl.ds(field * modes, modes)
        x = ref[...].reshape(modes * rows, width)
        terms = jnp.dot(plain, x, preferred_element_type=F32)
        corners = jnp.dot(corner, x, preferred_element_type=F32)
        corners = shifted(corners, lane, 1) + shifted(corners, lane, -1)
        low_ref[0, at, :] = (STIFF * terms[:modes]).astype(BF16)
        low_ref[1, at, :] = (STIFF * (terms[modes : 2 * modes] + corners[:modes])).astype(BF16)
        high_ref[0, at, :] = (STIFF * (terms[2 * modes : 3 * modes] + corners[modes:])).astype(BF16)
        high_ref[1, at, :] = (STIFF * terms[3 * modes :]).astype(BF16)


def edges(displacement, direction):
    modes, rows, width = displacement.shape
    whole = pl.BlockSpec(displacement.shape, lambda i: (0, 0, 0))
    edge = pl.BlockSpec((2, 2 * modes, width), lambda i: (0, 0, 0))
    return pl.pallas_call(
        functools.partial(edges_kernel, 512),
        grid=(1,),
        in_specs=[whole, whole],
        out_specs=[edge, edge],
        out_shape=[pltpu.HBM((2, 2 * modes, width), BF16)] * 2,
        compiler_params=pltpu.CompilerParams(vmem_limit_bytes=VMEM),
        cost_estimate=pl.CostEstimate(flops=1048576, bytes_accessed=1048576, transcendentals=0),
        name="edges",
    )(pltpu.with_memory_space_constraint(displacement, HBM), pltpu.with_memory_space_constraint(direction, HBM))


def merge_kernel(groups, force_ref, res_ref, tan_ref, res_out, tan_out, in_buf, buf, in_sem, out_sem):
    count, rows, both, each = force_ref.shape
    modes = both // 2
    size = both * rows
    per = count // groups
    span = per * each

    def loads(g):
        cols = pl.ds(g * span, span)
        return [
            pltpu.make_async_copy(ref.at[:, :, cols], in_buf.at[f, :, :, cols], in_sem.at[f, g])
            for f, ref in enumerate((res_ref, tan_ref))
        ]

    def stores(g):
        cols = pl.ds(g * span, span)
        return [
            pltpu.make_async_copy(buf.at[f, :, :, cols], ref.at[:, :, cols], out_sem.at[f, g])
            for f, ref in enumerate((res_out, tan_out))
        ]

    for g in range(groups):
        for copy in loads(g):
            copy.start()
    to, frm = iotas((size, size))
    hit = (to % rows == frm // both) & (to // rows == frm % both)
    moves = jnp.where(hit, jnp.where(to // rows < modes, -1.0, 2.0), 0.0).astype(BF16)
    for g in range(groups):
        for copy in loads(g):
            copy.wait()
        for d in range(g * per, (g + 1) * per):
            cols = pl.ds(d * each, each)
            moved = jnp.dot(moves, force_ref[d].reshape(size, each), preferred_element_type=F32)
            moved = moved.reshape(2, modes, rows, each)
            buf[:, :, :, cols] = in_buf[:, :, :, cols].astype(F32) + moved
        for copy in stores(g):
            copy.start()
    for g in range(groups):
        for copy in stores(g):
            copy.wait()


def merge(force, res, tan, groups=8):
    count, rows, both, each = force.shape
    vmem = pl.BlockSpec(memory_space=pltpu.VMEM)
    hbm = pl.BlockSpec(memory_space=HBM)
    return pl.pallas_call(
        functools.partial(merge_kernel, groups),
        in_specs=[vmem, hbm, hbm],
        out_specs=[hbm] * 2,
        out_shape=[pltpu.HBM(res.shape, F32)] * 2,
        scratch_shapes=[
            pltpu.VMEM((2,) + res.shape, BF16),
            pltpu.VMEM((2,) + res.shape, F32),
            pltpu.SemaphoreType.DMA((2, groups)),
            pltpu.SemaphoreType.DMA((2, groups)),
        ],
        compiler_params=pltpu.CompilerParams(vmem_limit_bytes=VMEM),
        cost_estimate=pl.CostEstimate(flops=2 * (both * rows) ** 2 * each * count, bytes_accessed=10 * MIB, transcendentals=0),
        name="merge",
    )(force, pltpu.with_memory_space_constraint(res, HBM), pltpu.with_memory_space_constraint(tan, HBM))


def shards(displacement, direction, quad_nodes, quad_weights, gap_nominal, pressure_load, degrees):
    count = lax.axis_size("mode")
    bands = lax.axis_size("space")
    send = pack(displacement, direction, count)
    table = basis(quad_nodes, degrees)
    scale = quad_weights * pressure_load * (STEEP * STEEP)
    table_w = (table.astype(F32) * scale[None, :]).astype(BF16)
    table_t = -STEEP * table.T
    shift = jnp.broadcast_to((STEEP * (gap_nominal - FLOOR))[:, None], (gap_nominal.shape[0], 128))
    first, second, send = lax.optimization_barrier((displacement, direction, send))
    got = lax.all_to_all(send, "mode", split_axis=0, concat_axis=0, tiled=True)
    low, high = edges(first, second)
    above = lax.ppermute(high, "space", [(i, i + 1) for i in range(bands - 1)])
    below = lax.ppermute(low, "space", [(i + 1, i) for i in range(bands - 1)])
    got, _, _ = lax.optimization_barrier((got, low, high))
    force = quad_forces(got, table_t, table_w, shift)
    back = lax.all_to_all(force, "mode", split_axis=0, concat_axis=0, tiled=True)
    res = stencil(displacement, above, below, 0)
    tan = stencil(direction, above, below, 1)
    return tuple(merge(back, res, tan))


def solution(mesh):
    in_specs = (P("mode", "space", None), P("mode", "space", None), P(), P(), P(), P(), P())
    out_specs = (P("mode", "space", None), P("mode", "space", None))
    return jax.shard_map(shards, mesh=mesh, in_specs=in_specs, out_specs=out_specs, check_vma=False)
```

time: 122 us -> 93.4 us (0.77)
  the two profiles are of different devices: /device:TPU:2 before, /device:TPU:1 now
where the time goes in v2:
time: 93.4 us; the launch traced here: 93.1 us
  waiting for transfers between devices  37.8 us (40%)
  Pallas kernels  30.8 us (33%)
  starting transfers between devices  20.3 us (22%)
  other arithmetic  2.32 us (2%)
  local copies, waits for them, and re-layouts  0.95 us (1%)
    all_to_all x1, waiting for transfers between devices, shards(): got = lax.all_to_all(send, 'mode', split_axis=0, concat_axis=0, tiled=True)  23.9 us
    all_to_all x1, waiting for transfers between devices, shards(): lax.all_to_all(force, 'mode', split_axis=0, concat_axis=0, tiled=True)  13.9 us
    pallas_call x2, Pallas kernels, stencil(): pl.pallas_call(functools.partial(stencil_kernel, 512), grid=(1,), in_spec...  13.3 us
    all_to_all x1, starting transfers between devices, shards(): got = lax.all_to_all(send, 'mode', split_axis=0, concat_axis=0, tiled=True)  7.86 us
    pallas_call x1, Pallas kernels, quad_forces(): pl.pallas_call(functools.partial(quad_kernel, 128), in_specs=[vmem] * 4,...  6.44 us
    ppermute x1, starting transfers between devices, shards(): above = lax.ppermute(high, 'space', [(i, i + 1) for i in range(bands - 1)])  6.31 us
    all_to_all x1, starting transfers between devices, shards(): lax.all_to_all(force, 'mode', split_axis=0, concat_axis=0, tiled=True)  4.86 us
    pallas_call x1, Pallas kernels, merge(): pl.pallas_call(functools.partial(merge_kernel, groups), in_specs=[vmem, h...  3.9 us
  transfers between devices with their start and end apart: 4, of which 2 were waited for; matrix products, arithmetic and copies ran while one was open for 3% of the time, Pallas kernels for 25%

profile of v2, /device:TPU:1, one launch (start us, length us, event | category | flops | bytes accessed | tf_op | source)
XLA Modules:
  0.0 93.1 jit_solution(13591483456799396955)
XLA Ops:
  0.6 3.8 %pack.1 = bf16[16,8,32,256]{3,2,1,0:T(8,128)(2,1)} custom-call(bf16[16,8,4096]{2,1,0:T(8,128)(2,1)} %x_ref.2, bf16[16,8,4096]{2,1,0:T(8,128)(2,1)} %x_ref.3), custom_call_target="tpu_custom_call" | custom-call | flops 536870912 | bytes 4194304 | tf_op jit(solution)/shard_map/pack/pallas_call | solution.py:93
  4.4 7.9 %all-to-all-start = ((bf16[16,8,32,256]{3,2,1,0:T(8,128)(2,1)}), bf16[16,8,32,256]{3,2,1,0:T(8,128)(2,1)S(1)}, u32[]{:S(2)}, u32[]{:S(2)}) async-start(bf16[16,8,32,256]{3,2,1,0:T(8,128)(2,1)} %pack.1), calls=%async_computation | async-start | bytes 4194304 | tf_op jit(solution)/shard_map/all_to_all | solution.py:347
  12.3 0.0 copy-start.1
  12.3 0.0 copy-start
  12.3 0.0 copy-start.4
  12.3 0.0 copy-start.2
  12.3 0.0 copy-start.3
  12.3 3.5 %edges.1 = (bf16[2,32,4096]{2,1,0:T(8,128)(2,1)}, bf16[2,32,4096]{2,1,0:T(8,128)(2,1)}) custom-call(bf16[16,8,4096]{2,1,0:T(8,128)(2,1)} %x_ref.2, bf16[16,8,4096]{2,1,0:T(8,128)(2,1)} %x_ref.3), custom_call_target="tpu_custom_call" | custom-call | flops 1048576 | bytes 1048576 | tf_op jit(solution)/shard_map/edges/pallas_call | solution.py:262
  15.8 1.3 %collective-permute-start.1 = (bf16[2,32,4096]{2,1,0:T(8,128)(2,1)}, bf16[2,32,4096]{2,1,0:T(8,128)(2,1)S(1)}, u32[]{:S(2)}, u32[]{:S(2)}) collective-permute-start(bf16[2,32,4096]{2,1,0:T(8,128)(2,1)} %get-tuple-element.11), channel_id=1, source_target_pairs={{16,0},{32,16},{48,32},{64,48},{80,64},{96,80},{112,96},{17,1},{33... | collective-permute-start | bytes 1572872 | tf_op jit(solution)/shard_map/ppermute | solution.py:350
  17.1 6.3 %collective-permute-start = (bf16[2,32,4096]{2,1,0:T(8,128)(2,1)}, bf16[2,32,4096]{2,1,0:T(8,128)(2,1)}, u32[]{:S(2)}, u32[]{:S(2)}) collective-permute-start(bf16[2,32,4096]{2,1,0:T(8,128)(2,1)} %get-tuple-element.12), channel_id=1, source_target_pairs={{0,16},{16,32},{32,48},{48,64},{64,80},{80,96},{96,112},{1,17},{17... | collective-permute-start | bytes 1572872 | tf_op jit(solution)/shard_map/ppermute | solution.py:349
  23.4 0.0 copy-done.1
  23.4 0.2 copy.18
  23.6 0.2 copy.19
  23.7 0.2 copy.21
  23.9 0.2 copy.20
  24.1 0.0 copy-done
  24.1 2.2 %select_reduce_fusion = bf16[256,512]{1,0:T(8,128)(2,1)S(1)} fusion(f32[512,8]{0,1:T(8,128)S(1)} %get-tuple-element.15, f32[512,8]{0,1:T(8,128)S(1)} %get-tuple-element.16, f32[512,8]{0,1:T(8,128)S(1)} %get-tuple-element.14, f32[512,8]{0,1:T(8,128)S(1)} %copy-done, pred[256,8]{1,0:T(8,128)(4,1)S(1)} %copy.21, pred[256,8]{1,0:T(8,128)(4,1)S(1)} %copy.20, ...), kind=kLoop, calls=%fused_computation | loop fusion | flops 5111808 | bytes 335872 | tf_op jit(solution)/shard_map/reduce_prod | solution.py:41
  26.4 0.1 copy.22.table_t_ref
  26.5 0.0 copy-done.4
  26.5 0.0 copy-done.2
  26.5 0.0 copy-done.3
  26.6 23.9 %all-to-all-done.got_ref = bf16[16,8,32,256]{3,2,1,0:T(8,128)(2,1)S(1)} async-done(((bf16[16,8,32,256]{3,2,1,0:T(8,128)(2,1)}), bf16[16,8,32,256]{3,2,1,0:T(8,128)(2,1)S(1)}, u32[]{:S(2)}, u32[]{:S(2)}) %all-to-all-start) | async-done | bytes 2097184 | tf_op jit(solution)/shard_map/all_to_all | solution.py:347
  50.5 0.1 broadcast_in_dim.80.shift_ref
  50.7 6.4 %quad_forces.1 = bf16[16,8,32,256]{3,2,1,0:T(8,128)(2,1)} custom-call(bf16[16,8,32,256]{3,2,1,0:T(8,128)(2,1)S(1)} %all-to-all-done.got_ref, bf16[512,256]{1,0:T(8,128)(2,1)S(1)} %copy.22.table_t_ref, bf16[256,512]{1,0:T(8,128)(2,1)S(1)} %multiply_convert_fusion.table_w_ref, f32[512,128]{1,0:T(8,128)S(1)} %broadcast_in_dim.80.shift_ref), custom_call_target="tpu_custom_call" | custom-call | flops 8589934592 | bytes 4194304 | tf_op jit(solution)/shard_map/quad_forces/pallas_call | solution.py:154
  57.1 4.9 %all-to-all-start.1 = ((bf16[16,8,32,256]{3,2,1,0:T(8,128)(2,1)}), bf16[16,8,32,256]{3,2,1,0:T(8,128)(2,1)S(1)}, u32[]{:S(2)}, u32[]{:S(2)}) async-start(bf16[16,8,32,256]{3,2,1,0:T(8,128)(2,1)} %quad_forces.1), calls=%async_computation.1 | async-start | bytes 4194304 | tf_op jit(solution)/shard_map/all_to_all | solution.py:353
  62.0 0.0 collective-permute-done.1.below_ref
  62.0 0.0 collective-permute-done.above_ref
  62.0 6.7 %stencil.3.tan_ref = bf16[16,8,4096]{2,1,0:T(8,128)(2,1)} custom-call(bf16[16,8,4096]{2,1,0:T(8,128)(2,1)} %x_ref.3, bf16[2,32,4096]{2,1,0:T(8,128)(2,1)} %collective-permute-done.above_ref, bf16[2,32,4096]{2,1,0:T(8,128)(2,1)S(1)} %collective-permute-done.1.below_ref), custom_call_target="tpu_custom_call" | custom-call | flops 8589934592 | bytes 4194304 | tf_op jit(solution)/shard_map/stencil/pallas_call | solution.py:214
  68.6 6.6 %stencil.2.res_ref = bf16[16,8,4096]{2,1,0:T(8,128)(2,1)} custom-call(bf16[16,8,4096]{2,1,0:T(8,128)(2,1)} %x_ref.2, bf16[2,32,4096]{2,1,0:T(8,128)(2,1)} %collective-permute-done.above_ref, bf16[2,32,4096]{2,1,0:T(8,128)(2,1)S(1)} %collective-permute-done.1.below_ref), custom_call_target="tpu_custom_call" | custom-call | flops 8589934592 | bytes 4194304 | tf_op jit(solution)/shard_map/stencil/pallas_call | solution.py:214
  75.3 13.9 %all-to-all-done.1.force_ref = bf16[16,8,32,256]{3,2,1,0:T(8,128)(2,1)S(1)} async-done(((bf16[16,8,32,256]{3,2,1,0:T(8,128)(2,1)}), bf16[16,8,32,256]{3,2,1,0:T(8,128)(2,1)S(1)}, u32[]{:S(2)}, u32[]{:S(2)}) %all-to-all-start.1) | async-done | bytes 2097184 | tf_op jit(solution)/shard_map/all_to_all | solution.py:353
  89.2 3.9 %merge.1 = (f32[16,8,4096]{2,1,0:T(8,128)}, f32[16,8,4096]{2,1,0:T(8,128)}) custom-call(bf16[16,8,32,256]{3,2,1,0:T(8,128)(2,1)S(1)} %all-to-all-done.1.force_ref, bf16[16,8,4096]{2,1,0:T(8,128)(2,1)} %stencil.2.res_ref, bf16[16,8,4096]{2,1,0:T(8,128)(2,1)} %stencil.3.tan_ref), custom_call_target="tpu_custom_call" | custom-call | flops 536870912 | bytes 10485760 | tf_op jit(solution)/shard_map/merge/pallas_call | solution.py:320
  (6 shorter events, 0.1 us)
Async XLA Ops:
  4.4 46.1 %all-to-all-start = ((bf16[16,8,32,256]{3,2,1,0:T(8,128)(2,1)}), bf16[16,8,32,256]{3,2,1,0:T(8,128)(2,1)S(1)}, u32[]{:S(2)}, u32[]{:S(2)}) async-start(bf16[16,8,32,256]{3,2,1,0:T(8,128)(2,1)} %pack.1), calls=%async_computation | async-start | bytes 4194304 | tf_op jit(solution)/shard_map/all_to_all | solution.py:347
  12.3 11.1 %copy-start.1 = (s32[256,8]{0,1:T(8,128)S(1)}, s32[256,8]{0,1:T(8,128)}, u32[]{:S(2)}) copy-start(s32[256,8]{0,1:T(8,128)} %param.13) | copy-start | bytes 24580
  12.3 11.8 %copy-start = (f32[512,8]{0,1:T(8,128)S(1)}, f32[512,8]{0,1:T(8,128)}, u32[]{:S(2)}) copy-start(f32[512,8]{0,1:T(8,128)} %param.9) | copy-start | bytes 49156
  12.3 14.2 %copy-start.4 = (f32[512]{0:T(512)S(1)}, f32[512]{0:T(512)}, u32[]{:S(2)}) copy-start(f32[512]{0:T(512)} %param.11) | copy-start | bytes 6148
  12.3 14.2 %copy-start.2 = (f32[512]{0:T(512)S(1)}, f32[512]{0:T(512)}, u32[]{:S(2)}) copy-start(f32[512]{0:T(512)} %param.10) | copy-start | bytes 6148
  12.3 14.2 %copy-start.3 = (f32[512]{0:T(512)S(1)}, f32[512]{0:T(512)}, u32[]{:S(2)}) copy-start(f32[512]{0:T(512)} %param.12) | copy-start | bytes 6148
  15.8 46.2 %collective-permute-start.1 = (bf16[2,32,4096]{2,1,0:T(8,128)(2,1)}, bf16[2,32,4096]{2,1,0:T(8,128)(2,1)S(1)}, u32[]{:S(2)}, u32[]{:S(2)}) collective-permute-start(bf16[2,32,4096]{2,1,0:T(8,128)(2,1)} %get-tuple-element.11), channel_id=1, source_target_pairs={{16,0},{32,16},{48,32},{64,48},{80,64},{96,80},{112,96},{17,1},{33... | collective-permute-start | bytes 1572872 | tf_op jit(solution)/shard_map/ppermute | solution.py:350
  17.1 44.9 %collective-permute-start = (bf16[2,32,4096]{2,1,0:T(8,128)(2,1)}, bf16[2,32,4096]{2,1,0:T(8,128)(2,1)}, u32[]{:S(2)}, u32[]{:S(2)}) collective-permute-start(bf16[2,32,4096]{2,1,0:T(8,128)(2,1)} %get-tuple-element.12), channel_id=1, source_target_pairs={{0,16},{16,32},{32,48},{48,64},{64,80},{80,96},{96,112},{1,17},{17... | collective-permute-start | bytes 1572872 | tf_op jit(solution)/shard_map/ppermute | solution.py:349
  57.1 32.1 %all-to-all-start.1 = ((bf16[16,8,32,256]{3,2,1,0:T(8,128)(2,1)}), bf16[16,8,32,256]{3,2,1,0:T(8,128)(2,1)S(1)}, u32[]{:S(2)}, u32[]{:S(2)}) async-start(bf16[16,8,32,256]{3,2,1,0:T(8,128)(2,1)} %quad_forces.1), calls=%async_computation.1 | async-start | bytes 4194304 | tf_op jit(solution)/shard_map/all_to_all | solution.py:353

commit v3 on v2

v3 whole, which is shorter than its diff:
```python
import functools

import jax
import jax.numpy as jnp
from jax import lax
from jax.experimental import pallas as pl
from jax.experimental.pallas import tpu as pltpu
from jax.sharding import PartitionSpec as P

HALF_ROOT = 0.7071067811865476
THIRD_NORM = 0.4082482904638631
FOURTH_NORM = 0.2041241452319315
FLOOR = 0.3
STEEP = 4.0
STIFF = 0.1
LOG2E = 1.4426950408889634
LN2 = 0.6931471805599453
MIB = 1 << 20
VMEM = 24 * MIB
F32 = jnp.float32
BF16 = jnp.bfloat16
HBM = pltpu.HBM


def basis(quad_nodes, degrees):
    points = quad_nodes[None, :, :]
    degree_grid = degrees[:, None, :]
    square = points * points
    third = (square * points - 3.0 * points) * THIRD_NORM
    fourth = (square * square - 6.0 * square + 3.0) * FOURTH_NORM
    second = (square - 1.0) * HALF_ROOT
    factor = jnp.where(
        degree_grid == 0,
        1.0,
        jnp.where(
            degree_grid == 1,
            points,
            jnp.where(degree_grid == 2, second, jnp.where(degree_grid == 3, third, fourth)),
        ),
    )
    return jnp.prod(factor, axis=2).astype(BF16)


def iotas(shape):
    return lax.broadcasted_iota(jnp.int32, shape, 0), lax.broadcasted_iota(jnp.int32, shape, 1)


def one_hot(hit):
    return jnp.where(hit, 1.0, 0.0).astype(BF16)


def in_hbm(x):
    return pltpu.with_memory_space_constraint(x, HBM)


def shifted(v, lane, by):
    width = v.shape[-1]
    inside = lane < width - 1 if by > 0 else lane > 0
    return jnp.where(inside, pltpu.roll(v, width - 1 if by > 0 else 1, 1), 0.0)


def pack_kernel(groups, step, disp_ref, dir_ref, send_ref, in_buf, out_buf, in_sem, out_sem):
    modes, rows, width = disp_ref.shape
    count, _, both, each = send_ref.shape
    size = both * rows
    per = count // groups
    span = per * each

    def loads(g):
        cols = pl.ds(g * span, span)
        return [
            pltpu.make_async_copy(ref.at[:, :, cols], in_buf.at[f, :, :, cols], in_sem.at[f, g])
            for f, ref in enumerate((disp_ref, dir_ref))
        ]

    def store(g):
        at = pl.ds(g * per, per)
        return pltpu.make_async_copy(out_buf.at[at], send_ref.at[at], out_sem.at[g])

    for g in range(groups):
        for copy in loads(g):
            copy.start()
    to, frm = iotas((size, size))
    perm = one_hot(frm == (to % both) * rows + to // both)
    for g in range(groups):
        for copy in loads(g):
            copy.wait()
        for d in range(g * per, (g + 1) * per, step):
            fields = in_buf[:, :, :, pl.ds(d * each, step * each)].reshape(size, step * each)
            moved = jnp.dot(perm, fields, preferred_element_type=F32).astype(BF16)
            for k in range(step):
                out_buf[d + k] = moved[:, k * each : (k + 1) * each].reshape(rows, both, each)
        store(g).start()
    for g in range(groups):
        store(g).wait()


def pack(displacement, direction, count, groups=8, step=2):
    modes, rows, width = displacement.shape
    each = width // count
    both = 2 * modes
    hbm = pl.BlockSpec(memory_space=HBM)
    shape = (count, rows, both, each)
    return pl.pallas_call(
        functools.partial(pack_kernel, groups, step),
        in_specs=[hbm, hbm],
        out_specs=hbm,
        out_shape=pltpu.HBM(shape, BF16),
        scratch_shapes=[
            pltpu.VMEM((2, modes, rows, width), BF16),
            pltpu.VMEM(shape, BF16),
            pltpu.SemaphoreType.DMA((2, groups)),
            pltpu.SemaphoreType.DMA((groups,)),
        ],
        compiler_params=pltpu.CompilerParams(vmem_limit_bytes=VMEM),
        cost_estimate=pl.CostEstimate(flops=2 * (2 * modes * rows) ** 2 * width, bytes_accessed=4 * MIB, transcendentals=0),
        name="pack",
    )(in_hbm(displacement), in_hbm(direction))


def quad_kernel(chunk, deep, got_ref, table_t_ref, table_w_ref, shift_ref, out_ref, out_buf, w_ref, cross_ref, out_sem):
    count, rows, both, each = got_ref.shape
    per = count // 2
    modes = both // 2
    quad = table_t_ref.shape[0]
    total = per * modes
    pairs = rows // deep
    steps = 2 * pairs

    def store(i):
        at = pl.ds(i // pairs * per, per)
        lines = pl.ds(i % pairs * deep, deep)
        return pltpu.make_async_copy(out_buf.at[at, lines], out_ref.at[at, lines], out_sem.at[i])

    def field_rows(i, f):
        at = pl.ds(i // pairs * per, per)
        lines = [
            got_ref[at, i % pairs * deep + k, f * modes : (f + 1) * modes, :].reshape(total, each) for k in range(deep)
        ]
        return jnp.concatenate(lines, axis=1)

    frm, to = iotas((deep * each, deep * each))
    far = frm % each - to % each
    for band in range(2):
        near = frm // each == band
        full = to // each == 1 - band
        value = jnp.where(far == 0, jnp.where(near, jnp.where(full, -8.0, 1.0), jnp.where(full, 1.0, 0.0)), 0.0)
        cross_ref[band] = jnp.where((jnp.abs(far) == 1) & near & full, 2.0, value).astype(BF16)

    def one_step(i, _):
        disp = field_rows(i, 0)
        dire = field_rows(i, 1)
        for q in range(quad // chunk):
            at = pl.ds(q * chunk, chunk)
            left = table_t_ref[at, :]
            shift = shift_ref[at, :]
            shift = jnp.concatenate([shift] * (deep * each // shift.shape[1]), axis=1)
            s = shift + jnp.dot(left, disp, preferred_element_type=F32)
            probe = jnp.dot(left, dire, preferred_element_type=F32)
            e = jnp.exp2(jnp.minimum(s, 80.0) * LOG2E)
            one = 1.0 + e
            big = jnp.maximum(s, jnp.log2(one) * LN2) + STEEP * FLOOR
            inv = pl.reciprocal(big, approx=True)
            sig = e * pl.reciprocal(one, approx=True)
            square = inv * inv
            w_ref[0, at, :] = square.astype(BF16)
            w_ref[1, at, :] = ((sig * inv) * (square * probe)).astype(BF16)
        table_w = table_w_ref[...]
        weight = jnp.where((i == pairs - 1) | (i == pairs), STIFF, 0.0)
        for f, factor in enumerate((-1.0, 0.5)):
            cross = jnp.dot(field_rows(steps - 1 - i, f), cross_ref[i // pairs], preferred_element_type=F32)
            force = jnp.dot(table_w, w_ref[f], preferred_element_type=F32)
            force = (force + (factor * weight) * cross).astype(BF16)
            for k in range(deep):
                part = force[:, k * each : (k + 1) * each].reshape(per, modes, each)
                out_buf[pl.ds(i // pairs * per, per), i % pairs * deep + k, f * modes : (f + 1) * modes, :] = part
        store(i).start()
        return 0

    lax.fori_loop(0, steps, one_step, 0)
    for i in range(steps):
        store(i).wait()


def quad_forces(got, table_t, table_w, shift, deep=2):
    count, rows, both, each = got.shape
    quad, total = table_t.shape
    vmem = pl.BlockSpec(memory_space=pltpu.VMEM)
    return pl.pallas_call(
        functools.partial(quad_kernel, 128, deep),
        in_specs=[vmem] * 4,
        out_specs=pl.BlockSpec(memory_space=HBM),
        out_shape=pltpu.HBM(got.shape, BF16),
        scratch_shapes=[
            pltpu.VMEM(got.shape, BF16),
            pltpu.VMEM((2, quad, deep * each), BF16),
            pltpu.VMEM((2, deep * each, deep * each), BF16),
            pltpu.SemaphoreType.DMA((2 * rows // deep,)),
        ],
        compiler_params=pltpu.CompilerParams(vmem_limit_bytes=VMEM),
        cost_estimate=pl.CostEstimate(flops=1 << 10, bytes_accessed=1 << 10, transcendentals=0),
        name="quad_forces",
    )(got, table_t, table_w, shift)


def stencil_kernel(chunk, block, odd_ref, x_ref, outer_ref, ends_ref, out_ref, inner_ref, side_ref):
    modes, rows, width = x_ref.shape
    size = modes * rows
    blocks = width // block
    odd = odd_ref[0]
    to, frm = iotas((size, size + modes))
    gap = jnp.abs(to - frm)
    same = to // rows == frm // rows
    centre = jnp.where(gap == 0, 20.0, jnp.where(gap == 1, -8.0, jnp.where(gap == 2, 1.0, 0.0)))
    corner = (frm - size == to // rows) & (to % rows == (rows - 1) * (1 - odd))
    centre = jnp.where(frm < size, jnp.where(same, centre, 0.0), jnp.where(corner, 2.0, 0.0)).astype(BF16)
    to, frm = iotas((size, size))
    gap = jnp.abs(to - frm)
    side = jnp.where(gap == 0, -8.0, jnp.where(gap == 1, 2.0, 0.0))
    side = jnp.where(to // rows == frm // rows, side, 0.0).astype(BF16)
    to, frm = iotas((size, 2 * modes))
    place = one_hot((frm % modes == to // rows) & (to % rows == frm // modes + (rows - 2) * odd))
    item, col = iotas((ends_ref.shape[1], chunk))
    target = jnp.where(item < blocks, item * block - 1, (item - blocks + 1) * block)
    target = jnp.where(item < 2 * blocks, target, -1)
    for c in range(width // chunk):
        cols = pl.ds(c * chunk, chunk)
        x = x_ref[:, :, cols].reshape(size, chunk)
        spread = jnp.dot(ends_ref[...], one_hot(target == col + c * chunk), preferred_element_type=F32).astype(BF16)
        inner = jnp.dot(centre, jnp.concatenate([x, spread], axis=0), preferred_element_type=F32)
        terms = jnp.dot(place, outer_ref[:, :, cols].reshape(2 * modes, chunk), preferred_element_type=F32)
        inner_ref[:, :, cols] = (STIFF * inner + terms).reshape(modes, rows, chunk)
        side_ref[:, :, cols] = jnp.dot(side, x, preferred_element_type=F32).reshape(modes, rows, chunk)
    lane = lax.broadcasted_iota(jnp.int32, (rows, width), 1)

    def one_mode(m, _):
        x = x_ref[m].astype(F32)
        y = side_ref[m]
        right = shifted(y + shifted(x, lane, 1), lane, 1)
        left = shifted(y + shifted(x, lane, -1), lane, -1)
        out_ref[m] = (inner_ref[m] + STIFF * (right + left)).astype(BF16)
        return 0

    lax.fori_loop(0, modes, one_mode, 0)


def stencil(odd, x, outer, ends, field, count):
    modes, rows, width = x.shape
    whole = pl.BlockSpec((modes, rows, width), lambda i: (0, 0, 0))
    return pl.pallas_call(
        functools.partial(stencil_kernel, 512, width // count),
        grid=(1,),
        in_specs=[
            pl.BlockSpec(memory_space=pltpu.SMEM),
            whole,
            pl.BlockSpec((2, modes, width), lambda i: (0, field, 0)),
            pl.BlockSpec((modes, ends.shape[1]), lambda i: (field, 0)),
        ],
        out_specs=whole,
        out_shape=pltpu.HBM(x.shape, BF16),
        scratch_shapes=[pltpu.VMEM(x.shape, F32)] * 2,
        compiler_params=pltpu.CompilerParams(vmem_limit_bytes=VMEM),
        cost_estimate=pl.CostEstimate(flops=1 << 33, bytes_accessed=4 * MIB, transcendentals=0),
        name="stencil",
    )(odd, in_hbm(x), outer, ends)


def edges_kernel(block, odd_ref, disp_ref, dir_ref, terms_ref, ends_ref):
    modes, rows, width = disp_ref.shape
    size = modes * rows
    blocks = width // block
    odd = odd_ref[0]
    outer = (rows - 1) * odd
    inner = jnp.where(odd == 1, rows - 2, 1)
    to, frm = iotas((2 * modes, size))
    same = to % modes == frm // rows
    row = frm % rows
    full = to // modes == 1 - odd
    plain = jnp.where(row == outer, jnp.where(full, -8.0, 1.0), jnp.where(full & (row == inner), 1.0, 0.0))
    plain = jnp.where(same, plain, 0.0).astype(BF16)
    to, frm = iotas((modes, size))
    same = to == frm // rows
    corner = jnp.where(same & (frm % rows == outer), 2.0, 0.0).astype(BF16)
    facing = one_hot(same & (frm % rows == rows - 1 - outer))
    lane = lax.broadcasted_iota(jnp.int32, (modes, width), 1)
    col, item = iotas((width, ends_ref.shape[1]))
    source = jnp.where(item < blocks, item * block, (item - blocks) * block + block - 1)
    pick = one_hot((col == source) & (item < 2 * blocks))
    first = jnp.where(odd == 1, 1.0, 0.0)
    for f, ref in enumerate((disp_ref, dir_ref)):
        at = pl.ds(f * modes, modes)
        x = ref[...].reshape(size, width)
        terms = jnp.dot(plain, x, preferred_element_type=F32)
        corners = jnp.dot(corner, x, preferred_element_type=F32)
        corners = shifted(corners, lane, 1) + shifted(corners, lane, -1)
        terms_ref[0, at, :] = (STIFF * (terms[:modes] + first * corners)).astype(BF16)
        terms_ref[1, at, :] = (STIFF * (terms[modes:] + (1.0 - first) * corners)).astype(BF16)
        line = jnp.dot(facing, x, preferred_element_type=F32).astype(BF16)
        ends_ref[at, :] = jnp.dot(line, pick, preferred_element_type=F32).astype(BF16)


def edges(odd, displacement, direction, count):
    modes, rows, width = displacement.shape
    lanes = max(128, 2 * count)
    whole = pl.BlockSpec(displacement.shape, lambda i: (0, 0, 0))
    return pl.pallas_call(
        functools.partial(edges_kernel, width // count),
        grid=(1,),
        in_specs=[pl.BlockSpec(memory_space=pltpu.SMEM), whole, whole],
        out_specs=[
            pl.BlockSpec((2, 2 * modes, width), lambda i: (0, 0, 0)),
            pl.BlockSpec((2 * modes, lanes), lambda i: (0, 0)),
        ],
        out_shape=[pltpu.HBM((2, 2 * modes, width), BF16), pltpu.HBM((2 * modes, lanes), BF16)],
        compiler_params=pltpu.CompilerParams(vmem_limit_bytes=VMEM),
        cost_estimate=pl.CostEstimate(flops=1 << 20, bytes_accessed=1 << 20, transcendentals=0),
        name="edges",
    )(odd, in_hbm(displacement), in_hbm(direction))


def merge_kernel(groups, step, force_ref, res_ref, tan_ref, res_out, tan_out, in_buf, buf, in_sem, out_sem):
    count, rows, both, each = force_ref.shape
    modes = both // 2
    size = both * rows
    per = count // groups
    span = per * each

    def loads(g):
        cols = pl.ds(g * span, span)
        return [
            pltpu.make_async_copy(ref.at[:, :, cols], in_buf.at[f, :, :, cols], in_sem.at[f, g])
            for f, ref in enumerate((res_ref, tan_ref))
        ]

    def stores(g):
        cols = pl.ds(g * span, span)
        return [
            pltpu.make_async_copy(buf.at[f, :, :, cols], ref.at[:, :, cols], out_sem.at[f, g])
            for f, ref in enumerate((res_out, tan_out))
        ]

    for g in range(groups):
        for copy in loads(g):
            copy.start()
    to, frm = iotas((size, size))
    hit = (to % rows == frm // both) & (to // rows == frm % both)
    moves = jnp.where(hit, jnp.where(to // rows < modes, -1.0, 2.0), 0.0).astype(BF16)
    for g in range(groups):
        for copy in loads(g):
            copy.wait()
        for d in range(g * per, (g + 1) * per, step):
            cols = pl.ds(d * each, step * each)
            force = jnp.concatenate([force_ref[d + k].reshape(size, each) for k in range(step)], axis=1)
            moved = jnp.dot(moves, force, preferred_element_type=F32).reshape(2, modes, rows, step * each)
            buf[:, :, :, cols] = in_buf[:, :, :, cols].astype(F32) + moved
        for copy in stores(g):
            copy.start()
    for g in range(groups):
        for copy in stores(g):
            copy.wait()


def merge(force, res, tan, groups=8, step=2):
    count, rows, both, each = force.shape
    vmem = pl.BlockSpec(memory_space=pltpu.VMEM)
    hbm = pl.BlockSpec(memory_space=HBM)
    return pl.pallas_call(
        functools.partial(merge_kernel, groups, step),
        in_specs=[vmem, hbm, hbm],
        out_specs=[hbm] * 2,
        out_shape=[pltpu.HBM(res.shape, F32)] * 2,
        scratch_shapes=[
            pltpu.VMEM((2,) + res.shape, BF16),
            pltpu.VMEM((2,) + res.shape, F32),
            pltpu.SemaphoreType.DMA((2, groups)),
            pltpu.SemaphoreType.DMA((2, groups)),
        ],
        compiler_params=pltpu.CompilerParams(vmem_limit_bytes=VMEM),
        cost_estimate=pl.CostEstimate(flops=2 * (both * rows) ** 2 * each * count, bytes_accessed=10 * MIB, transcendentals=0),
        name="merge",
    )(force, in_hbm(res), in_hbm(tan))


def shards(displacement, direction, quad_nodes, quad_weights, gap_nominal, pressure_load, degrees):
    bands = lax.axis_size("space")
    count = 2 * lax.axis_size("mode")
    odd = (lax.axis_index("space") % 2).astype(jnp.int32).reshape(1)
    pairs = [[p * count + i for i in range(count)] for p in range(bands // 2)]

    def exchange(x):
        return lax.all_to_all(x, ("space", "mode"), split_axis=0, concat_axis=0, axis_index_groups=pairs, tiled=True)

    send = pack(displacement, direction, count)
    first, second, send = lax.optimization_barrier((displacement, direction, send))
    got = exchange(send)
    terms, ends = edges(odd, first, second, count)
    ends = lax.ppermute(ends, "space", [(i, i ^ 1) for i in range(bands)])
    terms, ends, got = lax.optimization_barrier((terms, ends, got))
    outer = lax.ppermute(terms, "space", [(i + a, i + b) for i in range(1, bands - 1, 2) for a, b in ((0, 1), (1, 0))])
    table = basis(quad_nodes, degrees)
    scale = quad_weights * pressure_load * (STEEP * STEEP)
    table_w = (table.astype(F32) * scale[None, :]).astype(BF16)
    table_t = -STEEP * table.T
    shift = jnp.broadcast_to((STEEP * (gap_nominal - FLOOR))[:, None], (gap_nominal.shape[0], 128))
    force = quad_forces(got, table_t, table_w, shift)
    back = exchange(force)
    res = stencil(odd, displacement, outer, ends, 0, count)
    tan = stencil(odd, direction, outer, ends, 1, count)
    return tuple(merge(back, res, tan))


def solution(mesh):
    in_specs = (P("mode", "space", None), P("mode", "space", None), P(), P(), P(), P(), P())
    out_specs = (P("mode", "space", None), P("mode", "space", None))
    return jax.shard_map(shards, mesh=mesh, in_specs=in_specs, out_specs=out_specs, check_vma=False)
```

time: 93.4 us -> 91.4 us (0.979)
  waiting for transfers between devices: 37.8 us -> 31.3 us
  Pallas kernels: 30.8 us -> 33.2 us
  starting transfers between devices: 20.3 us -> 22.3 us
    all_to_all x2, waiting for transfers between devices: 37.8 us -> 14.6 us  [exchange(): lax.all_to_all(x, ('space', 'mode'), split_axis=0, concat_axis=0, axis_in...]
    ppermute x2, waiting for transfers between devices: 0.01 us -> 16.7 us  [the longest x1 16.7 us: shards(): ends = lax.ppermute(ends, 'space', [(i, i ^ 1) for i in range(bands)])]
    all_to_all x2, starting transfers between devices: 12.7 us -> 18.7 us  [exchange(): lax.all_to_all(x, ('space', 'mode'), split_axis=0, concat_axis=0, axis_in...]
    ppermute x2, starting transfers between devices: 7.59 us -> 3.58 us  [the longest x1 2.9 us: shards(): ends = lax.ppermute(ends, 'space', [(i, i ^ 1) for i in range(bands)])]
    pallas_call x6, Pallas kernels: 30.8 us -> 33.2 us  [the longest x2 15.3 us: stencil(): pl.pallas_call(functools.partial(stencil_kernel, 512, width // count), gr...]
  transfers between devices with their start and end apart: 4 -> 4, of which waited for: 2 -> 3; matrix products, arithmetic and copies ran while one was open for 3% -> 4% of each run, Pallas kernels for 25% -> 28%
where the time goes in v3:
time: 91.4 us; the launch traced here: 90.9 us
  Pallas kernels  33.2 us (36%)
  waiting for transfers between devices  31.3 us (34%)
  starting transfers between devices  22.3 us (24%)
  other arithmetic  2.32 us (3%)
  local copies, waits for them, and re-layouts  0.96 us (1%)
    all_to_all x2, starting transfers between devices, exchange(): lax.all_to_all(x, ('space', 'mode'), split_axis=0, concat_axis=0, axis_in...  18.7 us
    ppermute x1, waiting for transfers between devices, shards(): ends = lax.ppermute(ends, 'space', [(i, i ^ 1) for i in range(bands)])  16.7 us
    pallas_call x2, Pallas kernels, stencil(): pl.pallas_call(functools.partial(stencil_kernel, 512, width // count), gr...  15.3 us
    all_to_all x2, waiting for transfers between devices, exchange(): lax.all_to_all(x, ('space', 'mode'), split_axis=0, concat_axis=0, axis_in...  14.6 us
    pallas_call x1, Pallas kernels, quad_forces(): pl.pallas_call(functools.partial(quad_kernel, 128, deep), in_specs=[vmem]...  6.61 us
    pallas_call x1, Pallas kernels, merge(): pl.pallas_call(functools.partial(merge_kernel, groups, step), in_specs=[v...  3.92 us
    pallas_call x1, Pallas kernels, pack(): pl.pallas_call(functools.partial(pack_kernel, groups, step), in_specs=[hb...  3.77 us
    pallas_call x1, Pallas kernels, edges(): pl.pallas_call(functools.partial(edges_kernel, width // count), grid=(1,)...  3.63 us
  transfers between devices with their start and end apart: 4, of which 3 were waited for; matrix products, arithmetic and copies ran while one was open for 4% of the time, Pallas kernels for 28%

profile of v3, /device:TPU:1, one launch (start us, length us, event | category | flops | bytes accessed | tf_op | source)
XLA Modules:
  0.0 90.9 jit_solution(14697230441941000906)
XLA Ops:
  0.6 3.8 %pack.1 = bf16[32,8,32,128]{3,2,1,0:T(8,128)(2,1)} custom-call(bf16[16,8,4096]{2,1,0:T(8,128)(2,1)} %x_ref.2, bf16[16,8,4096]{2,1,0:T(8,128)(2,1)} %x_ref.3), custom_call_target="tpu_custom_call" | custom-call | flops 536870912 | bytes 4194304 | tf_op jit(solution)/shard_map/pack/pallas_call | solution.py:104
  4.4 9.6 %all-to-all-start = ((bf16[32,8,32,128]{3,2,1,0:T(8,128)(2,1)}), bf16[32,8,32,128]{3,2,1,0:T(8,128)(2,1)S(1)}, u32[]{:S(2)}, u32[]{:S(2)}) async-start(bf16[32,8,32,128]{3,2,1,0:T(8,128)(2,1)} %pack.1), calls=%async_computation | async-start | bytes 4194304 | tf_op jit(solution)/shard_map/all_to_all | solution.py:391
  14.0 0.0 copy-start.1
  14.0 0.0 copy-start.2
  14.0 0.0 copy-start.3
  14.0 0.0 copy-start
  14.0 0.0 copy-start.4
  14.1 3.6 %edges.1 = (bf16[2,32,4096]{2,1,0:T(8,128)(2,1)}, bf16[32,128]{1,0:T(8,128)(2,1)}) custom-call(s32[1]{0:T(128)} %bitcast.odd_ref, bf16[16,8,4096]{2,1,0:T(8,128)(2,1)} %x_ref.2, bf16[16,8,4096]{2,1,0:T(8,128)(2,1)} %x_ref.3), custom_call_target="tpu_custom_call" | custom-call | flops 1048576 | bytes 1048576 | tf_op jit(solution)/shard_map/edges/pallas_call | solution.py:306
  17.7 2.9 %collective-permute-start = (bf16[32,128]{1,0:T(8,128)(2,1)}, bf16[32,128]{1,0:T(8,128)(2,1)S(1)}, u32[]{:S(2)}, u32[]{:S(2)}) collective-permute-start(bf16[32,128]{1,0:T(8,128)(2,1)} %get-tuple-element.13), channel_id=1, source_target_pairs={{0,16},{16,0},{32,48},{48,32},{64,80},{80,64},{96,112},{112,96},{1... | collective-permute-start | bytes 24584 | tf_op jit(solution)/shard_map/ppermute | solution.py:397
  20.6 0.0 copy-done.1
  20.6 0.2 copy.18
  20.8 0.2 copy.19
  20.9 0.2 copy.21
  21.1 0.2 copy.20
  21.3 0.0 copy-done.2
  21.3 0.0 copy-done.3
  21.3 0.0 copy-done
  21.4 2.2 %select_reduce_fusion = bf16[256,512]{1,0:T(8,128)(2,1)S(1)} fusion(f32[512,8]{0,1:T(8,128)S(1)} %get-tuple-element.19, f32[512,8]{0,1:T(8,128)S(1)} %get-tuple-element.20, f32[512,8]{0,1:T(8,128)S(1)} %get-tuple-element.18, f32[512,8]{0,1:T(8,128)S(1)} %copy-done, pred[256,8]{1,0:T(8,128)(4,1)S(1)} %copy.21, pred[256,8]{1,0:T(8,128)(4,1)S(1)} %copy.20, ...), kind=kLoop, calls=%fused_computation | loop fusion | flops 5111808 | bytes 335872 | tf_op jit(solution)/shard_map/reduce_prod | solution.py:41
  23.7 16.7 %collective-permute-done.ends_ref = bf16[32,128]{1,0:T(8,128)(2,1)S(1)} collective-permute-done((bf16[32,128]{1,0:T(8,128)(2,1)}, bf16[32,128]{1,0:T(8,128)(2,1)S(1)}, u32[]{:S(2)}, u32[]{:S(2)}) %collective-permute-start) | collective-permute-done | bytes 8224 | tf_op jit(solution)/shard_map/ppermute | solution.py:397
  40.4 1.7 %all-to-all-done.got_ref = bf16[32,8,32,128]{3,2,1,0:T(8,128)(2,1)S(1)} async-done(((bf16[32,8,32,128]{3,2,1,0:T(8,128)(2,1)}), bf16[32,8,32,128]{3,2,1,0:T(8,128)(2,1)S(1)}, u32[]{:S(2)}, u32[]{:S(2)}) %all-to-all-start) | async-done | bytes 2097184 | tf_op jit(solution)/shard_map/all_to_all | solution.py:391
  42.1 0.7 collective-permute-start.1
  42.8 0.0 copy-done.4
  42.8 0.1 copy.22.table_t_ref
  43.0 0.1 broadcast_in_dim.80.shift_ref
  43.1 6.6 %quad_forces.1 = bf16[32,8,32,128]{3,2,1,0:T(8,128)(2,1)} custom-call(bf16[32,8,32,128]{3,2,1,0:T(8,128)(2,1)S(1)} %all-to-all-done.got_ref, bf16[512,256]{1,0:T(8,128)(2,1)S(1)} %copy.22.table_t_ref, bf16[256,512]{1,0:T(8,128)(2,1)S(1)} %multiply_convert_fusion.table_w_ref, f32[512,128]{1,0:T(8,128)S(1)} %broadcast_in_dim.80.shift_ref), custom_call_target="tpu_custom_call" | custom-call | flops 1024 | bytes 1024 | tf_op jit(solution)/shard_map/quad_forces/pallas_call | solution.py:189
  49.7 9.1 %all-to-all-start.1 = ((bf16[32,8,32,128]{3,2,1,0:T(8,128)(2,1)}), bf16[32,8,32,128]{3,2,1,0:T(8,128)(2,1)S(1)}, u32[]{:S(2)}, u32[]{:S(2)}) async-start(bf16[32,8,32,128]{3,2,1,0:T(8,128)(2,1)} %quad_forces.1), calls=%async_computation.1 | async-start | bytes 4194304 | tf_op jit(solution)/shard_map/all_to_all | solution.py:391
  58.9 0.0 collective-permute-done.1.outer_ref
  58.9 7.7 %stencil.3.tan_ref = bf16[16,8,4096]{2,1,0:T(8,128)(2,1)} custom-call(s32[1]{0:T(128)} %bitcast.odd_ref, bf16[16,8,4096]{2,1,0:T(8,128)(2,1)} %x_ref.3, bf16[2,32,4096]{2,1,0:T(8,128)(2,1)S(1)} %collective-permute-done.1.outer_ref, bf16[32,128]{1,0:T(8,128)(2,1)S(1)} %collective-permute-done.ends_ref), custom_call_target="tpu_custom_call" | custom-call | flops 8589934592 | bytes 4194304 | tf_op jit(solution)/shard_map/stencil/pallas_call | solution.py:250
  66.6 7.6 %stencil.2.res_ref = bf16[16,8,4096]{2,1,0:T(8,128)(2,1)} custom-call(s32[1]{0:T(128)} %bitcast.odd_ref, bf16[16,8,4096]{2,1,0:T(8,128)(2,1)} %x_ref.2, bf16[2,32,4096]{2,1,0:T(8,128)(2,1)S(1)} %collective-permute-done.1.outer_ref, bf16[32,128]{1,0:T(8,128)(2,1)S(1)} %collective-permute-done.ends_ref), custom_call_target="tpu_custom_call" | custom-call | flops 8589934592 | bytes 4194304 | tf_op jit(solution)/shard_map/stencil/pallas_call | solution.py:250
  74.2 12.8 %all-to-all-done.1.force_ref = bf16[32,8,32,128]{3,2,1,0:T(8,128)(2,1)S(1)} async-done(((bf16[32,8,32,128]{3,2,1,0:T(8,128)(2,1)}), bf16[32,8,32,128]{3,2,1,0:T(8,128)(2,1)S(1)}, u32[]{:S(2)}, u32[]{:S(2)}) %all-to-all-start.1) | async-done | bytes 2097184 | tf_op jit(solution)/shard_map/all_to_all | solution.py:391
  87.0 3.9 %merge.1 = (f32[16,8,4096]{2,1,0:T(8,128)}, f32[16,8,4096]{2,1,0:T(8,128)}) custom-call(bf16[32,8,32,128]{3,2,1,0:T(8,128)(2,1)S(1)} %all-to-all-done.1.force_ref, bf16[16,8,4096]{2,1,0:T(8,128)(2,1)} %stencil.2.res_ref, bf16[16,8,4096]{2,1,0:T(8,128)(2,1)} %stencil.3.tan_ref), custom_call_target="tpu_custom_call" | custom-call | flops 536870912 | bytes 10485760 | tf_op jit(solution)/shard_map/merge/pallas_call | solution.py:367
  (6 shorter events, 0.1 us)
Async XLA Ops:
  4.4 37.7 %all-to-all-start = ((bf16[32,8,32,128]{3,2,1,0:T(8,128)(2,1)}), bf16[32,8,32,128]{3,2,1,0:T(8,128)(2,1)S(1)}, u32[]{:S(2)}, u32[]{:S(2)}) async-start(bf16[32,8,32,128]{3,2,1,0:T(8,128)(2,1)} %pack.1), calls=%async_computation | async-start | bytes 4194304 | tf_op jit(solution)/shard_map/all_to_all | solution.py:391
  14.0 6.6 %copy-start.1 = (s32[256,8]{0,1:T(8,128)S(1)}, s32[256,8]{0,1:T(8,128)}, u32[]{:S(2)}) copy-start(s32[256,8]{0,1:T(8,128)} %param.13) | copy-start | bytes 24580
  14.0 7.3 %copy-start.2 = (f32[512]{0:T(512)S(1)}, f32[512]{0:T(512)}, u32[]{:S(2)}) copy-start(f32[512]{0:T(512)} %param.10) | copy-start | bytes 6148
  14.0 7.3 %copy-start.3 = (f32[512]{0:T(512)S(1)}, f32[512]{0:T(512)}, u32[]{:S(2)}) copy-start(f32[512]{0:T(512)} %param.12) | copy-start | bytes 6148
  14.0 7.3 %copy-start = (f32[512,8]{0,1:T(8,128)S(1)}, f32[512,8]{0,1:T(8,128)}, u32[]{:S(2)}) copy-start(f32[512,8]{0,1:T(8,128)} %param.9) | copy-start | bytes 49156
  14.0 28.8 %copy-start.4 = (f32[512]{0:T(512)S(1)}, f32[512]{0:T(512)}, u32[]{:S(2)}) copy-start(f32[512]{0:T(512)} %param.11) | copy-start | bytes 6148
  17.7 22.7 %collective-permute-start = (bf16[32,128]{1,0:T(8,128)(2,1)}, bf16[32,128]{1,0:T(8,128)(2,1)S(1)}, u32[]{:S(2)}, u32[]{:S(2)}) collective-permute-start(bf16[32,128]{1,0:T(8,128)(2,1)} %get-tuple-element.13), channel_id=1, source_target_pairs={{0,16},{16,0},{32,48},{48,32},{64,80},{80,64},{96,112},{112,96},{1... | collective-permute-start | bytes 24584 | tf_op jit(solution)/shard_map/ppermute | solution.py:397
  42.1 16.7 %collective-permute-start.1 = (bf16[2,32,4096]{2,1,0:T(8,128)(2,1)}, bf16[2,32,4096]{2,1,0:T(8,128)(2,1)S(1)}, u32[]{:S(2)}, u32[]{:S(2)}) collective-permute-start(bf16[2,32,4096]{2,1,0:T(8,128)(2,1)} %get-tuple-element.16), channel_id=1, source_target_pairs={{16,32},{32,16},{48,64},{64,48},{80,96},{96,80},{17,33},{33,17},{4... | collective-permute-start | bytes 1572872 | tf_op jit(solution)/shard_map/ppermute | solution.py:399
  49.7 37.3 %all-to-all-start.1 = ((bf16[32,8,32,128]{3,2,1,0:T(8,128)(2,1)}), bf16[32,8,32,128]{3,2,1,0:T(8,128)(2,1)S(1)}, u32[]{:S(2)}, u32[]{:S(2)}) async-start(bf16[32,8,32,128]{3,2,1,0:T(8,128)(2,1)} %quad_forces.1), calls=%async_computation.1 | async-start | bytes 4194304 | tf_op jit(solution)/shard_map/all_to_all | solution.py:391

commit v4 on v3

--- a/solution.py
+++ b/solution.py
@@ -59,15 +59,17 @@
     return jnp.where(inside, pltpu.roll(v, width - 1 if by > 0 else 1, 1), 0.0)
 
 
-def pack_kernel(groups, step, disp_ref, dir_ref, send_ref, in_buf, out_buf, in_sem, out_sem):
+def pack_kernel(groups, early, step, disp_ref, dir_ref, send_ref, in_buf, out_buf, in_sem, out_sem):
     modes, rows, width = disp_ref.shape
     count, _, both, each = send_ref.shape
     size = both * rows
     per = count // groups
     span = per * each
 
+    ahead = groups // early
+
     def loads(g):
-        cols = pl.ds(g * span, span)
+        cols = pl.ds(g * ahead * span, ahead * span)
         return [
             pltpu.make_async_copy(ref.at[:, :, cols], in_buf.at[f, :, :, cols], in_sem.at[f, g])
             for f, ref in enumerate((disp_ref, dir_ref))
@@ -77,13 +79,13 @@
         at = pl.ds(g * per, per)
         return pltpu.make_async_copy(out_buf.at[at], send_ref.at[at], out_sem.at[g])
 
-    for g in range(groups):
+    for g in range(early):
         for copy in loads(g):
             copy.start()
     to, frm = iotas((size, size))
     perm = one_hot(frm == (to % both) * rows + to // both)
     for g in range(groups):
-        for copy in loads(g):
+        for copy in loads(g // ahead) if g % ahead == 0 else []:
             copy.wait()
         for d in range(g * per, (g + 1) * per, step):
             fields = in_buf[:, :, :, pl.ds(d * each, step * each)].reshape(size, step * each)
@@ -95,21 +97,21 @@
         store(g).wait()
 
 
-def pack(displacement, direction, count, groups=8, step=2):
+def pack(displacement, direction, count, groups=4, early=2, step=2):
     modes, rows, width = displacement.shape
     each = width // count
     both = 2 * modes
     hbm = pl.BlockSpec(memory_space=HBM)
     shape = (count, rows, both, each)
     return pl.pallas_call(
-        functools.partial(pack_kernel, groups, step),
+        functools.partial(pack_kernel, groups, early, step),
         in_specs=[hbm, hbm],
         out_specs=hbm,
         out_shape=pltpu.HBM(shape, BF16),
         scratch_shapes=[
             pltpu.VMEM((2, modes, rows, width), BF16),
             pltpu.VMEM(shape, BF16),
-            pltpu.SemaphoreType.DMA((2, groups)),
+            pltpu.SemaphoreType.DMA((2, early)),
             pltpu.SemaphoreType.DMA((groups,)),
         ],
         compiler_params=pltpu.CompilerParams(vmem_limit_bytes=VMEM),
@@ -147,7 +149,8 @@
         value = jnp.where(far == 0, jnp.where(near, jnp.where(full, -8.0, 1.0), jnp.where(full, 1.0, 0.0)), 0.0)
         cross_ref[band] = jnp.where((jnp.abs(far) == 1) & near & full, 2.0, value).astype(BF16)
 
-    def one_step(i, _):
+    def forward(i):
+        slot = i % 2
         disp = field_rows(i, 0)
         dire = field_rows(i, 1)
         for q in range(quad // chunk):
@@ -163,21 +166,27 @@
             inv = pl.reciprocal(big, approx=True)
             sig = e * pl.reciprocal(one, approx=True)
             square = inv * inv
-            w_ref[0, at, :] = square.astype(BF16)
-            w_ref[1, at, :] = ((sig * inv) * (square * probe)).astype(BF16)
-        table_w = table_w_ref[...]
-        weight = jnp.where((i == pairs - 1) | (i == pairs), STIFF, 0.0)
-        for f, factor in enumerate((-1.0, 0.5)):
-            cross = jnp.dot(field_rows(steps - 1 - i, f), cross_ref[i // pairs], preferred_element_type=F32)
-            force = jnp.dot(table_w, w_ref[f], preferred_element_type=F32)
-            force = (force + (factor * weight) * cross).astype(BF16)
+            w_ref[slot, 0, at, :] = square.astype(BF16)
+            w_ref[slot, 1, at, :] = ((sig * inv) * (square * probe)).astype(BF16)
+
+    def back(i):
+        band, pair = i // pairs, i % pairs
+        for f, factor in enumerate((-STIFF, 0.5 * STIFF)):
+            force = jnp.dot(table_w_ref[...], w_ref[i % 2, f], preferred_element_type=F32)
+            if i in (pairs - 1, pairs):
+                facing = field_rows(steps - 1 - i, f)
+                force = force + factor * jnp.dot(facing, cross_ref[band], preferred_element_type=F32)
+            force = force.astype(BF16)
             for k in range(deep):
                 part = force[:, k * each : (k + 1) * each].reshape(per, modes, each)
-                out_buf[pl.ds(i // pairs * per, per), i % pairs * deep + k, f * modes : (f + 1) * modes, :] = part
+                out_buf[band * per : (band + 1) * per, pair * deep + k, f * modes : (f + 1) * modes, :] = part
         store(i).start()
-        return 0
-
-    lax.fori_loop(0, steps, one_step, 0)
+
+    for i in range(steps + 1):
+        if i < steps:
+            forward(i)
+        if i > 0:
+            back(i - 1)
     for i in range(steps):
         store(i).wait()
 
@@ -193,7 +202,7 @@
         out_shape=pltpu.HBM(got.shape, BF16),
         scratch_shapes=[
             pltpu.VMEM(got.shape, BF16),
-            pltpu.VMEM((2, quad, deep * each), BF16),
+            pltpu.VMEM((2, 2, quad, deep * each), BF16),
             pltpu.VMEM((2, deep * each, deep * each), BF16),
             pltpu.SemaphoreType.DMA((2 * rows // deep,)),
         ],
@@ -360,7 +369,7 @@
             copy.wait()
 
 
-def merge(force, res, tan, groups=8, step=2):
+def merge(force, res, tan, groups=4, step=2):
     count, rows, both, each = force.shape
     vmem = pl.BlockSpec(memory_space=pltpu.VMEM)
     hbm = pl.BlockSpec(memory_space=HBM)

time: 91.4 us -> 88.3 us (0.966)
  Pallas kernels: 33.2 us -> 30 us
    pallas_call x1, Pallas kernels: 6.61 us -> 4.6 us  [quad_forces(): pl.pallas_call(functools.partial(quad_kernel, 128, deep), in_specs=[vmem]...]
  transfers between devices with their start and end apart: 4 -> 4, of which waited for: 3 -> 3; matrix products, arithmetic and copies ran while one was open for 4% -> 4% of each run, Pallas kernels for 28% -> 27%
where the time goes in v4:
time: 88.3 us; the launch traced here: 87.9 us
  waiting for transfers between devices  31.3 us (35%)
  Pallas kernels  30 us (34%)
  starting transfers between devices  22.3 us (25%)
  other arithmetic  2.32 us (3%)
  between operations  1.01 us (1%)
  local copies, waits for them, and re-layouts  0.96 us (1%)
    all_to_all x2, starting transfers between devices, exchange(): lax.all_to_all(x, ('space', 'mode'), split_axis=0, concat_axis=0, axis_in...  18.7 us
    ppermute x1, waiting for transfers between devices, shards(): ends = lax.ppermute(ends, 'space', [(i, i ^ 1) for i in range(bands)])  16.7 us
    pallas_call x2, Pallas kernels, stencil(): pl.pallas_call(functools.partial(stencil_kernel, 512, width // count), gr...  15.3 us
    all_to_all x2, waiting for transfers between devices, exchange(): lax.all_to_all(x, ('space', 'mode'), split_axis=0, concat_axis=0, axis_in...  14.6 us
    pallas_call x1, Pallas kernels, quad_forces(): pl.pallas_call(functools.partial(quad_kernel, 128, deep), in_specs=[vmem]...  4.6 us
    pallas_call x1, Pallas kernels, edges(): pl.pallas_call(functools.partial(edges_kernel, width // count), grid=(1,)...  3.63 us
    pallas_call x1, Pallas kernels, merge(): pl.pallas_call(functools.partial(merge_kernel, groups, step), in_specs=[v...  3.48 us
    pallas_call x1, Pallas kernels, pack(): pl.pallas_call(functools.partial(pack_kernel, groups, early, step), in_sp...  2.99 us
  transfers between devices with their start and end apart: 4, of which 3 were waited for; matrix products, arithmetic and copies ran while one was open for 4% of the time, Pallas kernels for 27%

profile of v4, /device:TPU:1, one launch (start us, length us, event | category | flops | bytes accessed | tf_op | source)
XLA Modules:
  0.0 87.9 jit_solution(11320671491404346428)
XLA Ops:
  0.6 3.0 %pack.1 = bf16[32,8,32,128]{3,2,1,0:T(8,128)(2,1)} custom-call(bf16[16,8,4096]{2,1,0:T(8,128)(2,1)} %x_ref.2, bf16[16,8,4096]{2,1,0:T(8,128)(2,1)} %x_ref.3), custom_call_target="tpu_custom_call" | custom-call | flops 536870912 | bytes 4194304 | tf_op jit(solution)/shard_map/pack/pallas_call | solution.py:106
  3.6 9.6 %all-to-all-start = ((bf16[32,8,32,128]{3,2,1,0:T(8,128)(2,1)}), bf16[32,8,32,128]{3,2,1,0:T(8,128)(2,1)S(1)}, u32[]{:S(2)}, u32[]{:S(2)}) async-start(bf16[32,8,32,128]{3,2,1,0:T(8,128)(2,1)} %pack.1), calls=%async_computation | async-start | bytes 4194304 | tf_op jit(solution)/shard_map/all_to_all | solution.py:400
  13.2 0.0 copy-start.1
  13.3 0.0 copy-start.2
  13.3 0.0 copy-start.3
  13.3 0.0 copy-start
  13.3 0.0 copy-start.4
  13.3 3.6 %edges.1 = (bf16[2,32,4096]{2,1,0:T(8,128)(2,1)}, bf16[32,128]{1,0:T(8,128)(2,1)}) custom-call(s32[1]{0:T(128)} %bitcast.odd_ref, bf16[16,8,4096]{2,1,0:T(8,128)(2,1)} %x_ref.2, bf16[16,8,4096]{2,1,0:T(8,128)(2,1)} %x_ref.3), custom_call_target="tpu_custom_call" | custom-call | flops 1048576 | bytes 1048576 | tf_op jit(solution)/shard_map/edges/pallas_call | solution.py:315
  16.9 2.9 %collective-permute-start = (bf16[32,128]{1,0:T(8,128)(2,1)}, bf16[32,128]{1,0:T(8,128)(2,1)S(1)}, u32[]{:S(2)}, u32[]{:S(2)}) collective-permute-start(bf16[32,128]{1,0:T(8,128)(2,1)} %get-tuple-element.13), channel_id=1, source_target_pairs={{0,16},{16,0},{32,48},{48,32},{64,80},{80,64},{96,112},{112,96},{1... | collective-permute-start | bytes 24584 | tf_op jit(solution)/shard_map/ppermute | solution.py:406
  19.8 0.0 copy-done.1
  19.9 0.2 copy.18
  20.0 0.2 copy.19
  20.2 0.2 copy.21
  20.4 0.2 copy.20
  20.6 0.0 copy-done.2
  20.6 0.0 copy-done.3
  20.6 0.0 copy-done
  20.6 2.2 %select_reduce_fusion = bf16[256,512]{1,0:T(8,128)(2,1)S(1)} fusion(f32[512,8]{0,1:T(8,128)S(1)} %get-tuple-element.19, f32[512,8]{0,1:T(8,128)S(1)} %get-tuple-element.20, f32[512,8]{0,1:T(8,128)S(1)} %get-tuple-element.18, f32[512,8]{0,1:T(8,128)S(1)} %copy-done, pred[256,8]{1,0:T(8,128)(4,1)S(1)} %copy.21, pred[256,8]{1,0:T(8,128)(4,1)S(1)} %copy.20, ...), kind=kLoop, calls=%fused_computation | loop fusion | flops 5111808 | bytes 335872 | tf_op jit(solution)/shard_map/reduce_prod | solution.py:41
  22.9 16.7 %collective-permute-done.ends_ref = bf16[32,128]{1,0:T(8,128)(2,1)S(1)} collective-permute-done((bf16[32,128]{1,0:T(8,128)(2,1)}, bf16[32,128]{1,0:T(8,128)(2,1)S(1)}, u32[]{:S(2)}, u32[]{:S(2)}) %collective-permute-start) | collective-permute-done | bytes 8224 | tf_op jit(solution)/shard_map/ppermute | solution.py:406
  39.7 1.7 %all-to-all-done.got_ref = bf16[32,8,32,128]{3,2,1,0:T(8,128)(2,1)S(1)} async-done(((bf16[32,8,32,128]{3,2,1,0:T(8,128)(2,1)}), bf16[32,8,32,128]{3,2,1,0:T(8,128)(2,1)S(1)}, u32[]{:S(2)}, u32[]{:S(2)}) %all-to-all-start) | async-done | bytes 2097184 | tf_op jit(solution)/shard_map/all_to_all | solution.py:400
  41.4 0.7 collective-permute-start.1
  42.1 0.0 copy-done.4
  42.1 0.1 copy.22.table_t_ref
  42.2 0.1 broadcast_in_dim.80.shift_ref
  42.4 4.6 %quad_forces.1 = bf16[32,8,32,128]{3,2,1,0:T(8,128)(2,1)} custom-call(bf16[32,8,32,128]{3,2,1,0:T(8,128)(2,1)S(1)} %all-to-all-done.got_ref, bf16[512,256]{1,0:T(8,128)(2,1)S(1)} %copy.22.table_t_ref, bf16[256,512]{1,0:T(8,128)(2,1)S(1)} %multiply_convert_fusion.table_w_ref, f32[512,128]{1,0:T(8,128)S(1)} %broadcast_in_dim.80.shift_ref), custom_call_target="tpu_custom_call" | custom-call | flops 1024 | bytes 1024 | tf_op jit(solution)/shard_map/quad_forces/pallas_call | solution.py:198
  47.0 9.1 %all-to-all-start.1 = ((bf16[32,8,32,128]{3,2,1,0:T(8,128)(2,1)}), bf16[32,8,32,128]{3,2,1,0:T(8,128)(2,1)S(1)}, u32[]{:S(2)}, u32[]{:S(2)}) async-start(bf16[32,8,32,128]{3,2,1,0:T(8,128)(2,1)} %quad_forces.1), calls=%async_computation.1 | async-start | bytes 4194304 | tf_op jit(solution)/shard_map/all_to_all | solution.py:400
  56.1 0.0 collective-permute-done.1.outer_ref
  56.1 7.7 %stencil.3.tan_ref = bf16[16,8,4096]{2,1,0:T(8,128)(2,1)} custom-call(s32[1]{0:T(128)} %bitcast.odd_ref, bf16[16,8,4096]{2,1,0:T(8,128)(2,1)} %x_ref.3, bf16[2,32,4096]{2,1,0:T(8,128)(2,1)S(1)} %collective-permute-done.1.outer_ref, bf16[32,128]{1,0:T(8,128)(2,1)S(1)} %collective-permute-done.ends_ref), custom_call_target="tpu_custom_call" | custom-call | flops 8589934592 | bytes 4194304 | tf_op jit(solution)/shard_map/stencil/pallas_call | solution.py:259
  63.8 7.6 %stencil.2.res_ref = bf16[16,8,4096]{2,1,0:T(8,128)(2,1)} custom-call(s32[1]{0:T(128)} %bitcast.odd_ref, bf16[16,8,4096]{2,1,0:T(8,128)(2,1)} %x_ref.2, bf16[2,32,4096]{2,1,0:T(8,128)(2,1)S(1)} %collective-permute-done.1.outer_ref, bf16[32,128]{1,0:T(8,128)(2,1)S(1)} %collective-permute-done.ends_ref), custom_call_target="tpu_custom_call" | custom-call | flops 8589934592 | bytes 4194304 | tf_op jit(solution)/shard_map/stencil/pallas_call | solution.py:259
  71.4 12.8 %all-to-all-done.1.force_ref = bf16[32,8,32,128]{3,2,1,0:T(8,128)(2,1)S(1)} async-done(((bf16[32,8,32,128]{3,2,1,0:T(8,128)(2,1)}), bf16[32,8,32,128]{3,2,1,0:T(8,128)(2,1)S(1)}, u32[]{:S(2)}, u32[]{:S(2)}) %all-to-all-start.1) | async-done | bytes 2097184 | tf_op jit(solution)/shard_map/all_to_all | solution.py:400
  84.2 3.5 %merge.1 = (f32[16,8,4096]{2,1,0:T(8,128)}, f32[16,8,4096]{2,1,0:T(8,128)}) custom-call(bf16[32,8,32,128]{3,2,1,0:T(8,128)(2,1)S(1)} %all-to-all-done.1.force_ref, bf16[16,8,4096]{2,1,0:T(8,128)(2,1)} %stencil.2.res_ref, bf16[16,8,4096]{2,1,0:T(8,128)(2,1)} %stencil.3.tan_ref), custom_call_target="tpu_custom_call" | custom-call | flops 536870912 | bytes 10485760 | tf_op jit(solution)/shard_map/merge/pallas_call | solution.py:376
  (6 shorter events, 0.1 us)
Async XLA Ops:
  3.6 37.8 %all-to-all-start = ((bf16[32,8,32,128]{3,2,1,0:T(8,128)(2,1)}), bf16[32,8,32,128]{3,2,1,0:T(8,128)(2,1)S(1)}, u32[]{:S(2)}, u32[]{:S(2)}) async-start(bf16[32,8,32,128]{3,2,1,0:T(8,128)(2,1)} %pack.1), calls=%async_computation | async-start | bytes 4194304 | tf_op jit(solution)/shard_map/all_to_all | solution.py:400
  13.2 6.6 %copy-start.1 = (s32[256,8]{0,1:T(8,128)S(1)}, s32[256,8]{0,1:T(8,128)}, u32[]{:S(2)}) copy-start(s32[256,8]{0,1:T(8,128)} %param.13) | copy-start | bytes 24580
  13.3 7.3 %copy-start.2 = (f32[512]{0:T(512)S(1)}, f32[512]{0:T(512)}, u32[]{:S(2)}) copy-start(f32[512]{0:T(512)} %param.10) | copy-start | bytes 6148
  13.3 7.3 %copy-start.3 = (f32[512]{0:T(512)S(1)}, f32[512]{0:T(512)}, u32[]{:S(2)}) copy-start(f32[512]{0:T(512)} %param.12) | copy-start | bytes 6148
  13.3 7.3 %copy-start = (f32[512,8]{0,1:T(8,128)S(1)}, f32[512,8]{0,1:T(8,128)}, u32[]{:S(2)}) copy-start(f32[512,8]{0,1:T(8,128)} %param.9) | copy-start | bytes 49156
  13.3 28.8 %copy-start.4 = (f32[512]{0:T(512)S(1)}, f32[512]{0:T(512)}, u32[]{:S(2)}) copy-start(f32[512]{0:T(512)} %param.11) | copy-start | bytes 6148
  16.9 22.7 %collective-permute-start = (bf16[32,128]{1,0:T(8,128)(2,1)}, bf16[32,128]{1,0:T(8,128)(2,1)S(1)}, u32[]{:S(2)}, u32[]{:S(2)}) collective-permute-start(bf16[32,128]{1,0:T(8,128)(2,1)} %get-tuple-element.13), channel_id=1, source_target_pairs={{0,16},{16,0},{32,48},{48,32},{64,80},{80,64},{96,112},{112,96},{1... | collective-permute-start | bytes 24584 | tf_op jit(solution)/shard_map/ppermute | solution.py:406
  41.4 14.7 %collective-permute-start.1 = (bf16[2,32,4096]{2,1,0:T(8,128)(2,1)}, bf16[2,32,4096]{2,1,0:T(8,128)(2,1)S(1)}, u32[]{:S(2)}, u32[]{:S(2)}) collective-permute-start(bf16[2,32,4096]{2,1,0:T(8,128)(2,1)} %get-tuple-element.16), channel_id=1, source_target_pairs={{16,32},{32,16},{48,64},{64,48},{80,96},{96,80},{17,33},{33,17},{4... | collective-permute-start | bytes 1572872 | tf_op jit(solution)/shard_map/ppermute | solution.py:408
  47.0 37.3 %all-to-all-start.1 = ((bf16[32,8,32,128]{3,2,1,0:T(8,128)(2,1)}), bf16[32,8,32,128]{3,2,1,0:T(8,128)(2,1)S(1)}, u32[]{:S(2)}, u32[]{:S(2)}) async-start(bf16[32,8,32,128]{3,2,1,0:T(8,128)(2,1)} %quad_forces.1), calls=%async_computation.1 | async-start | bytes 4194304 | tf_op jit(solution)/shard_map/all_to_all | solution.py:400

commit v5 on v4

--- a/solution.py
+++ b/solution.py
@@ -207,38 +207,25 @@
             pltpu.SemaphoreType.DMA((2 * rows // deep,)),
         ],
         compiler_params=pltpu.CompilerParams(vmem_limit_bytes=VMEM),
-        cost_estimate=pl.CostEstimate(flops=1 << 10, bytes_accessed=1 << 10, transcendentals=0),
+        cost_estimate=pl.CostEstimate(flops=3 << 31, bytes_accessed=1 << 10, transcendentals=0),
         name="quad_forces",
     )(got, table_t, table_w, shift)
 
 
-def stencil_kernel(chunk, block, odd_ref, x_ref, outer_ref, ends_ref, out_ref, inner_ref, side_ref):
+def stencil_kernel(chunk, x_ref, out_ref, side_ref):
     modes, rows, width = x_ref.shape
     size = modes * rows
-    blocks = width // block
-    odd = odd_ref[0]
-    to, frm = iotas((size, size + modes))
+    to, frm = iotas((size, size))
     gap = jnp.abs(to - frm)
     same = to // rows == frm // rows
     centre = jnp.where(gap == 0, 20.0, jnp.where(gap == 1, -8.0, jnp.where(gap == 2, 1.0, 0.0)))
-    corner = (frm - size == to // rows) & (to % rows == (rows - 1) * (1 - odd))
-    centre = jnp.where(frm < size, jnp.where(same, centre, 0.0), jnp.where(corner, 2.0, 0.0)).astype(BF16)
-    to, frm = iotas((size, size))
-    gap = jnp.abs(to - frm)
+    centre = jnp.where(same, centre, 0.0).astype(BF16)
     side = jnp.where(gap == 0, -8.0, jnp.where(gap == 1, 2.0, 0.0))
-    side = jnp.where(to // rows == frm // rows, side, 0.0).astype(BF16)
-    to, frm = iotas((size, 2 * modes))
-    place = one_hot((frm % modes == to // rows) & (to % rows == frm // modes + (rows - 2) * odd))
-    item, col = iotas((ends_ref.shape[1], chunk))
-    target = jnp.where(item < blocks, item * block - 1, (item - blocks + 1) * block)
-    target = jnp.where(item < 2 * blocks, target, -1)
+    side = jnp.where(same, side, 0.0).astype(BF16)
     for c in range(width // chunk):
         cols = pl.ds(c * chunk, chunk)
         x = x_ref[:, :, cols].reshape(size, chunk)
-        spread = jnp.dot(ends_ref[...], one_hot(target == col + c * chunk), preferred_element_type=F32).astype(BF16)
-        inner = jnp.dot(centre, jnp.concatenate([x, spread], axis=0), preferred_element_type=F32)
-        terms = jnp.dot(place, outer_ref[:, :, cols].reshape(2 * modes, chunk), preferred_element_type=F32)
-        inner_ref[:, :, cols] = (STIFF * inner + terms).reshape(modes, rows, chunk)
+        out_ref[:, :, cols] = jnp.dot(centre, x, preferred_element_type=F32).reshape(modes, rows, chunk)
         side_ref[:, :, cols] = jnp.dot(side, x, preferred_element_type=F32).reshape(modes, rows, chunk)
     lane = lax.broadcasted_iota(jnp.int32, (rows, width), 1)
 
@@ -247,31 +234,66 @@
         y = side_ref[m]
         right = shifted(y + shifted(x, lane, 1), lane, 1)
         left = shifted(y + shifted(x, lane, -1), lane, -1)
-        out_ref[m] = (inner_ref[m] + STIFF * (right + left)).astype(BF16)
+        out_ref[m] = STIFF * (out_ref[m] + right + left)
         return 0
 
     lax.fori_loop(0, modes, one_mode, 0)
 
 
-def stencil(odd, x, outer, ends, field, count):
-    modes, rows, width = x.shape
-    whole = pl.BlockSpec((modes, rows, width), lambda i: (0, 0, 0))
-    return pl.pallas_call(
-        functools.partial(stencil_kernel, 512, width // count),
+def stencil(x):
+    whole = pl.BlockSpec(x.shape, lambda i: (0, 0, 0))
+    return pl.pallas_call(
+        functools.partial(stencil_kernel, 512),
         grid=(1,),
+        in_specs=[whole],
+        out_specs=whole,
+        out_shape=pltpu.HBM(x.shape, F32),
+        scratch_shapes=[pltpu.VMEM(x.shape, F32)],
+        compiler_params=pltpu.CompilerParams(vmem_limit_bytes=VMEM),
+        cost_estimate=pl.CostEstimate(flops=1 << 30, bytes_accessed=1 << 20, transcendentals=0),
+        name="stencil",
+    )(in_hbm(x))
+
+
+def outer_kernel(block, blocks, odd_ref, outer_ref, ends_ref, res_ref, tan_ref, res_out, tan_out):
+    modes, rows, chunk = res_ref.shape
+    size = modes * rows
+    odd = odd_ref[0]
+    to, frm = iotas((size, modes))
+    corner = one_hot((frm == to // rows) & (to % rows == (rows - 1) * (1 - odd)))
+    item, col = iotas((ends_ref.shape[1], chunk))
+    target = jnp.where(item < blocks, item * block - 1, (item - blocks + 1) * block)
+    target = jnp.where(item < 2 * blocks, target, -1)
+    spread = jnp.dot(ends_ref[...], one_hot(target == col + pl.program_id(0) * chunk), preferred_element_type=F32).astype(BF16)
+    to, frm = iotas((size, 2 * modes))
+    place = one_hot((frm % modes == to // rows) & (to % rows == frm // modes + (rows - 2) * odd))
+    for f, (ref, out) in enumerate(((res_ref, res_out), (tan_ref, tan_out))):
+        terms = outer_ref[:, f * modes : (f + 1) * modes, :].reshape(2 * modes, chunk)
+        terms = jnp.dot(place, terms, preferred_element_type=F32)
+        corners = jnp.dot(corner, spread[f * modes : (f + 1) * modes], preferred_element_type=F32)
+        terms = (terms + (2.0 * STIFF) * corners).reshape(modes, rows, chunk)
+        out[...] = (ref[...] + terms).astype(BF16)
+
+
+def add_outer(odd, outer, ends, res, tan, count, steps=4):
+    modes, rows, width = res.shape
+    field = pl.BlockSpec((modes, rows, width // steps), lambda i: (0, 0, i))
+    return pl.pallas_call(
+        functools.partial(outer_kernel, width // count, count),
+        grid=(steps,),
         in_specs=[
             pl.BlockSpec(memory_space=pltpu.SMEM),
-            whole,
-            pl.BlockSpec((2, modes, width), lambda i: (0, field, 0)),
-            pl.BlockSpec((modes, ends.shape[1]), lambda i: (field, 0)),
+            pl.BlockSpec((2, 2 * modes, width // steps), lambda i: (0, 0, i)),
+            pl.BlockSpec(ends.shape, lambda i: (0, 0)),
+            field,
+            field,
         ],
-        out_specs=whole,
-        out_shape=pltpu.HBM(x.shape, BF16),
-        scratch_shapes=[pltpu.VMEM(x.shape, F32)] * 2,
-        compiler_params=pltpu.CompilerParams(vmem_limit_bytes=VMEM),
-        cost_estimate=pl.CostEstimate(flops=1 << 33, bytes_accessed=4 * MIB, transcendentals=0),
-        name="stencil",
-    )(odd, in_hbm(x), outer, ends)
+        out_specs=[field, field],
+        out_shape=[pltpu.HBM(res.shape, BF16)] * 2,
+        compiler_params=pltpu.CompilerParams(vmem_limit_bytes=VMEM),
+        cost_estimate=pl.CostEstimate(flops=5 << 32, bytes_accessed=7 * MIB, transcendentals=0),
+        name="add_outer",
+    )(odd, outer, ends, in_hbm(res), in_hbm(tan))
 
 
 def edges_kernel(block, odd_ref, disp_ref, dir_ref, terms_ref, ends_ref):
@@ -404,17 +426,18 @@
     got = exchange(send)
     terms, ends = edges(odd, first, second, count)
     ends = lax.ppermute(ends, "space", [(i, i ^ 1) for i in range(bands)])
-    terms, ends, got = lax.optimization_barrier((terms, ends, got))
-    outer = lax.ppermute(terms, "space", [(i + a, i + b) for i in range(1, bands - 1, 2) for a, b in ((0, 1), (1, 0))])
+    res, tan = stencil(first), stencil(second)
     table = basis(quad_nodes, degrees)
     scale = quad_weights * pressure_load * (STEEP * STEEP)
     table_w = (table.astype(F32) * scale[None, :]).astype(BF16)
     table_t = -STEEP * table.T
     shift = jnp.broadcast_to((STEEP * (gap_nominal - FLOOR))[:, None], (gap_nominal.shape[0], 128))
+    terms, res, tan, table_t, table_w, shift = lax.optimization_barrier((terms, res, tan, table_t, table_w, shift))
+    outer = lax.ppermute(terms, "space", [(i + a, i + b) for i in range(1, bands - 1, 2) for a, b in ((0, 1), (1, 0))])
+    got, ends = lax.optimization_barrier((got, ends))
     force = quad_forces(got, table_t, table_w, shift)
     back = exchange(force)
-    res = stencil(odd, displacement, outer, ends, 0, count)
-    tan = stencil(odd, direction, outer, ends, 1, count)
+    res, tan = add_outer(odd, outer, ends, res, tan, count)
     return tuple(merge(back, res, tan))
 
 

time: 88.3 us -> 85.9 us (0.973)
  waiting for transfers between devices: 31.3 us -> 25.5 us
  Pallas kernels: 30 us -> 33.1 us
  starting transfers between devices: 22.3 us -> 21 us
  local copies, waits for them, and re-layouts: 0.96 us -> 1.89 us
    ppermute x1, waiting for transfers between devices: 16.7 us -> 0.75 us  [shards(): ends = lax.ppermute(ends, 'space', [(i, i ^ 1) for i in range(bands)])]
    all_to_all x2, waiting for transfers between devices: 14.6 us -> 24.8 us  [exchange(): lax.all_to_all(x, ('space', 'mode'), split_axis=0, concat_axis=0, axis_in...]
    pallas_call x2 -> x3, Pallas kernels: 15.3 us -> 18.4 us  [the longest x2 13.3 us: stencil(): pl.pallas_call(functools.partial(stencil_kernel, 512), grid=(1,), in_spec...]
    all_to_all x2, starting transfers between devices: 18.7 us -> 17.3 us  [exchange(): lax.all_to_all(x, ('space', 'mode'), split_axis=0, concat_axis=0, axis_in...]
    optimization_barrier x0 -> x1, local copies, waits for them, and re-layouts: none -> 1.08 us  [shards(): lax.optimization_barrier((terms, res, tan, table_t, table_w, shift))]
  transfers between devices with their start and end apart: 4 -> 4, of which waited for: 3 -> 3; matrix products, arithmetic and copies ran while one was open for 4% -> 6% of each run, Pallas kernels for 27% -> 31%
where the time goes in v5:
time: 85.9 us; the launch traced here: 85.3 us
  Pallas kernels  33.1 us (39%)
  waiting for transfers between devices  25.5 us (30%)
  starting transfers between devices  21 us (24%)
  other arithmetic  3.03 us (4%)
  local copies, waits for them, and re-layouts  1.89 us (2%)
    all_to_all x2, waiting for transfers between devices, exchange(): lax.all_to_all(x, ('space', 'mode'), split_axis=0, concat_axis=0, axis_in...  24.8 us
    all_to_all x2, starting transfers between devices, exchange(): lax.all_to_all(x, ('space', 'mode'), split_axis=0, concat_axis=0, axis_in...  17.3 us
    pallas_call x2, Pallas kernels, stencil(): pl.pallas_call(functools.partial(stencil_kernel, 512), grid=(1,), in_spec...  13.3 us
    pallas_call x1, Pallas kernels, add_outer(): pl.pallas_call(functools.partial(outer_kernel, width // count, count), gr...  5.11 us
    pallas_call x1, Pallas kernels, quad_forces(): pl.pallas_call(functools.partial(quad_kernel, 128, deep), in_specs=[vmem]...  4.57 us
    pallas_call x1, Pallas kernels, edges(): pl.pallas_call(functools.partial(edges_kernel, width // count), grid=(1,)...  3.66 us
    pallas_call x1, Pallas kernels, merge(): pl.pallas_call(functools.partial(merge_kernel, groups, step), in_specs=[v...  3.48 us
    pallas_call x1, Pallas kernels, pack(): pl.pallas_call(functools.partial(pack_kernel, groups, early, step), in_sp...  2.99 us
  transfers between devices with their start and end apart: 4, of which 3 were waited for; matrix products, arithmetic and copies ran while one was open for 6% of the time, Pallas kernels for 31%

profile of v5, /device:TPU:1, one launch (start us, length us, event | category | flops | bytes accessed | tf_op | source)
XLA Modules:
  0.0 85.3 jit_solution(15792411573619067136)
XLA Ops:
  0.6 3.0 %pack.1 = bf16[32,8,32,128]{3,2,1,0:T(8,128)(2,1)} custom-call(bf16[16,8,4096]{2,1,0:T(8,128)(2,1)} %x_ref, bf16[16,8,4096]{2,1,0:T(8,128)(2,1)} %x_ref.1), custom_call_target="tpu_custom_call" | custom-call | flops 536870912 | bytes 4194304 | tf_op jit(solution)/shard_map/pack/pallas_call | solution.py:106
  3.6 9.6 %all-to-all-start = ((bf16[32,8,32,128]{3,2,1,0:T(8,128)(2,1)}), bf16[32,8,32,128]{3,2,1,0:T(8,128)(2,1)S(1)}, u32[]{:S(2)}, u32[]{:S(2)}) async-start(bf16[32,8,32,128]{3,2,1,0:T(8,128)(2,1)} %pack.1), calls=%async_computation | async-start | bytes 4194304 | tf_op jit(solution)/shard_map/all_to_all | solution.py:422
  13.2 0.0 copy-start.1
  13.3 3.7 %edges.1 = (bf16[2,32,4096]{2,1,0:T(8,128)(2,1)}, bf16[32,128]{1,0:T(8,128)(2,1)}) custom-call(s32[1]{0:T(128)} %bitcast.odd_ref, bf16[16,8,4096]{2,1,0:T(8,128)(2,1)} %x_ref, bf16[16,8,4096]{2,1,0:T(8,128)(2,1)} %x_ref.1), custom_call_target="tpu_custom_call" | custom-call | flops 1048576 | bytes 1048576 | tf_op jit(solution)/shard_map/edges/pallas_call | solution.py:337
  16.9 0.0 copy-start.4
  16.9 0.0 copy-start.2
  16.9 0.0 copy-start.3
  16.9 3.0 %collective-permute-start = (bf16[32,128]{1,0:T(8,128)(2,1)}, bf16[32,128]{1,0:T(8,128)(2,1)S(1)}, u32[]{:S(2)}, u32[]{:S(2)}) collective-permute-start(bf16[32,128]{1,0:T(8,128)(2,1)} %get-tuple-element.20), channel_id=1, source_target_pairs={{0,16},{16,0},{32,48},{48,32},{64,80},{80,64},{96,112},{112,96},{1... | collective-permute-start | bytes 24584 | tf_op jit(solution)/shard_map/ppermute | solution.py:428
  19.9 0.0 copy-done.1
  19.9 0.2 copy.18
  20.1 0.2 copy.19
  20.3 0.2 copy.21
  20.4 0.2 copy.20
  20.6 6.6 %stencil.2.res_ref = f32[16,8,4096]{2,1,0:T(8,128)} custom-call(bf16[16,8,4096]{2,1,0:T(8,128)(2,1)} %x_ref), custom_call_target="tpu_custom_call" | custom-call | flops 1073741824 | bytes 1048576 | tf_op jit(solution)/shard_map/stencil/pallas_call | solution.py:245
  27.3 0.0 copy-done.4
  27.3 0.0 copy-done.2
  27.3 0.0 copy-done.3
  27.3 0.0 copy-done
  27.3 2.2 %select_reduce_fusion = bf16[256,512]{1,0:T(8,128)(2,1)S(1)} fusion(f32[512,8]{0,1:T(8,128)S(1)} %get-tuple-element.33, f32[512,8]{0,1:T(8,128)S(1)} %get-tuple-element.34, f32[512,8]{0,1:T(8,128)S(1)} %get-tuple-element.32, f32[512,8]{0,1:T(8,128)S(1)} %copy-done, pred[256,8]{1,0:T(8,128)(4,1)S(1)} %copy.21, pred[256,8]{1,0:T(8,128)(4,1)S(1)} %copy.20, ...), kind=kLoop, calls=%fused_computation | loop fusion | flops 5111808 | bytes 335872 | tf_op jit(solution)/shard_map/reduce_prod | solution.py:41
  29.6 0.7 multiply_bitcast_fusion
  30.3 6.6 %stencil.3.tan_ref = f32[16,8,4096]{2,1,0:T(8,128)} custom-call(bf16[16,8,4096]{2,1,0:T(8,128)(2,1)} %x_ref.1), custom_call_target="tpu_custom_call" | custom-call | flops 1073741824 | bytes 1048576 | tf_op jit(solution)/shard_map/stencil/pallas_call | solution.py:245
  37.0 0.1 broadcast_in_dim.80.shift_ref
  37.1 0.7 collective-permute-start.1
  37.8 1.1 %copy.22.table_t_ref = bf16[512,256]{1,0:T(8,128)(2,1)S(1)} copy(bf16[512,256]{0,1:T(8,128)(2,1)} %multiply_bitcast_fusion) | data formatting | bytes 524288 | tf_op jit(solution)/shard_map/optimization_barrier | solution.py:435
  38.9 0.7 collective-permute-done.ends_ref
  39.7 1.7 %all-to-all-done.got_ref = bf16[32,8,32,128]{3,2,1,0:T(8,128)(2,1)S(1)} async-done(((bf16[32,8,32,128]{3,2,1,0:T(8,128)(2,1)}), bf16[32,8,32,128]{3,2,1,0:T(8,128)(2,1)S(1)}, u32[]{:S(2)}, u32[]{:S(2)}) %all-to-all-start) | async-done | bytes 2097184 | tf_op jit(solution)/shard_map/all_to_all | solution.py:422
  41.4 4.6 %quad_forces.1 = bf16[32,8,32,128]{3,2,1,0:T(8,128)(2,1)} custom-call(bf16[32,8,32,128]{3,2,1,0:T(8,128)(2,1)S(1)} %all-to-all-done.got_ref, bf16[512,256]{1,0:T(8,128)(2,1)S(1)} %copy.22.table_t_ref, bf16[256,512]{1,0:T(8,128)(2,1)S(1)} %multiply_convert_fusion.table_w_ref, f32[512,128]{1,0:T(8,128)S(1)} %broadcast_in_dim.80.shift_ref), custom_call_target="tpu_custom_call" | custom-call | flops 6442450944 | bytes 1024 | tf_op jit(solution)/shard_map/quad_forces/pallas_call | solution.py:198
  46.0 7.7 %all-to-all-start.1 = ((bf16[32,8,32,128]{3,2,1,0:T(8,128)(2,1)}), bf16[32,8,32,128]{3,2,1,0:T(8,128)(2,1)S(1)}, u32[]{:S(2)}, u32[]{:S(2)}) async-start(bf16[32,8,32,128]{3,2,1,0:T(8,128)(2,1)} %quad_forces.1), calls=%async_computation.1 | async-start | bytes 4194304 | tf_op jit(solution)/shard_map/all_to_all | solution.py:422
  53.7 0.0 collective-permute-done.1.outer_ref
  53.7 5.1 %add_outer.1 = (bf16[16,8,4096]{2,1,0:T(8,128)(2,1)}, bf16[16,8,4096]{2,1,0:T(8,128)(2,1)}) custom-call(s32[1]{0:T(128)} %bitcast.odd_ref, bf16[2,32,4096]{2,1,0:T(8,128)(2,1)S(1)} %collective-permute-done.1.outer_ref, bf16[32,128]{1,0:T(8,128)(2,1)S(1)} %collective-permute-done.ends_ref, f32[16,8,4096]{2,1,0:T(8,128)} %stencil.2.res_ref, ...), custom_call_target="tpu_custom_call" | custom-call | flops 21474836480 | bytes 7340032 | tf_op jit(solution)/shard_map/add_outer/pallas_call | solution.py:281
  58.8 23.0 %all-to-all-done.1.force_ref = bf16[32,8,32,128]{3,2,1,0:T(8,128)(2,1)S(1)} async-done(((bf16[32,8,32,128]{3,2,1,0:T(8,128)(2,1)}), bf16[32,8,32,128]{3,2,1,0:T(8,128)(2,1)S(1)}, u32[]{:S(2)}, u32[]{:S(2)}) %all-to-all-start.1) | async-done | bytes 2097184 | tf_op jit(solution)/shard_map/all_to_all | solution.py:422
  81.8 3.5 %merge.1 = (f32[16,8,4096]{2,1,0:T(8,128)}, f32[16,8,4096]{2,1,0:T(8,128)}) custom-call(bf16[32,8,32,128]{3,2,1,0:T(8,128)(2,1)S(1)} %all-to-all-done.1.force_ref, bf16[16,8,4096]{2,1,0:T(8,128)(2,1)} %get-tuple-element.30.res_ref, bf16[16,8,4096]{2,1,0:T(8,128)(2,1)} %get-tuple-element.31.tan_ref), custom_call_target="tpu_custom_call" | custom-call | flops 536870912 | bytes 10485760 | tf_op jit(solution)/shard_map/merge/pallas_call | solution.py:398
  (6 shorter events, 0.1 us)
Async XLA Ops:
  3.6 37.8 %all-to-all-start = ((bf16[32,8,32,128]{3,2,1,0:T(8,128)(2,1)}), bf16[32,8,32,128]{3,2,1,0:T(8,128)(2,1)S(1)}, u32[]{:S(2)}, u32[]{:S(2)}) async-start(bf16[32,8,32,128]{3,2,1,0:T(8,128)(2,1)} %pack.1), calls=%async_computation | async-start | bytes 4194304 | tf_op jit(solution)/shard_map/all_to_all | solution.py:422
  13.2 6.7 %copy-start.1 = (s32[256,8]{0,1:T(8,128)S(1)}, s32[256,8]{0,1:T(8,128)}, u32[]{:S(2)}) copy-start(s32[256,8]{0,1:T(8,128)} %param.13) | copy-start | bytes 24580
  16.9 10.3 %copy-start.4 = (f32[512]{0:T(512)S(1)}, f32[512]{0:T(512)}, u32[]{:S(2)}) copy-start(f32[512]{0:T(512)} %param.11) | copy-start | bytes 6148
  16.9 10.3 %copy-start.2 = (f32[512]{0:T(512)S(1)}, f32[512]{0:T(512)}, u32[]{:S(2)}) copy-start(f32[512]{0:T(512)} %param.10) | copy-start | bytes 6148
  16.9 10.3 %copy-start.3 = (f32[512]{0:T(512)S(1)}, f32[512]{0:T(512)}, u32[]{:S(2)}) copy-start(f32[512]{0:T(512)} %param.12) | copy-start | bytes 6148
  16.9 10.4 %copy-start = (f32[512,8]{0,1:T(8,128)S(1)}, f32[512,8]{0,1:T(8,128)}, u32[]{:S(2)}) copy-start(f32[512,8]{0,1:T(8,128)} %param.9) | copy-start | bytes 49156
  16.9 22.7 %collective-permute-start = (bf16[32,128]{1,0:T(8,128)(2,1)}, bf16[32,128]{1,0:T(8,128)(2,1)S(1)}, u32[]{:S(2)}, u32[]{:S(2)}) collective-permute-start(bf16[32,128]{1,0:T(8,128)(2,1)} %get-tuple-element.20), channel_id=1, source_target_pairs={{0,16},{16,0},{32,48},{48,32},{64,80},{80,64},{96,112},{112,96},{1... | collective-permute-start | bytes 24584 | tf_op jit(solution)/shard_map/ppermute | solution.py:428
  37.1 16.6 %collective-permute-start.1 = (bf16[2,32,4096]{2,1,0:T(8,128)(2,1)}, bf16[2,32,4096]{2,1,0:T(8,128)(2,1)S(1)}, u32[]{:S(2)}, u32[]{:S(2)}) collective-permute-start(bf16[2,32,4096]{2,1,0:T(8,128)(2,1)} %get-tuple-element.26), channel_id=1, source_target_pairs={{16,32},{32,16},{48,64},{64,48},{80,96},{96,80},{17,33},{33,17},{4... | collective-permute-start | bytes 1572872 | tf_op jit(solution)/shard_map/ppermute | solution.py:436
  46.0 35.9 %all-to-all-start.1 = ((bf16[32,8,32,128]{3,2,1,0:T(8,128)(2,1)}), bf16[32,8,32,128]{3,2,1,0:T(8,128)(2,1)S(1)}, u32[]{:S(2)}, u32[]{:S(2)}) async-start(bf16[32,8,32,128]{3,2,1,0:T(8,128)(2,1)} %quad_forces.1), calls=%async_computation.1 | async-start | bytes 4194304 | tf_op jit(solution)/shard_map/all_to_all | solution.py:422

commit v6 on v5

--- a/solution.py
+++ b/solution.py
@@ -430,7 +430,8 @@
     table = basis(quad_nodes, degrees)
     scale = quad_weights * pressure_load * (STEEP * STEEP)
     table_w = (table.astype(F32) * scale[None, :]).astype(BF16)
-    table_t = -STEEP * table.T
+    turn = one_hot(jnp.equal(*iotas((table.shape[0],) * 2))) * (-STEEP)
+    table_t = lax.dot_general(table, turn.astype(BF16), (((0,), (0,)), ((), ())), preferred_element_type=F32).astype(BF16)
     shift = jnp.broadcast_to((STEEP * (gap_nominal - FLOOR))[:, None], (gap_nominal.shape[0], 128))
     terms, res, tan, table_t, table_w, shift = lax.optimization_barrier((terms, res, tan, table_t, table_w, shift))
     outer = lax.ppermute(terms, "space", [(i + a, i + b) for i in range(1, bands - 1, 2) for a, b in ((0, 1), (1, 0))])

time: 85.9 us -> 84.3 us (0.981)
  waiting for transfers between devices: 25.5 us -> 27.1 us
  starting transfers between devices: 21 us -> 19.5 us
  local copies, waits for them, and re-layouts: 1.89 us -> 0.81 us
    ppermute x1, waiting for transfers between devices: 0.75 us -> 2.31 us  [shards(): ends = lax.ppermute(ends, 'space', [(i, i ^ 1) for i in range(bands)])]
    all_to_all x2, starting transfers between devices: 17.3 us -> 15.8 us  [exchange(): lax.all_to_all(x, ('space', 'mode'), split_axis=0, concat_axis=0, axis_in...]
    optimization_barrier x1 -> x0, local copies, waits for them, and re-layouts: 1.08 us -> none  [shards(): lax.optimization_barrier((terms, res, tan, table_t, table_w, shift))]
  transfers between devices with their start and end apart: 4 -> 4, of which waited for: 3 -> 3; matrix products, arithmetic and copies ran while one was open for 6% -> 4% of each run, Pallas kernels for 31% -> 32%
where the time goes in v6:
time: 84.3 us; the launch traced here: 83.8 us
  Pallas kernels  33.1 us (39%)
  waiting for transfers between devices  27.1 us (32%)
  starting transfers between devices  19.5 us (23%)
  other arithmetic  2.3 us (3%)
    all_to_all x2, waiting for transfers between devices, exchange(): lax.all_to_all(x, ('space', 'mode'), split_axis=0, concat_axis=0, axis_in...  24.8 us
    all_to_all x2, starting transfers between devices, exchange(): lax.all_to_all(x, ('space', 'mode'), split_axis=0, concat_axis=0, axis_in...  15.8 us
    pallas_call x2, Pallas kernels, stencil(): pl.pallas_call(functools.partial(stencil_kernel, 512), grid=(1,), in_spec...  13.3 us
    pallas_call x1, Pallas kernels, add_outer(): pl.pallas_call(functools.partial(outer_kernel, width // count, count), gr...  5.11 us
    pallas_call x1, Pallas kernels, quad_forces(): pl.pallas_call(functools.partial(quad_kernel, 128, deep), in_specs=[vmem]...  4.57 us
    pallas_call x1, Pallas kernels, edges(): pl.pallas_call(functools.partial(edges_kernel, width // count), grid=(1,)...  3.64 us
    pallas_call x1, Pallas kernels, merge(): pl.pallas_call(functools.partial(merge_kernel, groups, step), in_specs=[v...  3.48 us
    pallas_call x1, Pallas kernels, pack(): pl.pallas_call(functools.partial(pack_kernel, groups, early, step), in_sp...  2.99 us
  transfers between devices with their start and end apart: 4, of which 3 were waited for; matrix products, arithmetic and copies ran while one was open for 4% of the time, Pallas kernels for 32%

profile of v6, /device:TPU:1, one launch (start us, length us, event | category | flops | bytes accessed | tf_op | source)
XLA Modules:
  0.0 83.8 jit_solution(3801665291308973544)
XLA Ops:
  0.6 3.0 %pack.1 = bf16[32,8,32,128]{3,2,1,0:T(8,128)(2,1)} custom-call(bf16[16,8,4096]{2,1,0:T(8,128)(2,1)} %x_ref, bf16[16,8,4096]{2,1,0:T(8,128)(2,1)} %x_ref.1), custom_call_target="tpu_custom_call" | custom-call | flops 536870912 | bytes 4194304 | tf_op jit(solution)/shard_map/pack/pallas_call | solution.py:106
  3.6 9.6 %all-to-all-start = ((bf16[32,8,32,128]{3,2,1,0:T(8,128)(2,1)}), bf16[32,8,32,128]{3,2,1,0:T(8,128)(2,1)S(1)}, u32[]{:S(2)}, u32[]{:S(2)}) async-start(bf16[32,8,32,128]{3,2,1,0:T(8,128)(2,1)} %pack.1), calls=%async_computation | async-start | bytes 4194304 | tf_op jit(solution)/shard_map/all_to_all | solution.py:422
  13.2 0.0 copy-start.1
  13.3 3.6 %edges.1 = (bf16[2,32,4096]{2,1,0:T(8,128)(2,1)}, bf16[32,128]{1,0:T(8,128)(2,1)}) custom-call(s32[1]{0:T(128)} %bitcast.odd_ref, bf16[16,8,4096]{2,1,0:T(8,128)(2,1)} %x_ref, bf16[16,8,4096]{2,1,0:T(8,128)(2,1)} %x_ref.1), custom_call_target="tpu_custom_call" | custom-call | flops 1048576 | bytes 1048576 | tf_op jit(solution)/shard_map/edges/pallas_call | solution.py:337
  16.9 0.0 copy-start.4
  16.9 0.0 copy-start.2
  16.9 0.0 copy-start.3
  16.9 0.0 copy-start
  16.9 3.0 %collective-permute-start = (bf16[32,128]{1,0:T(8,128)(2,1)}, bf16[32,128]{1,0:T(8,128)(2,1)S(1)}, u32[]{:S(2)}, u32[]{:S(2)}) collective-permute-start(bf16[32,128]{1,0:T(8,128)(2,1)} %get-tuple-element.20), channel_id=1, source_target_pairs={{0,16},{16,0},{32,48},{48,32},{64,80},{80,64},{96,112},{112,96},{1... | collective-permute-start | bytes 24584 | tf_op jit(solution)/shard_map/ppermute | solution.py:428
  19.9 0.0 copy-done.1
  19.9 0.2 copy.17
  20.1 0.2 copy.18
  20.3 0.2 copy.20
  20.4 0.2 copy.19
  20.6 6.6 %stencil.2.res_ref = f32[16,8,4096]{2,1,0:T(8,128)} custom-call(bf16[16,8,4096]{2,1,0:T(8,128)(2,1)} %x_ref), custom_call_target="tpu_custom_call" | custom-call | flops 1073741824 | bytes 1048576 | tf_op jit(solution)/shard_map/stencil/pallas_call | solution.py:245
  27.2 0.0 copy-done.4
  27.3 0.0 copy-done.2
  27.3 0.0 copy-done.3
  27.3 0.0 copy-done
  27.3 2.2 %select_reduce_fusion = bf16[256,512]{1,0:T(8,128)(2,1)S(1)} fusion(f32[512,8]{0,1:T(8,128)S(1)} %get-tuple-element.33, f32[512,8]{0,1:T(8,128)S(1)} %get-tuple-element.34, f32[512,8]{0,1:T(8,128)S(1)} %get-tuple-element.32, f32[512,8]{0,1:T(8,128)S(1)} %copy-done, pred[256,8]{1,0:T(8,128)(4,1)S(1)} %copy.20, pred[256,8]{1,0:T(8,128)(4,1)S(1)} %copy.19, ...), kind=kLoop, calls=%fused_computation | loop fusion | flops 5111808 | bytes 335872 | tf_op jit(solution)/shard_map/reduce_prod | solution.py:41
  29.5 0.3 convolution_convert_fusion.table_t_ref
  29.9 6.6 %stencil.3.tan_ref = f32[16,8,4096]{2,1,0:T(8,128)} custom-call(bf16[16,8,4096]{2,1,0:T(8,128)(2,1)} %x_ref.1), custom_call_target="tpu_custom_call" | custom-call | flops 1073741824 | bytes 1048576 | tf_op jit(solution)/shard_map/stencil/pallas_call | solution.py:245
  36.5 0.1 broadcast_in_dim.90.shift_ref
  36.6 0.7 collective-permute-start.1
  37.3 2.3 %collective-permute-done.ends_ref = bf16[32,128]{1,0:T(8,128)(2,1)S(1)} collective-permute-done((bf16[32,128]{1,0:T(8,128)(2,1)}, bf16[32,128]{1,0:T(8,128)(2,1)S(1)}, u32[]{:S(2)}, u32[]{:S(2)}) %collective-permute-start) | collective-permute-done | bytes 8224 | tf_op jit(solution)/shard_map/ppermute | solution.py:428
  39.7 1.7 %all-to-all-done.got_ref = bf16[32,8,32,128]{3,2,1,0:T(8,128)(2,1)S(1)} async-done(((bf16[32,8,32,128]{3,2,1,0:T(8,128)(2,1)}), bf16[32,8,32,128]{3,2,1,0:T(8,128)(2,1)S(1)}, u32[]{:S(2)}, u32[]{:S(2)}) %all-to-all-start) | async-done | bytes 2097184 | tf_op jit(solution)/shard_map/all_to_all | solution.py:422
  41.4 4.6 %quad_forces.1 = bf16[32,8,32,128]{3,2,1,0:T(8,128)(2,1)} custom-call(bf16[32,8,32,128]{3,2,1,0:T(8,128)(2,1)S(1)} %all-to-all-done.got_ref, bf16[512,256]{1,0:T(8,128)(2,1)S(1)} %convolution_convert_fusion.table_t_ref, bf16[256,512]{1,0:T(8,128)(2,1)S(1)} %multiply_convert_fusion.table_w_ref, f32[512,128]{1,0:T(8,128)S(1)} %broadcast_in_dim.90.shift_ref), custom_call_target="tpu_custom_call" | custom-call | flops 6442450944 | bytes 1024 | tf_op jit(solution)/shard_map/quad_forces/pallas_call | solution.py:198
  46.0 6.2 %all-to-all-start.1 = ((bf16[32,8,32,128]{3,2,1,0:T(8,128)(2,1)}), bf16[32,8,32,128]{3,2,1,0:T(8,128)(2,1)S(1)}, u32[]{:S(2)}, u32[]{:S(2)}) async-start(bf16[32,8,32,128]{3,2,1,0:T(8,128)(2,1)} %quad_forces.1), calls=%async_computation.1 | async-start | bytes 4194304 | tf_op jit(solution)/shard_map/all_to_all | solution.py:422
  52.2 0.0 collective-permute-done.1.outer_ref
  52.2 5.1 %add_outer.1 = (bf16[16,8,4096]{2,1,0:T(8,128)(2,1)}, bf16[16,8,4096]{2,1,0:T(8,128)(2,1)}) custom-call(s32[1]{0:T(128)} %bitcast.odd_ref, bf16[2,32,4096]{2,1,0:T(8,128)(2,1)S(1)} %collective-permute-done.1.outer_ref, bf16[32,128]{1,0:T(8,128)(2,1)S(1)} %collective-permute-done.ends_ref, f32[16,8,4096]{2,1,0:T(8,128)} %stencil.2.res_ref, ...), custom_call_target="tpu_custom_call" | custom-call | flops 21474836480 | bytes 7340032 | tf_op jit(solution)/shard_map/add_outer/pallas_call | solution.py:281
  57.3 23.0 %all-to-all-done.1.force_ref = bf16[32,8,32,128]{3,2,1,0:T(8,128)(2,1)S(1)} async-done(((bf16[32,8,32,128]{3,2,1,0:T(8,128)(2,1)}), bf16[32,8,32,128]{3,2,1,0:T(8,128)(2,1)S(1)}, u32[]{:S(2)}, u32[]{:S(2)}) %all-to-all-start.1) | async-done | bytes 2097184 | tf_op jit(solution)/shard_map/all_to_all | solution.py:422
  80.3 3.5 %merge.1 = (f32[16,8,4096]{2,1,0:T(8,128)}, f32[16,8,4096]{2,1,0:T(8,128)}) custom-call(bf16[32,8,32,128]{3,2,1,0:T(8,128)(2,1)S(1)} %all-to-all-done.1.force_ref, bf16[16,8,4096]{2,1,0:T(8,128)(2,1)} %get-tuple-element.30.res_ref, bf16[16,8,4096]{2,1,0:T(8,128)(2,1)} %get-tuple-element.31.tan_ref), custom_call_target="tpu_custom_call" | custom-call | flops 536870912 | bytes 10485760 | tf_op jit(solution)/shard_map/merge/pallas_call | solution.py:398
  (5 shorter events, 0.1 us)
Async XLA Ops:
  3.6 37.8 %all-to-all-start = ((bf16[32,8,32,128]{3,2,1,0:T(8,128)(2,1)}), bf16[32,8,32,128]{3,2,1,0:T(8,128)(2,1)S(1)}, u32[]{:S(2)}, u32[]{:S(2)}) async-start(bf16[32,8,32,128]{3,2,1,0:T(8,128)(2,1)} %pack.1), calls=%async_computation | async-start | bytes 4194304 | tf_op jit(solution)/shard_map/all_to_all | solution.py:422
  13.2 6.7 %copy-start.1 = (s32[256,8]{0,1:T(8,128)S(1)}, s32[256,8]{0,1:T(8,128)}, u32[]{:S(2)}) copy-start(s32[256,8]{0,1:T(8,128)} %param.13) | copy-start | bytes 24580
  16.9 10.3 %copy-start.4 = (f32[512]{0:T(512)S(1)}, f32[512]{0:T(512)}, u32[]{:S(2)}) copy-start(f32[512]{0:T(512)} %param.11) | copy-start | bytes 6148
  16.9 10.3 %copy-start.2 = (f32[512]{0:T(512)S(1)}, f32[512]{0:T(512)}, u32[]{:S(2)}) copy-start(f32[512]{0:T(512)} %param.10) | copy-start | bytes 6148
  16.9 10.4 %copy-start.3 = (f32[512]{0:T(512)S(1)}, f32[512]{0:T(512)}, u32[]{:S(2)}) copy-start(f32[512]{0:T(512)} %param.12) | copy-start | bytes 6148
  16.9 10.4 %copy-start = (f32[512,8]{0,1:T(8,128)S(1)}, f32[512,8]{0,1:T(8,128)}, u32[]{:S(2)}) copy-start(f32[512,8]{0,1:T(8,128)} %param.9) | copy-start | bytes 49156
  16.9 22.7 %collective-permute-start = (bf16[32,128]{1,0:T(8,128)(2,1)}, bf16[32,128]{1,0:T(8,128)(2,1)S(1)}, u32[]{:S(2)}, u32[]{:S(2)}) collective-permute-start(bf16[32,128]{1,0:T(8,128)(2,1)} %get-tuple-element.20), channel_id=1, source_target_pairs={{0,16},{16,0},{32,48},{48,32},{64,80},{80,64},{96,112},{112,96},{1... | collective-permute-start | bytes 24584 | tf_op jit(solution)/shard_map/ppermute | solution.py:428
  36.6 15.5 %collective-permute-start.1 = (bf16[2,32,4096]{2,1,0:T(8,128)(2,1)}, bf16[2,32,4096]{2,1,0:T(8,128)(2,1)S(1)}, u32[]{:S(2)}, u32[]{:S(2)}) collective-permute-start(bf16[2,32,4096]{2,1,0:T(8,128)(2,1)} %get-tuple-element.26), channel_id=1, source_target_pairs={{16,32},{32,16},{48,64},{64,48},{80,96},{96,80},{17,33},{33,17},{4... | collective-permute-start | bytes 1572872 | tf_op jit(solution)/shard_map/ppermute | solution.py:437
  46.0 34.3 %all-to-all-start.1 = ((bf16[32,8,32,128]{3,2,1,0:T(8,128)(2,1)}), bf16[32,8,32,128]{3,2,1,0:T(8,128)(2,1)S(1)}, u32[]{:S(2)}, u32[]{:S(2)}) async-start(bf16[32,8,32,128]{3,2,1,0:T(8,128)(2,1)} %quad_forces.1), calls=%async_computation.1 | async-start | bytes 4194304 | tf_op jit(solution)/shard_map/all_to_all | solution.py:422

commit v7 on v6

--- a/solution.py
+++ b/solution.py
@@ -212,7 +212,7 @@
     )(got, table_t, table_w, shift)
 
 
-def stencil_kernel(chunk, x_ref, out_ref, side_ref):
+def stencil_kernel(chunk, x_ref, out_ref, inner_ref, side_ref):
     modes, rows, width = x_ref.shape
     size = modes * rows
     to, frm = iotas((size, size))
@@ -225,7 +225,7 @@
     for c in range(width // chunk):
         cols = pl.ds(c * chunk, chunk)
         x = x_ref[:, :, cols].reshape(size, chunk)
-        out_ref[:, :, cols] = jnp.dot(centre, x, preferred_element_type=F32).reshape(modes, rows, chunk)
+        inner_ref[:, :, cols] = jnp.dot(centre, x, preferred_element_type=F32).reshape(modes, rows, chunk)
         side_ref[:, :, cols] = jnp.dot(side, x, preferred_element_type=F32).reshape(modes, rows, chunk)
     lane = lax.broadcasted_iota(jnp.int32, (rows, width), 1)
 
@@ -234,7 +234,7 @@
         y = side_ref[m]
         right = shifted(y + shifted(x, lane, 1), lane, 1)
         left = shifted(y + shifted(x, lane, -1), lane, -1)
-        out_ref[m] = STIFF * (out_ref[m] + right + left)
+        out_ref[m] = (STIFF * (inner_ref[m] + right + left)).astype(BF16)
         return 0
 
     lax.fori_loop(0, modes, one_mode, 0)
@@ -247,8 +247,8 @@
         grid=(1,),
         in_specs=[whole],
         out_specs=whole,
-        out_shape=pltpu.HBM(x.shape, F32),
-        scratch_shapes=[pltpu.VMEM(x.shape, F32)],
+        out_shape=pltpu.HBM(x.shape, BF16),
+        scratch_shapes=[pltpu.VMEM(x.shape, F32)] * 2,
         compiler_params=pltpu.CompilerParams(vmem_limit_bytes=VMEM),
         cost_estimate=pl.CostEstimate(flops=1 << 30, bytes_accessed=1 << 20, transcendentals=0),
         name="stencil",
@@ -272,7 +272,7 @@
         terms = jnp.dot(place, terms, preferred_element_type=F32)
         corners = jnp.dot(corner, spread[f * modes : (f + 1) * modes], preferred_element_type=F32)
         terms = (terms + (2.0 * STIFF) * corners).reshape(modes, rows, chunk)
-        out[...] = (ref[...] + terms).astype(BF16)
+        out[...] = (ref[...].astype(F32) + terms).astype(BF16)
 
 
 def add_outer(odd, outer, ends, res, tan, count, steps=4):
@@ -349,22 +349,22 @@
     )(odd, in_hbm(displacement), in_hbm(direction))
 
 
-def merge_kernel(groups, step, force_ref, res_ref, tan_ref, res_out, tan_out, in_buf, buf, in_sem, out_sem):
+def merge_kernel(cuts, step, force_ref, res_ref, tan_ref, res_out, tan_out, in_buf, buf, in_sem, out_sem):
     count, rows, both, each = force_ref.shape
     modes = both // 2
     size = both * rows
-    per = count // groups
-    span = per * each
+    groups = len(cuts) - 1
+    span = step * each
 
     def loads(g):
-        cols = pl.ds(g * span, span)
+        cols = pl.ds(cuts[g] * span, (cuts[g + 1] - cuts[g]) * span)
         return [
             pltpu.make_async_copy(ref.at[:, :, cols], in_buf.at[f, :, :, cols], in_sem.at[f, g])
             for f, ref in enumerate((res_ref, tan_ref))
         ]
 
     def stores(g):
-        cols = pl.ds(g * span, span)
+        cols = pl.ds(cuts[g] * span, (cuts[g + 1] - cuts[g]) * span)
         return [
             pltpu.make_async_copy(buf.at[f, :, :, cols], ref.at[:, :, cols], out_sem.at[f, g])
             for f, ref in enumerate((res_out, tan_out))
@@ -376,14 +376,20 @@
     to, frm = iotas((size, size))
     hit = (to % rows == frm // both) & (to // rows == frm % both)
     moves = jnp.where(hit, jnp.where(to // rows < modes, -1.0, 2.0), 0.0).astype(BF16)
+    def moved(t):
+        force = [force_ref[t * step + k].reshape(size, each) for k in range(step)]
+        terms = jnp.dot(moves, jnp.concatenate(force, axis=1), preferred_element_type=F32)
+        return terms.reshape(2, modes, rows, span)
+
+    for t in range(cuts[1]):
+        buf[:, :, :, pl.ds(t * span, span)] = moved(t)
     for g in range(groups):
         for copy in loads(g):
             copy.wait()
-        for d in range(g * per, (g + 1) * per, step):
-            cols = pl.ds(d * each, step * each)
-            force = jnp.concatenate([force_ref[d + k].reshape(size, each) for k in range(step)], axis=1)
-            moved = jnp.dot(moves, force, preferred_element_type=F32).reshape(2, modes, rows, step * each)
-            buf[:, :, :, cols] = in_buf[:, :, :, cols].astype(F32) + moved
+        for t in range(cuts[g], cuts[g + 1]):
+            cols = pl.ds(t * span, span)
+            terms = buf[:, :, :, cols] if g == 0 else moved(t)
+            buf[:, :, :, cols] = in_buf[:, :, :, cols].astype(F32) + terms
         for copy in stores(g):
             copy.start()
     for g in range(groups):
@@ -391,20 +397,20 @@
             copy.wait()
 
 
-def merge(force, res, tan, groups=4, step=2):
+def merge(force, res, tan, cuts=(0, 4, 8, 12, 16), step=2):
     count, rows, both, each = force.shape
     vmem = pl.BlockSpec(memory_space=pltpu.VMEM)
     hbm = pl.BlockSpec(memory_space=HBM)
     return pl.pallas_call(
-        functools.partial(merge_kernel, groups, step),
+        functools.partial(merge_kernel, cuts, step),
         in_specs=[vmem, hbm, hbm],
         out_specs=[hbm] * 2,
         out_shape=[pltpu.HBM(res.shape, F32)] * 2,
         scratch_shapes=[
             pltpu.VMEM((2,) + res.shape, BF16),
             pltpu.VMEM((2,) + res.shape, F32),
-            pltpu.SemaphoreType.DMA((2, groups)),
-            pltpu.SemaphoreType.DMA((2, groups)),
+            pltpu.SemaphoreType.DMA((2, len(cuts) - 1)),
+            pltpu.SemaphoreType.DMA((2, len(cuts) - 1)),
         ],
         compiler_params=pltpu.CompilerParams(vmem_limit_bytes=VMEM),
         cost_estimate=pl.CostEstimate(flops=2 * (both * rows) ** 2 * each * count, bytes_accessed=10 * MIB, transcendentals=0),

time: 84.3 us -> 83.4 us (0.989)
  Pallas kernels: 33.1 us -> 31.8 us
  waiting for transfers between devices: 27.1 us -> 28.1 us
  transfers between devices with their start and end apart: 4 -> 4, of which waited for: 3 -> 3; matrix products, arithmetic and copies ran while one was open for 4% -> 4% of each run, Pallas kernels for 32% -> 31%
where the time goes in v7:
time: 83.4 us; the launch traced here: 82.9 us
  Pallas kernels  31.8 us (38%)
  waiting for transfers between devices  28.1 us (34%)
  starting transfers between devices  18.8 us (23%)
  other arithmetic  2.3 us (3%)
    all_to_all x2, waiting for transfers between devices, exchange(): lax.all_to_all(x, ('space', 'mode'), split_axis=0, concat_axis=0, axis_in...  25.1 us
    all_to_all x2, starting transfers between devices, exchange(): lax.all_to_all(x, ('space', 'mode'), split_axis=0, concat_axis=0, axis_in...  15.1 us
    pallas_call x2, Pallas kernels, stencil(): pl.pallas_call(functools.partial(stencil_kernel, 512), grid=(1,), in_spec...  12.6 us
    pallas_call x1, Pallas kernels, add_outer(): pl.pallas_call(functools.partial(outer_kernel, width // count, count), gr...  4.74 us
    pallas_call x1, Pallas kernels, quad_forces(): pl.pallas_call(functools.partial(quad_kernel, 128, deep), in_specs=[vmem]...  4.57 us
    pallas_call x1, Pallas kernels, edges(): pl.pallas_call(functools.partial(edges_kernel, width // count), grid=(1,)...  3.64 us
    pallas_call x1, Pallas kernels, merge(): pl.pallas_call(functools.partial(merge_kernel, cuts, step), in_specs=[vme...  3.31 us
    ppermute x1, waiting for transfers between devices, shards(): ends = lax.ppermute(ends, 'space', [(i, i ^ 1) for i in range(bands)])  3.01 us
  transfers between devices with their start and end apart: 4, of which 3 were waited for; matrix products, arithmetic and copies ran while one was open for 4% of the time, Pallas kernels for 31%

profile of v7, /device:TPU:1, one launch (start us, length us, event | category | flops | bytes accessed | tf_op | source)
XLA Modules:
  0.0 82.9 jit_solution(13419402103682391245)
XLA Ops:
  0.6 3.0 %pack.1 = bf16[32,8,32,128]{3,2,1,0:T(8,128)(2,1)} custom-call(bf16[16,8,4096]{2,1,0:T(8,128)(2,1)} %x_ref, bf16[16,8,4096]{2,1,0:T(8,128)(2,1)} %x_ref.1), custom_call_target="tpu_custom_call" | custom-call | flops 536870912 | bytes 4194304 | tf_op jit(solution)/shard_map/pack/pallas_call | solution.py:106
  3.6 9.6 %all-to-all-start = ((bf16[32,8,32,128]{3,2,1,0:T(8,128)(2,1)}), bf16[32,8,32,128]{3,2,1,0:T(8,128)(2,1)S(1)}, u32[]{:S(2)}, u32[]{:S(2)}) async-start(bf16[32,8,32,128]{3,2,1,0:T(8,128)(2,1)} %pack.1), calls=%async_computation | async-start | bytes 4194304 | tf_op jit(solution)/shard_map/all_to_all | solution.py:428
  13.2 0.0 copy-start.1
  13.3 3.6 %edges.1 = (bf16[2,32,4096]{2,1,0:T(8,128)(2,1)}, bf16[32,128]{1,0:T(8,128)(2,1)}) custom-call(s32[1]{0:T(128)} %bitcast.odd_ref, bf16[16,8,4096]{2,1,0:T(8,128)(2,1)} %x_ref, bf16[16,8,4096]{2,1,0:T(8,128)(2,1)} %x_ref.1), custom_call_target="tpu_custom_call" | custom-call | flops 1048576 | bytes 1048576 | tf_op jit(solution)/shard_map/edges/pallas_call | solution.py:337
  16.9 0.0 copy-start.4
  16.9 0.0 copy-start.2
  16.9 0.0 copy-start.3
  16.9 0.0 copy-start
  16.9 3.0 %collective-permute-start = (bf16[32,128]{1,0:T(8,128)(2,1)}, bf16[32,128]{1,0:T(8,128)(2,1)S(1)}, u32[]{:S(2)}, u32[]{:S(2)}) collective-permute-start(bf16[32,128]{1,0:T(8,128)(2,1)} %get-tuple-element.20), channel_id=1, source_target_pairs={{0,16},{16,0},{32,48},{48,32},{64,80},{80,64},{96,112},{112,96},{1... | collective-permute-start | bytes 24584 | tf_op jit(solution)/shard_map/ppermute | solution.py:434
  19.9 0.0 copy-done.1
  19.9 0.2 copy.17
  20.1 0.2 copy.18
  20.3 0.2 copy.20
  20.4 0.2 copy.19
  20.6 6.3 %stencil.2.res_ref = bf16[16,8,4096]{2,1,0:T(8,128)(2,1)} custom-call(bf16[16,8,4096]{2,1,0:T(8,128)(2,1)} %x_ref), custom_call_target="tpu_custom_call" | custom-call | flops 1073741824 | bytes 1048576 | tf_op jit(solution)/shard_map/stencil/pallas_call | solution.py:245
  26.9 0.0 copy-done.4
  26.9 0.0 copy-done.2
  26.9 0.0 copy-done.3
  26.9 0.0 copy-done
  27.0 2.2 %select_reduce_fusion = bf16[256,512]{1,0:T(8,128)(2,1)S(1)} fusion(f32[512,8]{0,1:T(8,128)S(1)} %get-tuple-element.33, f32[512,8]{0,1:T(8,128)S(1)} %get-tuple-element.34, f32[512,8]{0,1:T(8,128)S(1)} %get-tuple-element.32, f32[512,8]{0,1:T(8,128)S(1)} %copy-done, pred[256,8]{1,0:T(8,128)(4,1)S(1)} %copy.20, pred[256,8]{1,0:T(8,128)(4,1)S(1)} %copy.19, ...), kind=kLoop, calls=%fused_computation | loop fusion | flops 5111808 | bytes 335872 | tf_op jit(solution)/shard_map/reduce_prod | solution.py:41
  29.2 0.3 convolution_convert_fusion.table_t_ref
  29.5 6.3 %stencil.3.tan_ref = bf16[16,8,4096]{2,1,0:T(8,128)(2,1)} custom-call(bf16[16,8,4096]{2,1,0:T(8,128)(2,1)} %x_ref.1), custom_call_target="tpu_custom_call" | custom-call | flops 1073741824 | bytes 1048576 | tf_op jit(solution)/shard_map/stencil/pallas_call | solution.py:245
  35.8 0.1 broadcast_in_dim.90.shift_ref
  35.9 0.7 collective-permute-start.1
  36.6 3.0 %collective-permute-done.ends_ref = bf16[32,128]{1,0:T(8,128)(2,1)S(1)} collective-permute-done((bf16[32,128]{1,0:T(8,128)(2,1)}, bf16[32,128]{1,0:T(8,128)(2,1)S(1)}, u32[]{:S(2)}, u32[]{:S(2)}) %collective-permute-start) | collective-permute-done | bytes 8224 | tf_op jit(solution)/shard_map/ppermute | solution.py:434
  39.7 1.7 %all-to-all-done.got_ref = bf16[32,8,32,128]{3,2,1,0:T(8,128)(2,1)S(1)} async-done(((bf16[32,8,32,128]{3,2,1,0:T(8,128)(2,1)}), bf16[32,8,32,128]{3,2,1,0:T(8,128)(2,1)S(1)}, u32[]{:S(2)}, u32[]{:S(2)}) %all-to-all-start) | async-done | bytes 2097184 | tf_op jit(solution)/shard_map/all_to_all | solution.py:428
  41.4 4.6 %quad_forces.1 = bf16[32,8,32,128]{3,2,1,0:T(8,128)(2,1)} custom-call(bf16[32,8,32,128]{3,2,1,0:T(8,128)(2,1)S(1)} %all-to-all-done.got_ref, bf16[512,256]{1,0:T(8,128)(2,1)S(1)} %convolution_convert_fusion.table_t_ref, bf16[256,512]{1,0:T(8,128)(2,1)S(1)} %multiply_convert_fusion.table_w_ref, f32[512,128]{1,0:T(8,128)S(1)} %broadcast_in_dim.90.shift_ref), custom_call_target="tpu_custom_call" | custom-call | flops 6442450944 | bytes 1024 | tf_op jit(solution)/shard_map/quad_forces/pallas_call | solution.py:198
  46.0 5.5 %all-to-all-start.1 = ((bf16[32,8,32,128]{3,2,1,0:T(8,128)(2,1)}), bf16[32,8,32,128]{3,2,1,0:T(8,128)(2,1)S(1)}, u32[]{:S(2)}, u32[]{:S(2)}) async-start(bf16[32,8,32,128]{3,2,1,0:T(8,128)(2,1)} %quad_forces.1), calls=%async_computation.1 | async-start | bytes 4194304 | tf_op jit(solution)/shard_map/all_to_all | solution.py:428
  51.4 0.0 collective-permute-done.1.outer_ref
  51.5 4.7 %add_outer.1 = (bf16[16,8,4096]{2,1,0:T(8,128)(2,1)}, bf16[16,8,4096]{2,1,0:T(8,128)(2,1)}) custom-call(s32[1]{0:T(128)} %bitcast.odd_ref, bf16[2,32,4096]{2,1,0:T(8,128)(2,1)S(1)} %collective-permute-done.1.outer_ref, bf16[32,128]{1,0:T(8,128)(2,1)S(1)} %collective-permute-done.ends_ref, bf16[16,8,4096]{2,1,0:T(8,128)(2,1)} %stencil.2.res_ref, ...), custom_call_target="tpu_custom_call" | custom-call | flops 21474836480 | bytes 7340032 | tf_op jit(solution)/shard_map/add_outer/pallas_call | solution.py:281
  56.2 23.4 %all-to-all-done.1.force_ref = bf16[32,8,32,128]{3,2,1,0:T(8,128)(2,1)S(1)} async-done(((bf16[32,8,32,128]{3,2,1,0:T(8,128)(2,1)}), bf16[32,8,32,128]{3,2,1,0:T(8,128)(2,1)S(1)}, u32[]{:S(2)}, u32[]{:S(2)}) %all-to-all-start.1) | async-done | bytes 2097184 | tf_op jit(solution)/shard_map/all_to_all | solution.py:428
  79.6 3.3 %merge.1 = (f32[16,8,4096]{2,1,0:T(8,128)}, f32[16,8,4096]{2,1,0:T(8,128)}) custom-call(bf16[32,8,32,128]{3,2,1,0:T(8,128)(2,1)S(1)} %all-to-all-done.1.force_ref, bf16[16,8,4096]{2,1,0:T(8,128)(2,1)} %get-tuple-element.30.res_ref, bf16[16,8,4096]{2,1,0:T(8,128)(2,1)} %get-tuple-element.31.tan_ref), custom_call_target="tpu_custom_call" | custom-call | flops 536870912 | bytes 10485760 | tf_op jit(solution)/shard_map/merge/pallas_call | solution.py:404
  (5 shorter events, 0.1 us)
Async XLA Ops:
  3.6 37.8 %all-to-all-start = ((bf16[32,8,32,128]{3,2,1,0:T(8,128)(2,1)}), bf16[32,8,32,128]{3,2,1,0:T(8,128)(2,1)S(1)}, u32[]{:S(2)}, u32[]{:S(2)}) async-start(bf16[32,8,32,128]{3,2,1,0:T(8,128)(2,1)} %pack.1), calls=%async_computation | async-start | bytes 4194304 | tf_op jit(solution)/shard_map/all_to_all | solution.py:428
  13.2 6.7 %copy-start.1 = (s32[256,8]{0,1:T(8,128)S(1)}, s32[256,8]{0,1:T(8,128)}, u32[]{:S(2)}) copy-start(s32[256,8]{0,1:T(8,128)} %param.13) | copy-start | bytes 24580
  16.9 10.0 %copy-start.4 = (f32[512]{0:T(512)S(1)}, f32[512]{0:T(512)}, u32[]{:S(2)}) copy-start(f32[512]{0:T(512)} %param.11) | copy-start | bytes 6148
  16.9 10.0 %copy-start.2 = (f32[512]{0:T(512)S(1)}, f32[512]{0:T(512)}, u32[]{:S(2)}) copy-start(f32[512]{0:T(512)} %param.10) | copy-start | bytes 6148
  16.9 10.0 %copy-start.3 = (f32[512]{0:T(512)S(1)}, f32[512]{0:T(512)}, u32[]{:S(2)}) copy-start(f32[512]{0:T(512)} %param.12) | copy-start | bytes 6148
  16.9 10.0 %copy-start = (f32[512,8]{0,1:T(8,128)S(1)}, f32[512,8]{0,1:T(8,128)}, u32[]{:S(2)}) copy-start(f32[512,8]{0,1:T(8,128)} %param.9) | copy-start | bytes 49156
  16.9 22.7 %collective-permute-start = (bf16[32,128]{1,0:T(8,128)(2,1)}, bf16[32,128]{1,0:T(8,128)(2,1)S(1)}, u32[]{:S(2)}, u32[]{:S(2)}) collective-permute-start(bf16[32,128]{1,0:T(8,128)(2,1)} %get-tuple-element.20), channel_id=1, source_target_pairs={{0,16},{16,0},{32,48},{48,32},{64,80},{80,64},{96,112},{112,96},{1... | collective-permute-start | bytes 24584 | tf_op jit(solution)/shard_map/ppermute | solution.py:434
  35.9 15.5 %collective-permute-start.1 = (bf16[2,32,4096]{2,1,0:T(8,128)(2,1)}, bf16[2,32,4096]{2,1,0:T(8,128)(2,1)S(1)}, u32[]{:S(2)}, u32[]{:S(2)}) collective-permute-start(bf16[2,32,4096]{2,1,0:T(8,128)(2,1)} %get-tuple-element.26), channel_id=1, source_target_pairs={{16,32},{32,16},{48,64},{64,48},{80,96},{96,80},{17,33},{33,17},{4... | collective-permute-start | bytes 1572872 | tf_op jit(solution)/shard_map/ppermute | solution.py:443
  46.0 33.6 %all-to-all-start.1 = ((bf16[32,8,32,128]{3,2,1,0:T(8,128)(2,1)}), bf16[32,8,32,128]{3,2,1,0:T(8,128)(2,1)S(1)}, u32[]{:S(2)}, u32[]{:S(2)}) async-start(bf16[32,8,32,128]{3,2,1,0:T(8,128)(2,1)} %quad_forces.1), calls=%async_computation.1 | async-start | bytes 4194304 | tf_op jit(solution)/shard_map/all_to_all | solution.py:428

commit v8 on v7

--- a/solution.py
+++ b/solution.py
@@ -149,7 +149,7 @@
         value = jnp.where(far == 0, jnp.where(near, jnp.where(full, -8.0, 1.0), jnp.where(full, 1.0, 0.0)), 0.0)
         cross_ref[band] = jnp.where((jnp.abs(far) == 1) & near & full, 2.0, value).astype(BF16)
 
-    def forward(i):
+    def forward(i, slots):
         slot = i % 2
         disp = field_rows(i, 0)
         dire = field_rows(i, 1)
@@ -168,25 +168,29 @@
             square = inv * inv
             w_ref[slot, 0, at, :] = square.astype(BF16)
             w_ref[slot, 1, at, :] = ((sig * inv) * (square * probe)).astype(BF16)
-
-    def back(i):
+            if i > 0 and q in slots:
+                back(i - 1, slots[q])
+
+    def back(i, f):
         band, pair = i // pairs, i % pairs
-        for f, factor in enumerate((-STIFF, 0.5 * STIFF)):
-            force = jnp.dot(table_w_ref[...], w_ref[i % 2, f], preferred_element_type=F32)
-            if i in (pairs - 1, pairs):
-                facing = field_rows(steps - 1 - i, f)
-                force = force + factor * jnp.dot(facing, cross_ref[band], preferred_element_type=F32)
-            force = force.astype(BF16)
-            for k in range(deep):
-                part = force[:, k * each : (k + 1) * each].reshape(per, modes, each)
-                out_buf[band * per : (band + 1) * per, pair * deep + k, f * modes : (f + 1) * modes, :] = part
-        store(i).start()
-
-    for i in range(steps + 1):
-        if i < steps:
-            forward(i)
+        factor = (-STIFF, 0.5 * STIFF)[f]
+        force = jnp.dot(table_w_ref[...], w_ref[i % 2, f], preferred_element_type=F32)
+        if i in (pairs - 1, pairs):
+            facing = field_rows(steps - 1 - i, f)
+            force = force + factor * jnp.dot(facing, cross_ref[band], preferred_element_type=F32)
+        force = force.astype(BF16)
+        for k in range(deep):
+            part = force[:, k * each : (k + 1) * each].reshape(per, modes, each)
+            out_buf[band * per : (band + 1) * per, pair * deep + k, f * modes : (f + 1) * modes, :] = part
+
+    slots = {quad // chunk // 2 - 1: 0, quad // chunk - 1: 1}
+    for i in range(steps):
+        forward(i, slots)
         if i > 0:
-            back(i - 1)
+            store(i - 1).start()
+    for f in range(2):
+        back(steps - 1, f)
+    store(steps - 1).start()
     for i in range(steps):
         store(i).wait()
 

time: 83.4 us -> 83.2 us (level)
  no operation moved by 1% of the time
where the time goes in v8:
time: 83.2 us; the launch traced here: 82.7 us
  Pallas kernels  31.6 us (38%)
  waiting for transfers between devices  28.1 us (34%)
  starting transfers between devices  18.8 us (23%)
  other arithmetic  2.3 us (3%)
    all_to_all x2, waiting for transfers between devices, exchange(): lax.all_to_all(x, ('space', 'mode'), split_axis=0, concat_axis=0, axis_in...  25.1 us
    all_to_all x2, starting transfers between devices, exchange(): lax.all_to_all(x, ('space', 'mode'), split_axis=0, concat_axis=0, axis_in...  15.1 us
    pallas_call x2, Pallas kernels, stencil(): pl.pallas_call(functools.partial(stencil_kernel, 512), grid=(1,), in_spec...  12.6 us
    pallas_call x1, Pallas kernels, add_outer(): pl.pallas_call(functools.partial(outer_kernel, width // count, count), gr...  4.75 us
    pallas_call x1, Pallas kernels, quad_forces(): pl.pallas_call(functools.partial(quad_kernel, 128, deep), in_specs=[vmem]...  4.36 us
    pallas_call x1, Pallas kernels, edges(): pl.pallas_call(functools.partial(edges_kernel, width // count), grid=(1,)...  3.64 us
    pallas_call x1, Pallas kernels, merge(): pl.pallas_call(functools.partial(merge_kernel, cuts, step), in_specs=[vme...  3.31 us
    ppermute x1, waiting for transfers between devices, shards(): ends = lax.ppermute(ends, 'space', [(i, i ^ 1) for i in range(bands)])  3.01 us
  transfers between devices with their start and end apart: 4, of which 3 were waited for; matrix products, arithmetic and copies ran while one was open for 4% of the time, Pallas kernels for 31%

profile of v8, /device:TPU:1, one launch (start us, length us, event | category | flops | bytes accessed | tf_op | source)
XLA Modules:
  0.0 82.7 jit_solution(4851715517341588307)
XLA Ops:
  0.6 3.0 %pack.1 = bf16[32,8,32,128]{3,2,1,0:T(8,128)(2,1)} custom-call(bf16[16,8,4096]{2,1,0:T(8,128)(2,1)} %x_ref, bf16[16,8,4096]{2,1,0:T(8,128)(2,1)} %x_ref.1), custom_call_target="tpu_custom_call" | custom-call | flops 536870912 | bytes 4194304 | tf_op jit(solution)/shard_map/pack/pallas_call | solution.py:106
  3.6 9.6 %all-to-all-start = ((bf16[32,8,32,128]{3,2,1,0:T(8,128)(2,1)}), bf16[32,8,32,128]{3,2,1,0:T(8,128)(2,1)S(1)}, u32[]{:S(2)}, u32[]{:S(2)}) async-start(bf16[32,8,32,128]{3,2,1,0:T(8,128)(2,1)} %pack.1), calls=%async_computation | async-start | bytes 4194304 | tf_op jit(solution)/shard_map/all_to_all | solution.py:432
  13.2 0.0 copy-start.1
  13.3 3.6 %edges.1 = (bf16[2,32,4096]{2,1,0:T(8,128)(2,1)}, bf16[32,128]{1,0:T(8,128)(2,1)}) custom-call(s32[1]{0:T(128)} %bitcast.odd_ref, bf16[16,8,4096]{2,1,0:T(8,128)(2,1)} %x_ref, bf16[16,8,4096]{2,1,0:T(8,128)(2,1)} %x_ref.1), custom_call_target="tpu_custom_call" | custom-call | flops 1048576 | bytes 1048576 | tf_op jit(solution)/shard_map/edges/pallas_call | solution.py:341
  16.9 0.0 copy-start.4
  16.9 0.0 copy-start.2
  16.9 0.0 copy-start.3
  16.9 0.0 copy-start
  16.9 3.0 %collective-permute-start = (bf16[32,128]{1,0:T(8,128)(2,1)}, bf16[32,128]{1,0:T(8,128)(2,1)S(1)}, u32[]{:S(2)}, u32[]{:S(2)}) collective-permute-start(bf16[32,128]{1,0:T(8,128)(2,1)} %get-tuple-element.20), channel_id=1, source_target_pairs={{0,16},{16,0},{32,48},{48,32},{64,80},{80,64},{96,112},{112,96},{1... | collective-permute-start | bytes 24584 | tf_op jit(solution)/shard_map/ppermute | solution.py:438
  19.9 0.0 copy-done.1
  19.9 0.2 copy.17
  20.1 0.2 copy.18
  20.3 0.2 copy.20
  20.4 0.2 copy.19
  20.6 6.3 %stencil.2.res_ref = bf16[16,8,4096]{2,1,0:T(8,128)(2,1)} custom-call(bf16[16,8,4096]{2,1,0:T(8,128)(2,1)} %x_ref), custom_call_target="tpu_custom_call" | custom-call | flops 1073741824 | bytes 1048576 | tf_op jit(solution)/shard_map/stencil/pallas_call | solution.py:249
  26.9 0.0 copy-done.4
  26.9 0.0 copy-done.2
  26.9 0.0 copy-done.3
  26.9 0.0 copy-done
  27.0 2.2 %select_reduce_fusion = bf16[256,512]{1,0:T(8,128)(2,1)S(1)} fusion(f32[512,8]{0,1:T(8,128)S(1)} %get-tuple-element.33, f32[512,8]{0,1:T(8,128)S(1)} %get-tuple-element.34, f32[512,8]{0,1:T(8,128)S(1)} %get-tuple-element.32, f32[512,8]{0,1:T(8,128)S(1)} %copy-done, pred[256,8]{1,0:T(8,128)(4,1)S(1)} %copy.20, pred[256,8]{1,0:T(8,128)(4,1)S(1)} %copy.19, ...), kind=kLoop, calls=%fused_computation | loop fusion | flops 5111808 | bytes 335872 | tf_op jit(solution)/shard_map/reduce_prod | solution.py:41
  29.2 0.3 convolution_convert_fusion.table_t_ref
  29.5 6.3 %stencil.3.tan_ref = bf16[16,8,4096]{2,1,0:T(8,128)(2,1)} custom-call(bf16[16,8,4096]{2,1,0:T(8,128)(2,1)} %x_ref.1), custom_call_target="tpu_custom_call" | custom-call | flops 1073741824 | bytes 1048576 | tf_op jit(solution)/shard_map/stencil/pallas_call | solution.py:249
  35.8 0.1 broadcast_in_dim.90.shift_ref
  35.9 0.7 collective-permute-start.1
  36.6 3.0 %collective-permute-done.ends_ref = bf16[32,128]{1,0:T(8,128)(2,1)S(1)} collective-permute-done((bf16[32,128]{1,0:T(8,128)(2,1)}, bf16[32,128]{1,0:T(8,128)(2,1)S(1)}, u32[]{:S(2)}, u32[]{:S(2)}) %collective-permute-start) | collective-permute-done | bytes 8224 | tf_op jit(solution)/shard_map/ppermute | solution.py:438
  39.7 1.7 %all-to-all-done.got_ref = bf16[32,8,32,128]{3,2,1,0:T(8,128)(2,1)S(1)} async-done(((bf16[32,8,32,128]{3,2,1,0:T(8,128)(2,1)}), bf16[32,8,32,128]{3,2,1,0:T(8,128)(2,1)S(1)}, u32[]{:S(2)}, u32[]{:S(2)}) %all-to-all-start) | async-done | bytes 2097184 | tf_op jit(solution)/shard_map/all_to_all | solution.py:432
  41.4 4.4 %quad_forces.1 = bf16[32,8,32,128]{3,2,1,0:T(8,128)(2,1)} custom-call(bf16[32,8,32,128]{3,2,1,0:T(8,128)(2,1)S(1)} %all-to-all-done.got_ref, bf16[512,256]{1,0:T(8,128)(2,1)S(1)} %convolution_convert_fusion.table_t_ref, bf16[256,512]{1,0:T(8,128)(2,1)S(1)} %multiply_convert_fusion.table_w_ref, f32[512,128]{1,0:T(8,128)S(1)} %broadcast_in_dim.90.shift_ref), custom_call_target="tpu_custom_call" | custom-call | flops 6442450944 | bytes 1024 | tf_op jit(solution)/shard_map/quad_forces/pallas_call | solution.py:202
  45.8 5.5 %all-to-all-start.1 = ((bf16[32,8,32,128]{3,2,1,0:T(8,128)(2,1)}), bf16[32,8,32,128]{3,2,1,0:T(8,128)(2,1)S(1)}, u32[]{:S(2)}, u32[]{:S(2)}) async-start(bf16[32,8,32,128]{3,2,1,0:T(8,128)(2,1)} %quad_forces.1), calls=%async_computation.1 | async-start | bytes 4194304 | tf_op jit(solution)/shard_map/all_to_all | solution.py:432
  51.2 0.0 collective-permute-done.1.outer_ref
  51.3 4.7 %add_outer.1 = (bf16[16,8,4096]{2,1,0:T(8,128)(2,1)}, bf16[16,8,4096]{2,1,0:T(8,128)(2,1)}) custom-call(s32[1]{0:T(128)} %bitcast.odd_ref, bf16[2,32,4096]{2,1,0:T(8,128)(2,1)S(1)} %collective-permute-done.1.outer_ref, bf16[32,128]{1,0:T(8,128)(2,1)S(1)} %collective-permute-done.ends_ref, bf16[16,8,4096]{2,1,0:T(8,128)(2,1)} %stencil.2.res_ref, ...), custom_call_target="tpu_custom_call" | custom-call | flops 21474836480 | bytes 7340032 | tf_op jit(solution)/shard_map/add_outer/pallas_call | solution.py:285
  56.0 23.4 %all-to-all-done.1.force_ref = bf16[32,8,32,128]{3,2,1,0:T(8,128)(2,1)S(1)} async-done(((bf16[32,8,32,128]{3,2,1,0:T(8,128)(2,1)}), bf16[32,8,32,128]{3,2,1,0:T(8,128)(2,1)S(1)}, u32[]{:S(2)}, u32[]{:S(2)}) %all-to-all-start.1) | async-done | bytes 2097184 | tf_op jit(solution)/shard_map/all_to_all | solution.py:432
  79.4 3.3 %merge.1 = (f32[16,8,4096]{2,1,0:T(8,128)}, f32[16,8,4096]{2,1,0:T(8,128)}) custom-call(bf16[32,8,32,128]{3,2,1,0:T(8,128)(2,1)S(1)} %all-to-all-done.1.force_ref, bf16[16,8,4096]{2,1,0:T(8,128)(2,1)} %get-tuple-element.30.res_ref, bf16[16,8,4096]{2,1,0:T(8,128)(2,1)} %get-tuple-element.31.tan_ref), custom_call_target="tpu_custom_call" | custom-call | flops 536870912 | bytes 10485760 | tf_op jit(solution)/shard_map/merge/pallas_call | solution.py:408
  (5 shorter events, 0.1 us)
Async XLA Ops:
  3.6 37.8 %all-to-all-start = ((bf16[32,8,32,128]{3,2,1,0:T(8,128)(2,1)}), bf16[32,8,32,128]{3,2,1,0:T(8,128)(2,1)S(1)}, u32[]{:S(2)}, u32[]{:S(2)}) async-start(bf16[32,8,32,128]{3,2,1,0:T(8,128)(2,1)} %pack.1), calls=%async_computation | async-start | bytes 4194304 | tf_op jit(solution)/shard_map/all_to_all | solution.py:432
  13.2 6.7 %copy-start.1 = (s32[256,8]{0,1:T(8,128)S(1)}, s32[256,8]{0,1:T(8,128)}, u32[]{:S(2)}) copy-start(s32[256,8]{0,1:T(8,128)} %param.13) | copy-start | bytes 24580
  16.9 10.0 %copy-start.4 = (f32[512]{0:T(512)S(1)}, f32[512]{0:T(512)}, u32[]{:S(2)}) copy-start(f32[512]{0:T(512)} %param.11) | copy-start | bytes 6148
  16.9 10.0 %copy-start.2 = (f32[512]{0:T(512)S(1)}, f32[512]{0:T(512)}, u32[]{:S(2)}) copy-start(f32[512]{0:T(512)} %param.10) | copy-start | bytes 6148
  16.9 10.0 %copy-start.3 = (f32[512]{0:T(512)S(1)}, f32[512]{0:T(512)}, u32[]{:S(2)}) copy-start(f32[512]{0:T(512)} %param.12) | copy-start | bytes 6148
  16.9 10.0 %copy-start = (f32[512,8]{0,1:T(8,128)S(1)}, f32[512,8]{0,1:T(8,128)}, u32[]{:S(2)}) copy-start(f32[512,8]{0,1:T(8,128)} %param.9) | copy-start | bytes 49156
  16.9 22.7 %collective-permute-start = (bf16[32,128]{1,0:T(8,128)(2,1)}, bf16[32,128]{1,0:T(8,128)(2,1)S(1)}, u32[]{:S(2)}, u32[]{:S(2)}) collective-permute-start(bf16[32,128]{1,0:T(8,128)(2,1)} %get-tuple-element.20), channel_id=1, source_target_pairs={{0,16},{16,0},{32,48},{48,32},{64,80},{80,64},{96,112},{112,96},{1... | collective-permute-start | bytes 24584 | tf_op jit(solution)/shard_map/ppermute | solution.py:438
  35.9 15.3 %collective-permute-start.1 = (bf16[2,32,4096]{2,1,0:T(8,128)(2,1)}, bf16[2,32,4096]{2,1,0:T(8,128)(2,1)S(1)}, u32[]{:S(2)}, u32[]{:S(2)}) collective-permute-start(bf16[2,32,4096]{2,1,0:T(8,128)(2,1)} %get-tuple-element.26), channel_id=1, source_target_pairs={{16,32},{32,16},{48,64},{64,48},{80,96},{96,80},{17,33},{33,17},{4... | collective-permute-start | bytes 1572872 | tf_op jit(solution)/shard_map/ppermute | solution.py:447
  45.8 33.6 %all-to-all-start.1 = ((bf16[32,8,32,128]{3,2,1,0:T(8,128)(2,1)}), bf16[32,8,32,128]{3,2,1,0:T(8,128)(2,1)S(1)}, u32[]{:S(2)}, u32[]{:S(2)}) async-start(bf16[32,8,32,128]{3,2,1,0:T(8,128)(2,1)} %quad_forces.1), calls=%async_computation.1 | async-start | bytes 4194304 | tf_op jit(solution)/shard_map/all_to_all | solution.py:432

commit v9 on v8

--- a/solution.py
+++ b/solution.py
@@ -133,6 +133,10 @@
         at = pl.ds(i // pairs * per, per)
         lines = pl.ds(i % pairs * deep, deep)
         return pltpu.make_async_copy(out_buf.at[at, lines], out_ref.at[at, lines], out_sem.at[i])
+
+    def last_half(f):
+        here = (pl.ds(per, per), pl.ds(rows - deep, deep), pl.ds(f * modes, modes))
+        return pltpu.make_async_copy(out_buf.at[here], out_ref.at[here], out_sem.at[steps - 1 + f])
 
     def field_rows(i, f):
         at = pl.ds(i // pairs * per, per)
@@ -190,9 +194,11 @@
             store(i - 1).start()
     for f in range(2):
         back(steps - 1, f)
-    store(steps - 1).start()
-    for i in range(steps):
+        last_half(f).start()
+    for i in range(steps - 1):
         store(i).wait()
+    for f in range(2):
+        last_half(f).wait()
 
 
 def quad_forces(got, table_t, table_w, shift, deep=2):
@@ -208,7 +214,7 @@
             pltpu.VMEM(got.shape, BF16),
             pltpu.VMEM((2, 2, quad, deep * each), BF16),
             pltpu.VMEM((2, deep * each, deep * each), BF16),
-            pltpu.SemaphoreType.DMA((2 * rows // deep,)),
+            pltpu.SemaphoreType.DMA((2 * rows // deep + 1,)),
         ],
         compiler_params=pltpu.CompilerParams(vmem_limit_bytes=VMEM),
         cost_estimate=pl.CostEstimate(flops=3 << 31, bytes_accessed=1 << 10, transcendentals=0),

time: 83.2 us -> 83.5 us (level)
  no operation moved by 1% of the time
where the time goes in v9:
time: 83.5 us; the launch traced here: 83 us
  Pallas kernels  31.9 us (38%)
  waiting for transfers between devices  28.1 us (34%)
  starting transfers between devices  18.8 us (23%)
  other arithmetic  2.3 us (3%)
    all_to_all x2, waiting for transfers between devices, exchange(): lax.all_to_all(x, ('space', 'mode'), split_axis=0, concat_axis=0, axis_in...  25.1 us
    all_to_all x2, starting transfers between devices, exchange(): lax.all_to_all(x, ('space', 'mode'), split_axis=0, concat_axis=0, axis_in...  15.1 us
    pallas_call x2, Pallas kernels, stencil(): pl.pallas_call(functools.partial(stencil_kernel, 512), grid=(1,), in_spec...  12.6 us
    pallas_call x1, Pallas kernels, add_outer(): pl.pallas_call(functools.partial(outer_kernel, width // count, count), gr...  4.74 us
    pallas_call x1, Pallas kernels, quad_forces(): pl.pallas_call(functools.partial(quad_kernel, 128, deep), in_specs=[vmem]...  4.62 us
    pallas_call x1, Pallas kernels, edges(): pl.pallas_call(functools.partial(edges_kernel, width // count), grid=(1,)...  3.64 us
    pallas_call x1, Pallas kernels, merge(): pl.pallas_call(functools.partial(merge_kernel, cuts, step), in_specs=[vme...  3.31 us
    ppermute x1, waiting for transfers between devices, shards(): ends = lax.ppermute(ends, 'space', [(i, i ^ 1) for i in range(bands)])  3.01 us
  transfers between devices with their start and end apart: 4, of which 3 were waited for; matrix products, arithmetic and copies ran while one was open for 4% of the time, Pallas kernels for 31%

profile of v9, /device:TPU:1, one launch (start us, length us, event | category | flops | bytes accessed | tf_op | source)
XLA Modules:
  0.0 83.0 jit_solution(10525367494040127038)
XLA Ops:
  0.6 3.0 %pack.1 = bf16[32,8,32,128]{3,2,1,0:T(8,128)(2,1)} custom-call(bf16[16,8,4096]{2,1,0:T(8,128)(2,1)} %x_ref, bf16[16,8,4096]{2,1,0:T(8,128)(2,1)} %x_ref.1), custom_call_target="tpu_custom_call" | custom-call | flops 536870912 | bytes 4194304 | tf_op jit(solution)/shard_map/pack/pallas_call | solution.py:106
  3.6 9.6 %all-to-all-start = ((bf16[32,8,32,128]{3,2,1,0:T(8,128)(2,1)}), bf16[32,8,32,128]{3,2,1,0:T(8,128)(2,1)S(1)}, u32[]{:S(2)}, u32[]{:S(2)}) async-start(bf16[32,8,32,128]{3,2,1,0:T(8,128)(2,1)} %pack.1), calls=%async_computation | async-start | bytes 4194304 | tf_op jit(solution)/shard_map/all_to_all | solution.py:438
  13.2 0.0 copy-start.1
  13.3 3.6 %edges.1 = (bf16[2,32,4096]{2,1,0:T(8,128)(2,1)}, bf16[32,128]{1,0:T(8,128)(2,1)}) custom-call(s32[1]{0:T(128)} %bitcast.odd_ref, bf16[16,8,4096]{2,1,0:T(8,128)(2,1)} %x_ref, bf16[16,8,4096]{2,1,0:T(8,128)(2,1)} %x_ref.1), custom_call_target="tpu_custom_call" | custom-call | flops 1048576 | bytes 1048576 | tf_op jit(solution)/shard_map/edges/pallas_call | solution.py:347
  16.9 0.0 copy-start.4
  16.9 0.0 copy-start.2
  16.9 0.0 copy-start.3
  16.9 0.0 copy-start
  16.9 3.0 %collective-permute-start = (bf16[32,128]{1,0:T(8,128)(2,1)}, bf16[32,128]{1,0:T(8,128)(2,1)S(1)}, u32[]{:S(2)}, u32[]{:S(2)}) collective-permute-start(bf16[32,128]{1,0:T(8,128)(2,1)} %get-tuple-element.20), channel_id=1, source_target_pairs={{0,16},{16,0},{32,48},{48,32},{64,80},{80,64},{96,112},{112,96},{1... | collective-permute-start | bytes 24584 | tf_op jit(solution)/shard_map/ppermute | solution.py:444
  19.9 0.0 copy-done.1
  19.9 0.2 copy.17
  20.1 0.2 copy.18
  20.3 0.2 copy.20
  20.4 0.2 copy.19
  20.6 6.3 %stencil.2.res_ref = bf16[16,8,4096]{2,1,0:T(8,128)(2,1)} custom-call(bf16[16,8,4096]{2,1,0:T(8,128)(2,1)} %x_ref), custom_call_target="tpu_custom_call" | custom-call | flops 1073741824 | bytes 1048576 | tf_op jit(solution)/shard_map/stencil/pallas_call | solution.py:255
  26.9 0.0 copy-done.4
  26.9 0.0 copy-done.2
  26.9 0.0 copy-done.3
  26.9 0.0 copy-done
  27.0 2.2 %select_reduce_fusion = bf16[256,512]{1,0:T(8,128)(2,1)S(1)} fusion(f32[512,8]{0,1:T(8,128)S(1)} %get-tuple-element.33, f32[512,8]{0,1:T(8,128)S(1)} %get-tuple-element.34, f32[512,8]{0,1:T(8,128)S(1)} %get-tuple-element.32, f32[512,8]{0,1:T(8,128)S(1)} %copy-done, pred[256,8]{1,0:T(8,128)(4,1)S(1)} %copy.20, pred[256,8]{1,0:T(8,128)(4,1)S(1)} %copy.19, ...), kind=kLoop, calls=%fused_computation | loop fusion | flops 5111808 | bytes 335872 | tf_op jit(solution)/shard_map/reduce_prod | solution.py:41
  29.2 0.3 convolution_convert_fusion.table_t_ref
  29.5 6.3 %stencil.3.tan_ref = bf16[16,8,4096]{2,1,0:T(8,128)(2,1)} custom-call(bf16[16,8,4096]{2,1,0:T(8,128)(2,1)} %x_ref.1), custom_call_target="tpu_custom_call" | custom-call | flops 1073741824 | bytes 1048576 | tf_op jit(solution)/shard_map/stencil/pallas_call | solution.py:255
  35.8 0.1 broadcast_in_dim.90.shift_ref
  35.9 0.7 collective-permute-start.1
  36.6 3.0 %collective-permute-done.ends_ref = bf16[32,128]{1,0:T(8,128)(2,1)S(1)} collective-permute-done((bf16[32,128]{1,0:T(8,128)(2,1)}, bf16[32,128]{1,0:T(8,128)(2,1)S(1)}, u32[]{:S(2)}, u32[]{:S(2)}) %collective-permute-start) | collective-permute-done | bytes 8224 | tf_op jit(solution)/shard_map/ppermute | solution.py:444
  39.7 1.7 %all-to-all-done.got_ref = bf16[32,8,32,128]{3,2,1,0:T(8,128)(2,1)S(1)} async-done(((bf16[32,8,32,128]{3,2,1,0:T(8,128)(2,1)}), bf16[32,8,32,128]{3,2,1,0:T(8,128)(2,1)S(1)}, u32[]{:S(2)}, u32[]{:S(2)}) %all-to-all-start) | async-done | bytes 2097184 | tf_op jit(solution)/shard_map/all_to_all | solution.py:438
  41.4 4.6 %quad_forces.1 = bf16[32,8,32,128]{3,2,1,0:T(8,128)(2,1)} custom-call(bf16[32,8,32,128]{3,2,1,0:T(8,128)(2,1)S(1)} %all-to-all-done.got_ref, bf16[512,256]{1,0:T(8,128)(2,1)S(1)} %convolution_convert_fusion.table_t_ref, bf16[256,512]{1,0:T(8,128)(2,1)S(1)} %multiply_convert_fusion.table_w_ref, f32[512,128]{1,0:T(8,128)S(1)} %broadcast_in_dim.90.shift_ref), custom_call_target="tpu_custom_call" | custom-call | flops 6442450944 | bytes 1024 | tf_op jit(solution)/shard_map/quad_forces/pallas_call | solution.py:208
  46.0 5.5 %all-to-all-start.1 = ((bf16[32,8,32,128]{3,2,1,0:T(8,128)(2,1)}), bf16[32,8,32,128]{3,2,1,0:T(8,128)(2,1)S(1)}, u32[]{:S(2)}, u32[]{:S(2)}) async-start(bf16[32,8,32,128]{3,2,1,0:T(8,128)(2,1)} %quad_forces.1), calls=%async_computation.1 | async-start | bytes 4194304 | tf_op jit(solution)/shard_map/all_to_all | solution.py:438
  51.5 0.0 collective-permute-done.1.outer_ref
  51.5 4.7 %add_outer.1 = (bf16[16,8,4096]{2,1,0:T(8,128)(2,1)}, bf16[16,8,4096]{2,1,0:T(8,128)(2,1)}) custom-call(s32[1]{0:T(128)} %bitcast.odd_ref, bf16[2,32,4096]{2,1,0:T(8,128)(2,1)S(1)} %collective-permute-done.1.outer_ref, bf16[32,128]{1,0:T(8,128)(2,1)S(1)} %collective-permute-done.ends_ref, bf16[16,8,4096]{2,1,0:T(8,128)(2,1)} %stencil.2.res_ref, ...), custom_call_target="tpu_custom_call" | custom-call | flops 21474836480 | bytes 7340032 | tf_op jit(solution)/shard_map/add_outer/pallas_call | solution.py:291
  56.3 23.4 %all-to-all-done.1.force_ref = bf16[32,8,32,128]{3,2,1,0:T(8,128)(2,1)S(1)} async-done(((bf16[32,8,32,128]{3,2,1,0:T(8,128)(2,1)}), bf16[32,8,32,128]{3,2,1,0:T(8,128)(2,1)S(1)}, u32[]{:S(2)}, u32[]{:S(2)}) %all-to-all-start.1) | async-done | bytes 2097184 | tf_op jit(solution)/shard_map/all_to_all | solution.py:438
  79.7 3.3 %merge.1 = (f32[16,8,4096]{2,1,0:T(8,128)}, f32[16,8,4096]{2,1,0:T(8,128)}) custom-call(bf16[32,8,32,128]{3,2,1,0:T(8,128)(2,1)S(1)} %all-to-all-done.1.force_ref, bf16[16,8,4096]{2,1,0:T(8,128)(2,1)} %get-tuple-element.30.res_ref, bf16[16,8,4096]{2,1,0:T(8,128)(2,1)} %get-tuple-element.31.tan_ref), custom_call_target="tpu_custom_call" | custom-call | flops 536870912 | bytes 10485760 | tf_op jit(solution)/shard_map/merge/pallas_call | solution.py:414
  (5 shorter events, 0.1 us)
Async XLA Ops:
  3.6 37.8 %all-to-all-start = ((bf16[32,8,32,128]{3,2,1,0:T(8,128)(2,1)}), bf16[32,8,32,128]{3,2,1,0:T(8,128)(2,1)S(1)}, u32[]{:S(2)}, u32[]{:S(2)}) async-start(bf16[32,8,32,128]{3,2,1,0:T(8,128)(2,1)} %pack.1), calls=%async_computation | async-start | bytes 4194304 | tf_op jit(solution)/shard_map/all_to_all | solution.py:438
  13.2 6.7 %copy-start.1 = (s32[256,8]{0,1:T(8,128)S(1)}, s32[256,8]{0,1:T(8,128)}, u32[]{:S(2)}) copy-start(s32[256,8]{0,1:T(8,128)} %param.13) | copy-start | bytes 24580
  16.9 10.0 %copy-start.4 = (f32[512]{0:T(512)S(1)}, f32[512]{0:T(512)}, u32[]{:S(2)}) copy-start(f32[512]{0:T(512)} %param.11) | copy-start | bytes 6148
  16.9 10.0 %copy-start.2 = (f32[512]{0:T(512)S(1)}, f32[512]{0:T(512)}, u32[]{:S(2)}) copy-start(f32[512]{0:T(512)} %param.10) | copy-start | bytes 6148
  16.9 10.0 %copy-start.3 = (f32[512]{0:T(512)S(1)}, f32[512]{0:T(512)}, u32[]{:S(2)}) copy-start(f32[512]{0:T(512)} %param.12) | copy-start | bytes 6148
  16.9 10.0 %copy-start = (f32[512,8]{0,1:T(8,128)S(1)}, f32[512,8]{0,1:T(8,128)}, u32[]{:S(2)}) copy-start(f32[512,8]{0,1:T(8,128)} %param.9) | copy-start | bytes 49156
  16.9 22.7 %collective-permute-start = (bf16[32,128]{1,0:T(8,128)(2,1)}, bf16[32,128]{1,0:T(8,128)(2,1)S(1)}, u32[]{:S(2)}, u32[]{:S(2)}) collective-permute-start(bf16[32,128]{1,0:T(8,128)(2,1)} %get-tuple-element.20), channel_id=1, source_target_pairs={{0,16},{16,0},{32,48},{48,32},{64,80},{80,64},{96,112},{112,96},{1... | collective-permute-start | bytes 24584 | tf_op jit(solution)/shard_map/ppermute | solution.py:444
  35.9 15.6 %collective-permute-start.1 = (bf16[2,32,4096]{2,1,0:T(8,128)(2,1)}, bf16[2,32,4096]{2,1,0:T(8,128)(2,1)S(1)}, u32[]{:S(2)}, u32[]{:S(2)}) collective-permute-start(bf16[2,32,4096]{2,1,0:T(8,128)(2,1)} %get-tuple-element.26), channel_id=1, source_target_pairs={{16,32},{32,16},{48,64},{64,48},{80,96},{96,80},{17,33},{33,17},{4... | collective-permute-start | bytes 1572872 | tf_op jit(solution)/shard_map/ppermute | solution.py:453
  46.0 33.6 %all-to-all-start.1 = ((bf16[32,8,32,128]{3,2,1,0:T(8,128)(2,1)}), bf16[32,8,32,128]{3,2,1,0:T(8,128)(2,1)S(1)}, u32[]{:S(2)}, u32[]{:S(2)}) async-start(bf16[32,8,32,128]{3,2,1,0:T(8,128)(2,1)} %quad_forces.1), calls=%async_computation.1 | async-start | bytes 4194304 | tf_op jit(solution)/shard_map/all_to_all | solution.py:438
